TPU v7x, 256 devices: a whole 4x4x8 slice. The times are simulated.
256 devices in a mesh: mesh: 2 (over core), patch: 128 (over z, y, x).
Axes of the slice: x: 4, y: 4, z: 8, core: 2. Of those that a mesh axis runs over, the one named last changes fastest.
Arguments:
- nodes: bfloat16 [2, 65536, 512], P('mesh', 'patch'), may hold values from -6 to 6
- edges: bfloat16 [2, 131072, 512], P('mesh', 'patch'), may hold values from -6 to 6
- cot_nodes: bfloat16 [2, 65536, 512], P('mesh', 'patch'), may hold values from -6 to 6
- weights: bfloat16 [3584, 512], replicated, may hold values from -0.1875 to 0.1875
- edge_src: int32 [2, 131072], P('mesh', 'patch'), may hold values from 0 to 639, as said below
- edge_dst: int32 [2, 131072], P('mesh', 'patch'), may hold values from 0 to 511
- halo_rows: int32 [2, 16384], P('mesh', 'patch'), may hold values from 0 to 511
- couple_rows: int32 [2, 128, 1024], P('mesh', 'patch'), may hold values from 0 to 511
- couple_count: int32 [2, 128, 128], P('mesh', 'patch'), may hold values from 0 to 8, as said below
- couple_target: int32 [2, 128, 1024], P('mesh', 'patch'), may hold values from 0 to 511
- couple_weight: float32 [2, 128, 1024], P('mesh', 'patch'), may hold values from 0.25 to 1
Outputs:
- new_nodes: bfloat16 [2, 65536, 512], P('mesh', 'patch')
- node_grads: bfloat16 [2, 65536, 512], P('mesh', 'patch')
- edge_grads: bfloat16 [2, 131072, 512], P('mesh', 'patch')
- weight_grads: float32 [7, 262144], P(None, 'patch')
Inputs may be any that keep to these rules, and one draw needn't show every extreme that they name: `edge_src`: in each patch the first 768 entries name own rows (below 512), the last 256 name rows received from neighbouring patches. `couple_count`: A sending patch has up to 4 live slots to any receiving patch, more to receiving patches within cyclic distance 3 of it; every sending patch fills all 8 slots for one receiver near it, and one receiving patch of each half gets 8 live slots from every sender. Loads of receiving patches differ.
All inputs are finite; a program needn't handle non-finite values.
Results may differ from a plain program's by a relative error of at most 0.011.
Values may be sent and summed in bfloat16 or wider, within the bound.
No kernel may reach another device: no remote copies, remote signals or barrier semaphores. Data moves between devices by JAX's collectives and lax.ppermute only.
A program may use at most 128 MiB of HBM per device.

v0:
```python
import math

import jax
import jax.numpy as jnp
from jax import lax
from jax.sharding import PartitionSpec as P

SLOT = 8


def from_partner(value, axis, stride):
    mask = 2**stride
    pairs = [(source, source ^ mask) for source in range(lax.axis_size(axis))]
    return lax.ppermute(value, axis, pairs)


def with_halo(block, sides, width):
    for axis, dim in sides:
        count = lax.axis_size(axis)
        forward = [(i, i + 1) for i in range(count - 1)]
        forward.append((count - 1, 0))
        backward = [(target, source) for source, target in forward]
        low = lax.ppermute(
            lax.slice_in_dim(block, block.shape[dim] - width, None, axis=dim), axis, forward
        )
        high = lax.ppermute(lax.slice_in_dim(block, 0, width, axis=dim), axis, backward)
        block = jnp.concatenate([low, block, high], axis=dim)
    return block


def silu_slope(value):
    sigma = jax.nn.sigmoid(value)
    return sigma * (1.0 + value * (1.0 - sigma))


def process_layer(
    nodes_own, edges_own, cotangent, source_feat, targets_edge, received, target, margin, weights
):
    count, width = nodes_own.shape
    edge_first = weights[: 3 * width]
    edge_second = weights[3 * width : 4 * width]
    node_first = weights[4 * width : 6 * width]
    node_second = weights[6 * width :]
    edge_input = jnp.concatenate([source_feat, nodes_own[targets_edge], edges_own], axis=1)
    edge_pre = jnp.dot(edge_input, edge_first, preferred_element_type=jnp.float32)
    edge_hidden = jax.nn.silu(edge_pre).astype(jnp.bfloat16)
    message = jnp.dot(edge_hidden, edge_second, preferred_element_type=jnp.float32)
    flat_received = received.reshape(-1, width).astype(jnp.float32)
    flat_target = target.reshape(-1)
    flat_margin = margin.reshape(-1)
    coupled = jax.ops.segment_sum(
        flat_received * flat_margin[:, None], flat_target, num_segments=count
    )
    pooled = (jax.ops.segment_sum(message, targets_edge, num_segments=count) + coupled).astype(
        jnp.bfloat16
    )
    node_input = jnp.concatenate([nodes_own, pooled], axis=1)
    node_pre = jnp.dot(node_input, node_first, preferred_element_type=jnp.float32)
    node_hidden = jax.nn.silu(node_pre).astype(jnp.bfloat16)
    update = jnp.dot(node_hidden, node_second, preferred_element_type=jnp.float32)
    new_nodes = (nodes_own.astype(jnp.float32) + update).astype(jnp.bfloat16)
    grad_node_second = jnp.dot(node_hidden.T, cotangent, preferred_element_type=jnp.float32)
    grad_node_pre = (
        jnp.dot(cotangent, node_second.T, preferred_element_type=jnp.float32) * silu_slope(node_pre)
    ).astype(jnp.bfloat16)
    grad_node_first = jnp.dot(node_input.T, grad_node_pre, preferred_element_type=jnp.float32)
    grad_node_input = jnp.dot(grad_node_pre, node_first.T, preferred_element_type=jnp.float32)
    grad_pooled = grad_node_input[:, width:].astype(jnp.bfloat16)
    grad_message = grad_pooled[targets_edge]
    grad_edge_second = jnp.dot(edge_hidden.T, grad_message, preferred_element_type=jnp.float32)
    grad_edge_pre = (
        jnp.dot(grad_message, edge_second.T, preferred_element_type=jnp.float32)
        * silu_slope(edge_pre)
    ).astype(jnp.bfloat16)
    grad_edge_first = jnp.dot(edge_input.T, grad_edge_pre, preferred_element_type=jnp.float32)
    grad_edge_input = jnp.dot(grad_edge_pre, edge_first.T, preferred_element_type=jnp.float32)
    edge_grads = grad_edge_input[:, 2 * width :].astype(jnp.bfloat16)
    node_part = cotangent.astype(jnp.float32) + grad_node_input[:, :width]
    node_part = node_part + jax.ops.segment_sum(
        grad_edge_input[:, width : 2 * width], targets_edge, num_segments=count
    )
    source_grad = grad_edge_input[:, :width]
    returned = (
        (grad_pooled[flat_target].astype(jnp.float32) * flat_margin[:, None])
        .astype(jnp.bfloat16)
        .reshape(received.shape)
    )
    weight_grad = jnp.concatenate(
        [grad_edge_first, grad_edge_second, grad_node_first, grad_node_second], axis=0
    )
    return (new_nodes, node_part, source_grad, returned, edge_grads, weight_grad)


def route(buffer):
    crossed = from_partner(buffer, "mesh", 0)
    return lax.all_to_all(crossed, "patch", split_axis=0, concat_axis=0, tiled=True)


def border(buffer, depth):
    framed = with_halo(buffer, (("patch", 0),), depth)
    return jnp.concatenate([framed[:depth], framed[-depth:]], axis=0)


def shards(
    nodes,
    edges,
    cot_nodes,
    weights,
    edge_src,
    edge_dst,
    halo_rows,
    couple_rows,
    couple_count,
    couple_target,
    couple_weight,
):
    nodes_own = nodes[0]
    edges_own = edges[0]
    cotangent = cot_nodes[0]
    count, width = nodes_own.shape
    sources = edge_src[0]
    targets_edge = edge_dst[0]
    halo_index = halo_rows[0]
    depth = halo_index.shape[0] // 2
    patches = lax.axis_size("patch")
    slot_rows = couple_rows[0, 0].reshape(patches, SLOT)
    live = lax.broadcasted_iota(jnp.int32, (patches, SLOT), 1) < couple_count[0, 0][:, None]
    outgoing = jnp.where(live[:, :, None], nodes_own[slot_rows], jnp.zeros((), nodes_own.dtype))
    received = route(outgoing)
    target = couple_target[0, 0].reshape(patches, SLOT)
    margin = couple_weight[0, 0].reshape(patches, SLOT)
    extended = jnp.concatenate([nodes_own, border(nodes_own[halo_index], depth)], axis=0)
    source_feat = extended[sources]
    new_nodes, node_part, source_grad, returned, edge_grads, weight_grad = process_layer(
        nodes_own,
        edges_own,
        cotangent,
        source_feat,
        targets_edge,
        received,
        target,
        margin,
        weights,
    )
    spread = jax.ops.segment_sum(source_grad, sources, num_segments=count + 2 * depth)
    halo_back = border(spread[count:].astype(jnp.bfloat16), depth).astype(jnp.float32)
    couple_back = route(returned)
    couple_back = jnp.where(live[:, :, None], couple_back, jnp.zeros((), couple_back.dtype))
    couple_back = couple_back.astype(jnp.float32).reshape(-1, width)
    node_total = node_part + spread[:count]
    node_total = node_total + jax.ops.segment_sum(halo_back, halo_index, num_segments=count)
    node_total = node_total + jax.ops.segment_sum(
        couple_back, slot_rows.reshape(-1), num_segments=count
    )
    scale = 1.0 / math.sqrt(2 * patches * edges_own.shape[0])
    local_grad = (weight_grad * scale).reshape(7, width * width)
    paired = lax.psum(local_grad.astype(jnp.bfloat16), "mesh").astype(jnp.float32)
    summed = lax.psum_scatter(paired, "patch", scatter_dimension=1, tiled=True)
    return (new_nodes[None], node_total.astype(jnp.bfloat16)[None], edge_grads[None], summed)


def solution(mesh):
    return jax.shard_map(
        shards,
        mesh=mesh,
        in_specs=(
            P("mesh", "patch", None),
            P("mesh", "patch", None),
            P("mesh", "patch", None),
            P(),
            P("mesh", "patch"),
            P("mesh", "patch"),
            P("mesh", "patch"),
            P("mesh", "patch", None),
            P("mesh", "patch", None),
            P("mesh", "patch", None),
            P("mesh", "patch", None),
        ),
        out_specs=(
            P("mesh", "patch", None),
            P("mesh", "patch", None),
            P("mesh", "patch", None),
            P(None, "patch"),
        ),
        check_vma=False,
    )
```

profile of v0, /device:TPU:0, one launch (start us, length us, event | category | flops | bytes accessed | tf_op | source)
XLA Modules:
  0.0 869.9 jit_solution(14284771438825368063)
XLA Ops:
  10.0 5.1 gather_fusion.3
  17.1 8.8 %collective-permute-start.1 = (bf16[64,512]{1,0:T(8,128)(2,1)S(1)}, bf16[64,512]{1,0:T(8,128)(2,1)S(1)}, u32[]{:S(2)}, u32[]{:S(2)}) collective-permute-start(bf16[64,512]{1,0:T(8,128)(2,1)S(1)} %get-tuple-element.7), channel_id=1, source_target_pairs={{1,0},{2,1},{3,2},{4,3},{5,4},{6,5},{7,6},{8,7},{9,8},{10,9},{11,1... | collective-permute-start | bytes 196616 | tf_op jit(solution)/shard_map/ppermute | solution.py:26
  26.0 7.6 all-to-all-start
  33.7 4.0 gather_fusion.2
  37.7 5.1 gather_fusion.1
  42.8 5.4 multiply_convert_fusion.1
  49.2 3.1 fusion.41
  52.2 8.4 scatter_custom_fusion
  60.7 3.5 all-to-all-done
  64.2 7.4 scatter_custom_fusion.1
  82.7 5.0 gather_fusion.4
  98.0 8.1 convert_element_type.76
  106.1 37.0 %all-reduce.2.cloned.1.call-done = bf16[7,262144]{1,0:T(8,128)(2,1)} async-done(((bf16[7,262144]{1,0:T(8,128)(2,1)}), bf16[7,262144]{1,0:T(8,128)(2,1)}) %all-reduce.2.cloned.1.call-update) | async-done | bytes 3670032 | tf_op jit(solution)/shard_map/psum | solution.py:157
  143.1 5.1 convert_element_type.77
  149.5 4.0 gather_fusion.5
  156.9 14.4 %all-to-all-start.1 = ((bf16[128,8,512]{2,1,0:T(8,128)(2,1)}), bf16[128,8,512]{2,1,0:T(8,128)(2,1)}, u32[]{:S(2)}, u32[]{:S(2)}) async-start(bf16[128,8,512]{2,1,0:T(8,128)(2,1)} %collective-permute-done.5), calls=%async_computation.1 | async-start | bytes 2097152 | tf_op jit(solution)/shard_map/all_to_all | solution.py:96
  171.3 5.9 fusion.9
  177.3 7.8 scatter_custom_fusion.2
  186.3 6.4 collective-permute-start.4
  195.3 2.7 fusion.17
  198.0 8.0 scatter_custom_fusion.3
  206.1 2.8 scatter_custom_fusion.4
  210.3 7.8 scatter_custom_fusion.5
  218.9 643.6 %reduce-scatter.2.cloned.1.call-done = f32[7,2048]{1,0:T(8,128)} async-done(((f32[7,262144]{1,0:T(8,128)}), f32[7,2048]{1,0:T(8,128)}) %reduce-scatter.2.cloned.1.call-update) | async-done | bytes 57360 | tf_op jit(solution)/shard_map/reduce_scatter | solution.py:158
  (99 shorter events, 37.9 us)
Async XLA Ops:
  15.3 18.3 %copy-start.13 = (s32[1,1024]{1,0:T(1,128)S(1)}, s32[1,1024]{1,0:T(1,128)}, u32[]{:S(2)}) copy-start(s32[1,1024]{1,0:T(1,128)} %param.15) | copy-start | bytes 12292
  15.3 18.3 %copy-start.14 = (s32[1,1024]{1,0:T(1,128)S(1)}, s32[1,1024]{1,0:T(1,128)}, u32[]{:S(2)}) copy-start(s32[1,1024]{1,0:T(1,128)} %param.16) | copy-start | bytes 12292
  15.4 10.6 %collective-permute-start.2 = (bf16[128,8,512]{2,1,0:T(8,128)(2,1)S(1)}, bf16[128,8,512]{2,1,0:T(8,128)(2,1)}, u32[]{:S(2)}, u32[]{:S(2)}) collective-permute-start(bf16[128,8,512]{2,1,0:T(8,128)(2,1)S(1)} %bitcast_select_fusion), channel_id=1, source_target_pairs={{0,128},{128,0},{1,129},{129,1},{2,130},{130,2},{3,131},{131,3},{4... | collective-permute-start | bytes 3145736 | tf_op jit(solution)/shard_map/ppermute | solution.py:14
  17.0 20.6 %collective-permute-start = (bf16[64,512]{1,0:T(8,128)(2,1)S(1)}, bf16[64,512]{1,0:T(8,128)(2,1)S(1)}, u32[]{:S(2)}, u32[]{:S(2)}) collective-permute-start(bf16[64,512]{1,0:T(8,128)(2,1)S(1)} %get-tuple-element.6), channel_id=1, source_target_pairs={{0,1},{1,2},{2,3},{3,4},{4,5},{5,6},{6,7},{7,8},{8,9},{9,10},{10,1... | collective-permute-start | bytes 196616 | tf_op jit(solution)/shard_map/ppermute | solution.py:23
  17.1 20.5 %collective-permute-start.1 = (bf16[64,512]{1,0:T(8,128)(2,1)S(1)}, bf16[64,512]{1,0:T(8,128)(2,1)S(1)}, u32[]{:S(2)}, u32[]{:S(2)}) collective-permute-start(bf16[64,512]{1,0:T(8,128)(2,1)S(1)} %get-tuple-element.7), channel_id=1, source_target_pairs={{1,0},{2,1},{3,2},{4,3},{5,4},{6,5},{7,6},{8,7},{9,8},{10,9},{11,1... | collective-permute-start | bytes 196616 | tf_op jit(solution)/shard_map/ppermute | solution.py:26
  26.0 38.3 %all-to-all-start = ((bf16[128,8,512]{2,1,0:T(8,128)(2,1)}), bf16[128,8,512]{2,1,0:T(8,128)(2,1)S(1)}, u32[]{:S(2)}, u32[]{:S(2)}) async-start(bf16[128,8,512]{2,1,0:T(8,128)(2,1)} %collective-permute-done.2), calls=%async_computation | async-start | bytes 2097152 | tf_op jit(solution)/shard_map/all_to_all | solution.py:96
  33.5 109.6 %all-reduce.2.cloned.1.call-start = ((), (), s32[]{:S(2)}) async-start(), calls=%async_computation.3 | async-start | bytes 8388608 | tf_op jit(solution)/shard_map/psum | solution.py:157
  37.6 5.2 copy-start.3
  49.2 15.1 %copy-start.11 = (f32[1,1,1024]{2,1,0:T(1,128)S(1)}, f32[1,1,1024]{2,1,0:T(1,128)}, u32[]{:S(2)}) copy-start(f32[1,1,1024]{2,1,0:T(1,128)} %param.21) | copy-start | bytes 12292
  49.2 15.1 %copy-start.12 = (s32[1,1,1024]{2,1,0:T(1,128)S(1)}, s32[1,1,1024]{2,1,0:T(1,128)}, u32[]{:S(2)}) copy-start(s32[1,1,1024]{2,1,0:T(1,128)} %param.20) | copy-start | bytes 12292
  87.7 2.4 copy-start.7
  87.7 2.5 copy-start.21
  90.3 3.4 copy-start.4
  90.3 3.4 copy-start.5
  90.3 3.4 copy-start.15
  106.1 756.5 %reduce-scatter.2.cloned.1.call-start = ((), (), s32[]{:S(2)}) async-start(), calls=%async_computation.4 | async-start | bytes 8454144 | tf_op jit(solution)/shard_map/reduce_scatter | solution.py:158
  153.5 17.8 %copy-start.18 = (bf16[1024,512]{1,0:T(8,128)(2,1)S(1)}, bf16[1024,512]{1,0:T(8,128)(2,1)}, u32[]{:S(2)}) copy-start(bf16[1024,512]{1,0:T(8,128)(2,1)} %copy-done.17) | copy-start | bytes 3145732
  153.8 3.1 collective-permute-start.5
  156.9 53.3 %all-to-all-start.1 = ((bf16[128,8,512]{2,1,0:T(8,128)(2,1)}), bf16[128,8,512]{2,1,0:T(8,128)(2,1)}, u32[]{:S(2)}, u32[]{:S(2)}) async-start(bf16[128,8,512]{2,1,0:T(8,128)(2,1)} %collective-permute-done.5), calls=%async_computation.1 | async-start | bytes 2097152 | tf_op jit(solution)/shard_map/all_to_all | solution.py:96
  177.3 15.4 %copy-start.10 = (bf16[1,512,512]{2,1,0:T(8,128)(2,1)S(1)}, bf16[1,512,512]{2,1,0:T(8,128)(2,1)}, u32[]{:S(2)}) copy-start(bf16[1,512,512]{2,1,0:T(8,128)(2,1)} %param.13) | copy-start | bytes 1572868
  185.0 7.7 copy-start.2
  185.1 7.9 copy-start.20
  185.2 20.9 %collective-permute-start.3 = (bf16[64,512]{1,0:T(8,128)(2,1)S(1)}, bf16[64,512]{1,0:T(8,128)(2,1)}, u32[]{:S(2)}, u32[]{:S(2)}) collective-permute-start(bf16[64,512]{1,0:T(8,128)(2,1)S(1)} %get-tuple-element.4), channel_id=1, source_target_pairs={{0,1},{1,2},{2,3},{3,4},{4,5},{5,6},{6,7},{7,8},{8,9},{9,10},{10,1... | collective-permute-start | bytes 196616 | tf_op jit(solution)/shard_map/ppermute | solution.py:23
  186.3 19.8 %collective-permute-start.4 = (bf16[64,512]{1,0:T(8,128)(2,1)S(1)}, bf16[64,512]{1,0:T(8,128)(2,1)}, u32[]{:S(2)}, u32[]{:S(2)}) collective-permute-start(bf16[64,512]{1,0:T(8,128)(2,1)S(1)} %get-tuple-element.5), channel_id=1, source_target_pairs={{1,0},{2,1},{3,2},{4,3},{5,4},{6,5},{7,6},{8,7},{9,8},{10,9},{11,1... | collective-permute-start | bytes 196616 | tf_op jit(solution)/shard_map/ppermute | solution.py:26
  (8 other events, 11.0 us)
Sparse Core Ops, SparseCore 0:
  106.2 36.9 all-reduce.1
  148.4 714.1 reduce-scatter.1
where the time goes:
time: 878 us; the launch traced here: 870 us
  waiting for transfers between devices  687 us (78%)
  other arithmetic  57.1 us (7%)
  local copies, waits for them, and re-layouts  40.4 us (5%)
  starting transfers between devices  39.2 us (4%)
  matrix products  31.5 us (4%)
  between operations  15 us (2%)
    reduce_scatter x1, waiting for transfers between devices, shards(): summed = lax.psum_scatter(paired, 'patch', scatter_dimension=1, tiled=True)  644 us
    psum x1, waiting for transfers between devices, shards(): lax.psum(local_grad.astype(jnp.bfloat16), 'mesh').astype(jnp.float32)  37 us
    all_to_all x2, starting transfers between devices, route(): lax.all_to_all(crossed, 'patch', split_axis=0, concat_axis=0, tiled=True)  21.9 us
  transfers between devices with their start and end apart: 10, of which 4 were waited for; matrix products, arithmetic and copies ran while one was open for 8% of the time, Pallas kernels for 0%

commit v1 on v0

v1 whole, which is shorter than its diff:
```python
import math

import jax
import jax.numpy as jnp
from jax import lax
from jax.sharding import PartitionSpec as P

SLOT = 8
PLANE = 16
BF = jnp.bfloat16
F32 = jnp.float32


def from_partner(value):
    return lax.ppermute(value, "mesh", [(0, 1), (1, 0)])


def shift(value, step):
    count = lax.axis_size("patch")
    return lax.ppermute(value, "patch", [(i, (i + step) % count) for i in range(count)])


def border(low_out, high_out):
    return jnp.concatenate([shift(high_out, 1), shift(low_out, -1)], axis=0)


def route(buffer):
    return lax.all_to_all(from_partner(buffer), "patch", split_axis=0, concat_axis=0, tiled=True)


def dot(a, b):
    return jnp.dot(a, b, preferred_element_type=F32)


def dot_tn(a, b):
    return lax.dot_general(a, b, (((0,), (0,)), ((), ())), preferred_element_type=F32)


def dot_nt(a, b):
    return lax.dot_general(a, b, (((1,), (1,)), ((), ())), preferred_element_type=F32)


def onehot(index, count, value=1.0):
    columns = lax.broadcasted_iota(jnp.int32, (index.shape[0], count), 1)
    return jnp.where(index[:, None] == columns, value, 0.0).astype(BF)


def row_order(width, patches):
    depth = patches // PLANE
    fine = width // patches
    row = lax.broadcasted_iota(jnp.int32, (width, width), 0)
    column = lax.broadcasted_iota(jnp.int32, (width, width), 1)
    plane, rest = row // (depth * fine), row % (depth * fine)
    source = ((rest // fine) * PLANE + plane) * fine + rest % fine
    return (column == source).astype(BF)


def reduce_blocks(blocks, order):
    count, width = len(blocks), blocks[0].shape[1]
    half = width // 2
    patches = lax.axis_size("patch")
    depth = patches // PLANE
    fine = width // patches
    first = lax.axis_index("mesh") == 0
    stacked = jnp.stack([dot(order, block.astype(BF)).astype(BF) for block in blocks])
    left, right = stacked[:, :, :half], stacked[:, :, half:]
    own = jnp.where(first, left, right)
    crossed = from_partner(jnp.where(first, right, left))
    paired = (own.astype(F32) + crossed.astype(F32)).astype(BF)
    paired = paired.reshape(count, PLANE, depth * fine, half).transpose(1, 0, 2, 3)
    planes = [[z * PLANE + i for i in range(PLANE)] for z in range(depth)]
    spread = lax.all_to_all(
        paired, "patch", split_axis=0, concat_axis=0, axis_index_groups=planes, tiled=True
    )
    part = jnp.sum(spread.astype(F32), axis=0).astype(BF)
    part = part.reshape(count, depth, fine, half).transpose(1, 0, 2, 3)
    columns = [
        [m * patches + z * PLANE + i for m in range(2) for z in range(depth)] for i in range(PLANE)
    ]
    both = lax.all_to_all(
        jnp.concatenate([part, part], axis=0),
        ("mesh", "patch"),
        split_axis=0,
        concat_axis=0,
        axis_index_groups=columns,
        tiled=True,
    )
    total = jnp.sum(both.reshape(2, depth, count, fine, half).astype(F32), axis=1)
    return total.transpose(1, 2, 0, 3).reshape(count, fine * width)


def silu_slope(value):
    sigma = jax.nn.sigmoid(value)
    return sigma * (1.0 + value * (1.0 - sigma))


def shards(
    nodes,
    edges,
    cot_nodes,
    weights,
    edge_src,
    edge_dst,
    halo_rows,
    couple_rows,
    couple_count,
    couple_target,
    couple_weight,
):
    nodes_own = nodes[0]
    edges_own = edges[0]
    cotangent = cot_nodes[0]
    count, width = nodes_own.shape
    halo_index = halo_rows[0]
    depth = halo_index.shape[0] // 2
    patches = lax.axis_size("patch")
    scale = 1.0 / math.sqrt(2 * patches * edges_own.shape[0])
    edge_a, edge_b, edge_c = (weights[i * width : (i + 1) * width] for i in range(3))
    edge_second = weights[3 * width : 4 * width]
    node_a = weights[4 * width : 5 * width]
    node_b = weights[5 * width : 6 * width]
    node_second = weights[6 * width :]

    slot_rows = couple_rows[0, 0].reshape(patches, SLOT)
    live = lax.broadcasted_iota(jnp.int32, (patches, SLOT), 1) < couple_count[0, 0][:, None]
    live_rows = jnp.where(live, slot_rows, -1).reshape(-1)
    out_pick = onehot(live_rows, count)
    outgoing = dot(out_pick, nodes_own).astype(BF).reshape(patches, SLOT, width)
    received = route(outgoing).reshape(-1, width)
    halo_pick = onehot(halo_index, count)
    halo_out = dot(halo_pick, nodes_own).astype(BF)
    extended = jnp.concatenate([nodes_own, border(halo_out[:depth], halo_out[depth:])], axis=0)

    src_pick = onehot(edge_src[0], count + 2 * depth)
    dst_pick = onehot(edge_dst[0], count)
    source_feat = dot(src_pick, extended).astype(BF)
    target_feat = dot(dst_pick, nodes_own).astype(BF)
    edge_pre = dot(source_feat, edge_a) + dot(target_feat, edge_b) + dot(edges_own, edge_c)
    edge_hidden = (edge_pre * jax.nn.sigmoid(edge_pre)).astype(BF)
    edge_slope = silu_slope(edge_pre)
    gathered = dot_tn(dst_pick, edge_hidden).astype(BF)
    message = dot(gathered, edge_second)

    couple_pick = onehot(couple_target[0, 0], count, couple_weight[0, 0][:, None])
    pooled = (message + dot_tn(couple_pick, received)).astype(BF)
    node_pre = dot(nodes_own, node_a) + dot(pooled, node_b)
    node_hidden = (node_pre * jax.nn.sigmoid(node_pre)).astype(BF)
    new_nodes = (nodes_own.astype(F32) + dot(node_hidden, node_second)).astype(BF)
    grad_node_pre = (dot_nt(cotangent, node_second) * silu_slope(node_pre)).astype(BF)
    grad_pooled = dot_nt(grad_node_pre, node_b).astype(BF)
    node_part = cotangent.astype(F32) + dot_nt(grad_node_pre, node_a)
    returned = dot(couple_pick, grad_pooled).astype(BF).reshape(patches, SLOT, width)
    couple_back = route(returned).reshape(-1, width)

    order = row_order(width, patches)
    late = [
        dot_tn(gathered, grad_pooled) * scale,
        dot_tn(nodes_own, grad_node_pre) * scale,
        dot_tn(pooled, grad_node_pre) * scale,
        dot_tn(node_hidden, cotangent) * scale,
    ]
    late = reduce_blocks(late, order)

    grad_message = dot(dst_pick, grad_pooled).astype(BF)
    grad_edge_pre = (dot_nt(grad_message, edge_second) * edge_slope).astype(BF)
    edge_grads = dot_nt(grad_edge_pre, edge_c).astype(BF)
    by_source = dot_tn(src_pick, grad_edge_pre).astype(BF)
    by_target = dot_tn(dst_pick, grad_edge_pre).astype(BF)
    early = [
        dot_tn(extended, by_source) * scale,
        dot_tn(nodes_own, by_target) * scale,
        dot_tn(edges_own, grad_edge_pre) * scale,
    ]
    early = reduce_blocks(early, order)
    spread = dot_nt(by_source, edge_a)
    halo_grad = spread[count:].astype(BF)
    halo_back = border(halo_grad[:depth], halo_grad[depth:])
    node_total = node_part + dot_nt(by_target, edge_b) + spread[:count]
    node_total = node_total + dot_tn(halo_pick, halo_back) + dot_tn(out_pick, couple_back)
    summed = jnp.concatenate([early, late], axis=0)
    return (new_nodes[None], node_total.astype(BF)[None], edge_grads[None], summed)


def solution(mesh):
    return jax.shard_map(
        shards,
        mesh=mesh,
        in_specs=(
            P("mesh", "patch", None),
            P("mesh", "patch", None),
            P("mesh", "patch", None),
            P(),
            P("mesh", "patch"),
            P("mesh", "patch"),
            P("mesh", "patch"),
            P("mesh", "patch", None),
            P("mesh", "patch", None),
            P("mesh", "patch", None),
            P("mesh", "patch", None),
        ),
        out_specs=(
            P("mesh", "patch", None),
            P("mesh", "patch", None),
            P("mesh", "patch", None),
            P(None, "patch"),
        ),
        check_vma=False,
    )
```

time: 878 us -> 199 us (0.23)
  the two profiles are of different devices: /device:TPU:0 before, /device:TPU:1 now
where the time goes in v1:
time: 199 us; the launch traced here: 197 us
  matrix products  64.9 us (33%)
  waiting for transfers between devices  58.3 us (29%)
  starting transfers between devices  56.5 us (28%)
  other arithmetic  8.56 us (4%)
  local copies, waits for them, and re-layouts  7.15 us (4%)
    dot_general x17, matrix products, dot(): return jnp.dot(a, b, preferred_element_type=F32)  39.6 us
    all_to_all x2, waiting for transfers between devices, route(): lax.all_to_all(from_partner(buffer), 'patch', split_axis=0, concat_axis=0...  22.7 us
    all_to_all x2, waiting for transfers between devices, reduce_blocks(): lax.all_to_all(paired, 'patch', split_axis=0, concat_axis=0, axis_index_g...  21.4 us
    dot_general x7, matrix products, dot_nt(): lax.dot_general(a, b, (((1,), (1,)), ((), ())), preferred_element_type=F32)  15.9 us
    ppermute x4, starting transfers between devices, shift(): lax.ppermute(value, 'patch', [(i, (i + step) % count) for i in range(coun...  15.7 us
    all_to_all x2, waiting for transfers between devices, reduce_blocks(): lax.all_to_all(jnp.concatenate([part, part], axis=0), ('mesh', 'patch'),...  13.6 us
    all_to_all x2, starting transfers between devices, route(): lax.all_to_all(from_partner(buffer), 'patch', split_axis=0, concat_axis=0...  13.6 us
    all_to_all x2, starting transfers between devices, reduce_blocks(): lax.all_to_all(jnp.concatenate([part, part], axis=0), ('mesh', 'patch'),...  10.8 us
  transfers between devices with their start and end apart: 14, of which 8 were waited for; matrix products, arithmetic and copies ran while one was open for 20% of the time, Pallas kernels for 0%

profile of v1, /device:TPU:1, one launch (start us, length us, event | category | flops | bytes accessed | tf_op | source)
XLA Modules:
  0.0 196.5 jit_solution(6210559164382774682)
XLA Ops:
  4.1 3.3 %collective-permute-start.2 = (bf16[128,8,512]{2,1,0:T(8,128)(2,1)S(1)}, bf16[128,8,512]{2,1,0:T(8,128)(2,1)}, u32[]{:S(2)}, u32[]{:S(2)}) collective-permute-start(bf16[128,8,512]{2,1,0:T(8,128)(2,1)S(1)} %fusion.12), channel_id=1, source_target_pairs={{0,128},{128,0},{1,129},{129,1},{2,130},{130,2},{3,131},{131,3},{4... | collective-permute-start | bytes 3145736 | tf_op jit(solution)/shard_map/ppermute | solution.py:15
  7.9 8.6 %collective-permute-start.1 = (bf16[64,512]{1,0:T(8,128)(2,1)S(1)}, bf16[64,512]{1,0:T(8,128)(2,1)S(1)}, u32[]{:S(2)}, u32[]{:S(2)}) collective-permute-start(bf16[64,512]{1,0:T(8,128)(2,1)S(1)} %get-tuple-element.7), channel_id=1, source_target_pairs={{0,127},{1,0},{2,1},{3,2},{4,3},{5,4},{6,5},{7,6},{8,7},{9,8},{10,... | collective-permute-start | bytes 196616 | tf_op jit(solution)/shard_map/ppermute | solution.py:20
  17.9 7.2 %all-to-all-start = ((bf16[128,8,512]{2,1,0:T(8,128)(2,1)}), bf16[128,8,512]{2,1,0:T(8,128)(2,1)S(1)}, u32[]{:S(2)}, u32[]{:S(2)}) async-start(bf16[128,8,512]{2,1,0:T(8,128)(2,1)} %collective-permute-done.2), calls=%async_computation | async-start | bytes 2097152 | tf_op jit(solution)/shard_map/all_to_all | solution.py:28
  25.1 3.9 %fusion.9 = f32[1024,512]{1,0:T(8,128)} fusion(s32[1024]{0:T(1024)S(1)} %bitcast.122, bf16[3584,512]{1,0:T(8,128)(2,1)} %param.14, bf16[1,512,512]{2,1,0:T(8,128)(2,1)} %param.11), kind=kOutput, calls=%fused_computation.36 | convolution fusion | flops 1075838976 | bytes 3149824 | tf_op jit(solution)/shard_map/dot_general | solution.py:32
  29.0 4.1 %fusion.17 = f32[1024,512]{1,0:T(8,128)} fusion(s32[1024]{0:T(1024)S(1)} %bitcast.120, bf16[3584,512]{1,0:T(8,128)(2,1)} %param.14, bf16[64,512]{1,0:T(8,128)(2,1)S(1)} %collective-permute-done.1, bf16[64,512]{1,0:T(8,128)(2,1)S(1)} %collective-permute-done, bf16[512,512]{1,0:T(8,128)(2,1)} %bitcast.110), kind=kOutput, calls=%fused_computation.58 | convolution fusion | flops 1212416000 | bytes 3280896 | tf_op jit(solution)/shard_map/dot_general | solution.py:32
  33.1 3.1 %add_add_fusion = f32[1024,512]{1,0:T(8,128)S(1)} fusion(f32[1024,512]{1,0:T(8,128)} %fusion.17, f32[1024,512]{1,0:T(8,128)} %fusion.9, bf16[1,1024,512]{2,1,0:T(8,128)(2,1)S(1)} %copy-done, bf16[3584,512]{1,0:T(8,128)(2,1)} %param.14), kind=kOutput, calls=%fused_computation.15 | convolution fusion | flops 537919488 | bytes 7864320 | tf_op jit(solution)/shard_map/dot_general | solution.py:32
  40.8 12.8 %all-to-all-done = bf16[128,8,512]{2,1,0:T(8,128)(2,1)S(1)} async-done(((bf16[128,8,512]{2,1,0:T(8,128)(2,1)}), bf16[128,8,512]{2,1,0:T(8,128)(2,1)S(1)}, u32[]{:S(2)}, u32[]{:S(2)}) %all-to-all-start) | async-done | bytes 1048608 | tf_op jit(solution)/shard_map/all_to_all | solution.py:28
  63.5 3.9 %multiply_convert_fusion = bf16[1024,512]{1,0:T(8,128)(2,1)} fusion(f32[1024,512]{1,0:T(8,128)S(1)} %copy-done.2, bf16[512,512]{1,0:T(8,128)(2,1)} %convolution_convert_fusion.10, s32[1024]{0:T(1024)S(1)} %bitcast.124, bf16[3584,512]{1,0:T(8,128)(2,1)} %param.14), kind=kOutput, calls=%fused_computation.8 | convolution fusion | flops 1080557568 | bytes 4198400 | tf_op jit(solution)/shard_map/dot_general | solution.py:40
  71.4 3.3 %fusion.44 = bf16[1,512,512]{2,1,0:T(8,128)(2,1)} fusion(bf16[1024,512]{1,0:T(8,128)(2,1)} %multiply_convert_fusion, bf16[1,1024,512]{2,1,0:T(8,128)(2,1)S(1)} %copy-done, s32[512]{0:T(512)S(1)} %get-tuple-element.10, s32[512]{0:T(512)S(1)} %get-tuple-element.13, s32[512]{0:T(512)S(1)} %get-tuple-element.11, s32[512]{0:T(512)S(1)} %get-tuple-element.12, ...), kind=kOutput, calls=%fused_computation.90 | convolution fusion | flops 812908544 | bytes 2630656 | tf_op jit(solution)/shard_map/dot_general | solution.py:32
  76.4 2.8 %fusion.45 = bf16[1,512,512]{2,1,0:T(8,128)(2,1)} fusion(bf16[512,512]{1,0:T(8,128)(2,1)S(1)} %copy-done.17, bf16[512,512]{1,0:T(8,128)(2,1)} %convolution_convert_fusion.10, s32[512]{0:T(512)S(1)} %get-tuple-element.10, s32[512]{0:T(512)S(1)} %get-tuple-element.13, s32[512]{0:T(512)S(1)} %get-tuple-element.11, s32[512]{0:T(512)S(1)} %get-tuple-element.12, ...), kind=kOutput, calls=%fused_computation.91 | convolution fusion | flops 544473088 | bytes 1582080 | tf_op jit(solution)/shard_map/dot_general | solution.py:32
  79.2 3.3 %fusion.46 = bf16[1,512,512]{2,1,0:T(8,128)(2,1)} fusion(bf16[512,512]{1,0:T(8,128)(2,1)} %copy-done.10, bf16[1,512,512]{2,1,0:T(8,128)(2,1)} %param.11, s32[512]{0:T(512)S(1)} %get-tuple-element.10, s32[512]{0:T(512)S(1)} %get-tuple-element.13, s32[512]{0:T(512)S(1)} %get-tuple-element.11, s32[512]{0:T(512)S(1)} %get-tuple-element.12, ...), kind=kOutput, calls=%fused_computation.92 | convolution fusion | flops 544473088 | bytes 1582080 | tf_op jit(solution)/shard_map/dot_general | solution.py:32
  89.9 3.5 %collective-permute-start.6 = (bf16[3,512,256]{2,1,0:T(8,128)(2,1)S(1)}, bf16[3,512,256]{2,1,0:T(8,128)(2,1)S(1)}, u32[]{:S(2)}, u32[]{:S(2)}) collective-permute-start(bf16[3,512,256]{2,1,0:T(8,128)(2,1)S(1)} %broadcast_select_fusion.1), channel_id=1, source_target_pairs={{0,128},{128,0},{1,129},{129,1},{2,130},{130,2},{3,131},{131,3},{4... | collective-permute-start | bytes 2359304 | tf_op jit(solution)/shard_map/ppermute | solution.py:15
  96.6 4.3 %all-to-all-start.2 = ((bf16[16,3,32,256]{3,2,1,0:T(8,128)(2,1)}), bf16[16,3,32,256]{3,2,1,0:T(8,128)(2,1)}, u32[]{:S(2)}, u32[]{:S(2)}) async-start(bf16[16,3,32,256]{3,2,1,0:T(8,128)(2,1)} %bitcast.108), calls=%async_computation.2 | async-start | bytes 1572864 | tf_op jit(solution)/shard_map/all_to_all | solution.py:72
  103.6 11.1 %all-to-all-done.2 = bf16[16,3,32,256]{3,2,1,0:T(8,128)(2,1)} async-done(((bf16[16,3,32,256]{3,2,1,0:T(8,128)(2,1)}), bf16[16,3,32,256]{3,2,1,0:T(8,128)(2,1)}, u32[]{:S(2)}, u32[]{:S(2)}) %all-to-all-start.2) | async-done | bytes 786464 | tf_op jit(solution)/shard_map/all_to_all | solution.py:72
  114.7 3.7 %all-to-all-start.4 = ((bf16[16,4,32,256]{3,2,1,0:T(8,128)(2,1)}), bf16[16,4,32,256]{3,2,1,0:T(8,128)(2,1)S(1)}, u32[]{:S(2)}, u32[]{:S(2)}) async-start(bf16[16,4,32,256]{3,2,1,0:T(8,128)(2,1)} %bitcast.105), calls=%async_computation.4 | async-start | bytes 2097152 | tf_op jit(solution)/shard_map/all_to_all | solution.py:72
  123.6 10.3 %all-to-all-done.4 = bf16[16,4,32,256]{3,2,1,0:T(8,128)(2,1)S(1)} async-done(((bf16[16,4,32,256]{3,2,1,0:T(8,128)(2,1)}), bf16[16,4,32,256]{3,2,1,0:T(8,128)(2,1)S(1)}, u32[]{:S(2)}, u32[]{:S(2)}) %all-to-all-start.4) | async-done | bytes 1048608 | tf_op jit(solution)/shard_map/all_to_all | solution.py:72
  133.9 6.3 %all-to-all-start.3 = ((bf16[16,3,4,256]{3,2,1,0:T(4,128)(2,1)}), bf16[16,3,4,256]{3,2,1,0:T(4,128)(2,1)S(1)}, u32[]{:S(2)}, u32[]{:S(2)}) async-start(bf16[16,3,4,256]{3,2,1,0:T(4,128)(2,1)} %copy.27), calls=%async_computation.3 | async-start | bytes 196608 | tf_op jit(solution)/shard_map/all_to_all | solution.py:80
  141.2 6.3 %all-to-all-done.3 = bf16[16,3,4,256]{3,2,1,0:T(4,128)(2,1)S(1)} async-done(((bf16[16,3,4,256]{3,2,1,0:T(4,128)(2,1)}), bf16[16,3,4,256]{3,2,1,0:T(4,128)(2,1)S(1)}, u32[]{:S(2)}, u32[]{:S(2)}) %all-to-all-start.3) | async-done | bytes 98336 | tf_op jit(solution)/shard_map/all_to_all | solution.py:80
  147.5 4.5 %all-to-all-start.5 = ((bf16[16,4,4,256]{3,2,1,0:T(4,128)(2,1)}), bf16[16,4,4,256]{3,2,1,0:T(4,128)(2,1)S(1)}, u32[]{:S(2)}, u32[]{:S(2)}) async-start(bf16[16,4,4,256]{3,2,1,0:T(4,128)(2,1)} %copy.31), calls=%async_computation.5 | async-start | bytes 262144 | tf_op jit(solution)/shard_map/all_to_all | solution.py:80
  152.0 7.4 %all-to-all-done.5 = bf16[16,4,4,256]{3,2,1,0:T(4,128)(2,1)S(1)} async-done(((bf16[16,4,4,256]{3,2,1,0:T(4,128)(2,1)}), bf16[16,4,4,256]{3,2,1,0:T(4,128)(2,1)S(1)}, u32[]{:S(2)}, u32[]{:S(2)}) %all-to-all-start.5) | async-done | bytes 131104 | tf_op jit(solution)/shard_map/all_to_all | solution.py:80
  159.3 6.4 %all-to-all-start.1 = ((bf16[128,8,512]{2,1,0:T(8,128)(2,1)}), bf16[128,8,512]{2,1,0:T(8,128)(2,1)S(1)}, u32[]{:S(2)}, u32[]{:S(2)}) async-start(bf16[128,8,512]{2,1,0:T(8,128)(2,1)} %collective-permute-done.5), calls=%async_computation.1 | async-start | bytes 2097152 | tf_op jit(solution)/shard_map/all_to_all | solution.py:28
  168.9 6.5 %collective-permute-start.4 = (bf16[64,512]{1,0:T(8,128)(2,1)}, bf16[64,512]{1,0:T(8,128)(2,1)S(1)}, u32[]{:S(2)}, u32[]{:S(2)}) collective-permute-start(bf16[64,512]{1,0:T(8,128)(2,1)} %get-tuple-element.5), channel_id=1, source_target_pairs={{0,127},{1,0},{2,1},{3,2},{4,3},{5,4},{6,5},{7,6},{8,7},{9,8},{10,... | collective-permute-start | bytes 196616 | tf_op jit(solution)/shard_map/ppermute | solution.py:20
  175.4 2.7 %fusion.14 = bf16[1,1024,512]{2,1,0:T(8,128)(2,1)} fusion(bf16[1024,512]{1,0:T(8,128)(2,1)S(1)} %copy-done.33, bf16[3584,512]{1,0:T(8,128)(2,1)} %param.14), kind=kOutput, calls=%fused_computation.54 | convolution fusion | flops 537395200 | bytes 2621440 | tf_op jit(solution)/shard_map/dot_general | solution.py:40
  184.5 9.8 %all-to-all-done.1 = bf16[128,8,512]{2,1,0:T(8,128)(2,1)S(1)} async-done(((bf16[128,8,512]{2,1,0:T(8,128)(2,1)}), bf16[128,8,512]{2,1,0:T(8,128)(2,1)S(1)}, u32[]{:S(2)}, u32[]{:S(2)}) %all-to-all-start.1) | async-done | bytes 1048608 | tf_op jit(solution)/shard_map/all_to_all | solution.py:28
  (133 shorter events, 56.4 us)
Async XLA Ops:
  0.6 32.5 %copy-start = (bf16[1,1024,512]{2,1,0:T(8,128)(2,1)S(1)}, bf16[1,1024,512]{2,1,0:T(8,128)(2,1)}, u32[]{:S(2)}) copy-start(bf16[1,1024,512]{2,1,0:T(8,128)(2,1)} %param.12) | copy-start | bytes 3145732
  4.1 13.8 %collective-permute-start.2 = (bf16[128,8,512]{2,1,0:T(8,128)(2,1)S(1)}, bf16[128,8,512]{2,1,0:T(8,128)(2,1)}, u32[]{:S(2)}, u32[]{:S(2)}) collective-permute-start(bf16[128,8,512]{2,1,0:T(8,128)(2,1)S(1)} %fusion.12), channel_id=1, source_target_pairs={{0,128},{128,0},{1,129},{129,1},{2,130},{130,2},{3,131},{131,3},{4... | collective-permute-start | bytes 3145736 | tf_op jit(solution)/shard_map/ppermute | solution.py:15
  7.8 21.3 %collective-permute-start = (bf16[64,512]{1,0:T(8,128)(2,1)S(1)}, bf16[64,512]{1,0:T(8,128)(2,1)S(1)}, u32[]{:S(2)}, u32[]{:S(2)}) collective-permute-start(bf16[64,512]{1,0:T(8,128)(2,1)S(1)} %get-tuple-element.6), channel_id=1, source_target_pairs={{0,1},{1,2},{2,3},{3,4},{4,5},{5,6},{6,7},{7,8},{8,9},{9,10},{10,1... | collective-permute-start | bytes 196616 | tf_op jit(solution)/shard_map/ppermute | solution.py:20
  7.8 17.3 %copy-start.28 = (s32[1,1024]{1,0:T(1,128)S(1)}, s32[1,1024]{1,0:T(1,128)}, u32[]{:S(2)}) copy-start(s32[1,1024]{1,0:T(1,128)} %param.16) | copy-start | bytes 12292
  7.9 21.2 %collective-permute-start.1 = (bf16[64,512]{1,0:T(8,128)(2,1)S(1)}, bf16[64,512]{1,0:T(8,128)(2,1)S(1)}, u32[]{:S(2)}, u32[]{:S(2)}) collective-permute-start(bf16[64,512]{1,0:T(8,128)(2,1)S(1)} %get-tuple-element.7), channel_id=1, source_target_pairs={{0,127},{1,0},{2,1},{3,2},{4,3},{5,4},{6,5},{7,6},{8,7},{9,8},{10,... | collective-permute-start | bytes 196616 | tf_op jit(solution)/shard_map/ppermute | solution.py:20
  17.9 35.7 %all-to-all-start = ((bf16[128,8,512]{2,1,0:T(8,128)(2,1)}), bf16[128,8,512]{2,1,0:T(8,128)(2,1)S(1)}, u32[]{:S(2)}, u32[]{:S(2)}) async-start(bf16[128,8,512]{2,1,0:T(8,128)(2,1)} %collective-permute-done.2), calls=%async_computation | async-start | bytes 2097152 | tf_op jit(solution)/shard_map/all_to_all | solution.py:28
  38.3 15.3 %copy-start.29 = (f32[1,1,1024]{2,1,0:T(1,128)S(1)}, f32[1,1,1024]{2,1,0:T(1,128)}, u32[]{:S(2)}) copy-start(f32[1,1,1024]{2,1,0:T(1,128)} %param.21) | copy-start | bytes 12292
  38.3 15.3 %copy-start.30 = (s32[1,1,1024]{2,1,0:T(1,128)S(1)}, s32[1,1,1024]{2,1,0:T(1,128)}, u32[]{:S(2)}) copy-start(s32[1,1,1024]{2,1,0:T(1,128)} %param.20) | copy-start | bytes 12292
  69.7 16.9 %copy-start.6 = (bf16[640,512]{1,0:T(8,128)(2,1)}, bf16[640,512]{1,0:T(8,128)(2,1)S(1)}, u32[]{:S(2)}) copy-start(bf16[640,512]{1,0:T(8,128)(2,1)S(1)} %fusion.15) | copy-start | bytes 1966084
  89.9 5.4 %collective-permute-start.6 = (bf16[3,512,256]{2,1,0:T(8,128)(2,1)S(1)}, bf16[3,512,256]{2,1,0:T(8,128)(2,1)S(1)}, u32[]{:S(2)}, u32[]{:S(2)}) collective-permute-start(bf16[3,512,256]{2,1,0:T(8,128)(2,1)S(1)} %broadcast_select_fusion.1), channel_id=1, source_target_pairs={{0,128},{128,0},{1,129},{129,1},{2,130},{130,2},{3,131},{131,3},{4... | collective-permute-start | bytes 2359304 | tf_op jit(solution)/shard_map/ppermute | solution.py:15
  94.8 6.1 %collective-permute-start.7 = (bf16[4,512,256]{2,1,0:T(8,128)(2,1)}, bf16[4,512,256]{2,1,0:T(8,128)(2,1)}, u32[]{:S(2)}, u32[]{:S(2)}) collective-permute-start(bf16[4,512,256]{2,1,0:T(8,128)(2,1)} %broadcast_select_fusion), channel_id=1, source_target_pairs={{0,128},{128,0},{1,129},{129,1},{2,130},{130,2},{3,131},{131,3},{4... | collective-permute-start | bytes 3145736 | tf_op jit(solution)/shard_map/ppermute | solution.py:15
  96.6 18.1 %all-to-all-start.2 = ((bf16[16,3,32,256]{3,2,1,0:T(8,128)(2,1)}), bf16[16,3,32,256]{3,2,1,0:T(8,128)(2,1)}, u32[]{:S(2)}, u32[]{:S(2)}) async-start(bf16[16,3,32,256]{3,2,1,0:T(8,128)(2,1)} %bitcast.108), calls=%async_computation.2 | async-start | bytes 1572864 | tf_op jit(solution)/shard_map/all_to_all | solution.py:72
  102.5 15.9 %copy-start.31 = (bf16[512,512]{1,0:T(8,128)(2,1)S(1)}, bf16[512,512]{1,0:T(8,128)(2,1)}, u32[]{:S(2)}) copy-start(bf16[512,512]{1,0:T(8,128)(2,1)} %convolution_convert_fusion.10) | copy-start | bytes 1572868
  114.7 19.2 %all-to-all-start.4 = ((bf16[16,4,32,256]{3,2,1,0:T(8,128)(2,1)}), bf16[16,4,32,256]{3,2,1,0:T(8,128)(2,1)S(1)}, u32[]{:S(2)}, u32[]{:S(2)}) async-start(bf16[16,4,32,256]{3,2,1,0:T(8,128)(2,1)} %bitcast.105), calls=%async_computation.4 | async-start | bytes 2097152 | tf_op jit(solution)/shard_map/all_to_all | solution.py:72
  120.2 31.8 %collective-permute-start.5 = (bf16[128,8,512]{2,1,0:T(8,128)(2,1)}, bf16[128,8,512]{2,1,0:T(8,128)(2,1)}, u32[]{:S(2)}, u32[]{:S(2)}) collective-permute-start(bf16[128,8,512]{2,1,0:T(8,128)(2,1)} %fusion.13), channel_id=1, source_target_pairs={{0,128},{128,0},{1,129},{129,1},{2,130},{130,2},{3,131},{131,3},{4... | collective-permute-start | bytes 3145736 | tf_op jit(solution)/shard_map/ppermute | solution.py:15
  133.9 13.6 %all-to-all-start.3 = ((bf16[16,3,4,256]{3,2,1,0:T(4,128)(2,1)}), bf16[16,3,4,256]{3,2,1,0:T(4,128)(2,1)S(1)}, u32[]{:S(2)}, u32[]{:S(2)}) async-start(bf16[16,3,4,256]{3,2,1,0:T(4,128)(2,1)} %copy.27), calls=%async_computation.3 | async-start | bytes 196608 | tf_op jit(solution)/shard_map/all_to_all | solution.py:80
  147.5 11.8 %all-to-all-start.5 = ((bf16[16,4,4,256]{3,2,1,0:T(4,128)(2,1)}), bf16[16,4,4,256]{3,2,1,0:T(4,128)(2,1)S(1)}, u32[]{:S(2)}, u32[]{:S(2)}) async-start(bf16[16,4,4,256]{3,2,1,0:T(4,128)(2,1)} %copy.31), calls=%async_computation.5 | async-start | bytes 262144 | tf_op jit(solution)/shard_map/all_to_all | solution.py:80
  159.3 35.0 %all-to-all-start.1 = ((bf16[128,8,512]{2,1,0:T(8,128)(2,1)}), bf16[128,8,512]{2,1,0:T(8,128)(2,1)S(1)}, u32[]{:S(2)}, u32[]{:S(2)}) async-start(bf16[128,8,512]{2,1,0:T(8,128)(2,1)} %collective-permute-done.5), calls=%async_computation.1 | async-start | bytes 2097152 | tf_op jit(solution)/shard_map/all_to_all | solution.py:28
  167.6 10.5 %copy-start.9 = (bf16[1,512,512]{2,1,0:T(8,128)(2,1)S(1)}, bf16[1,512,512]{2,1,0:T(8,128)(2,1)}, u32[]{:S(2)}) copy-start(bf16[1,512,512]{2,1,0:T(8,128)(2,1)} %param.13) | copy-start | bytes 1572868
  167.7 10.5 %copy-start.12 = (bf16[512,512]{1,0:T(8,128)(2,1)S(1)}, bf16[512,512]{1,0:T(8,128)(2,1)}, u32[]{:S(2)}) copy-start(bf16[512,512]{1,0:T(8,128)(2,1)} %copy-done.10) | copy-start | bytes 1572868
  168.3 27.0 %collective-permute-start.3 = (bf16[64,512]{1,0:T(8,128)(2,1)}, bf16[64,512]{1,0:T(8,128)(2,1)S(1)}, u32[]{:S(2)}, u32[]{:S(2)}) collective-permute-start(bf16[64,512]{1,0:T(8,128)(2,1)} %get-tuple-element.4), channel_id=1, source_target_pairs={{0,1},{1,2},{2,3},{3,4},{4,5},{5,6},{6,7},{7,8},{8,9},{9,10},{10,1... | collective-permute-start | bytes 196616 | tf_op jit(solution)/shard_map/ppermute | solution.py:20
  168.9 10.8 %copy-start.5 = (f32[512,512]{1,0:T(8,128)S(1)}, f32[512,512]{1,0:T(8,128)}, u32[]{:S(2)}) copy-start(f32[512,512]{1,0:T(8,128)} %copy-done.3) | copy-start | bytes 3145732
  168.9 10.8 %copy-start.15 = (bf16[1,512,512]{2,1,0:T(8,128)(2,1)S(1)}, bf16[1,512,512]{2,1,0:T(8,128)(2,1)}, u32[]{:S(2)}) copy-start(bf16[1,512,512]{2,1,0:T(8,128)(2,1)} %param.11) | copy-start | bytes 1572868
  168.9 26.5 %collective-permute-start.4 = (bf16[64,512]{1,0:T(8,128)(2,1)}, bf16[64,512]{1,0:T(8,128)(2,1)S(1)}, u32[]{:S(2)}, u32[]{:S(2)}) collective-permute-start(bf16[64,512]{1,0:T(8,128)(2,1)} %get-tuple-element.5), channel_id=1, source_target_pairs={{0,127},{1,0},{2,1},{3,2},{4,3},{5,4},{6,5},{7,6},{8,7},{9,8},{10,... | collective-permute-start | bytes 196616 | tf_op jit(solution)/shard_map/ppermute | solution.py:20
  (24 other events, 83.2 us)

commit v2 on v1

v2 whole, which is shorter than its diff:
```python
import math

import jax
import jax.numpy as jnp
from jax import lax
from jax.experimental import pallas as pl
from jax.experimental.pallas import tpu as pltpu
from jax.sharding import PartitionSpec as P

SLOT = 8
PLANE = 16
TILE = 256
BF = jnp.bfloat16
F32 = jnp.float32
I32 = jnp.int32
VMEM = pl.BlockSpec(memory_space=pltpu.VMEM)
SMEM = pl.BlockSpec(memory_space=pltpu.SMEM)


def dot(a, b):
    return jnp.dot(a, b, preferred_element_type=F32)


def dot_nt(a, b):
    return lax.dot_general(a, b, (((1,), (1,)), ((), ())), preferred_element_type=F32)


def column(row):
    return jnp.transpose(jnp.broadcast_to(row.astype(F32), (128, row.shape[1])))


def pick(col, count, value=None):
    base = lax.broadcasted_iota(I32, (col.shape[0], 128), 1).astype(F32)
    one = jnp.ones_like(base) if value is None else value
    parts = [jnp.where(col == base + float(k), one, 0.0).astype(BF) for k in range(0, count, 128)]
    return parts[0] if len(parts) == 1 else jnp.concatenate(parts, axis=1)


def pick_t(row, start, size, value=None):
    base = lax.broadcasted_iota(I32, (size, row.shape[1]), 0) + start
    one = jnp.ones(base.shape, F32) if value is None else jnp.broadcast_to(value, base.shape)
    return jnp.where(base == row, one, 0.0).astype(BF)


def row_order(width, patches):
    fine = width // patches
    depth = patches // PLANE
    row = lax.broadcasted_iota(I32, (width, width), 0)
    col = lax.broadcasted_iota(I32, (width, width), 1)
    plane, rest = row // (depth * fine), row % (depth * fine)
    source = ((rest // fine) * PLANE + plane) * fine + rest % fine
    return jnp.where(col == source, 1.0, 0.0).astype(BF)


def tiles(count):
    return [slice(i, i + TILE) for i in range(0, count, TILE)]


def call(kernel, args, outs, scratch=(), specs=None, flops=0):
    size = sum(math.prod(a.shape) * a.dtype.itemsize for a in list(args) + list(outs))
    return pl.pallas_call(
        kernel,
        out_shape=tuple(outs),
        in_specs=specs or [VMEM] * len(args),
        out_specs=tuple([VMEM] * len(outs)),
        scratch_shapes=list(scratch),
        compiler_params=pltpu.CompilerParams(vmem_limit_bytes=40 * 2**20),
        cost_estimate=pl.CostEstimate(flops=flops, bytes_accessed=size, transcendentals=0),
    )(*args)


def shape(dtype, *dims):
    return jax.ShapeDtypeStruct(dims, dtype)


def send_kernel(rows_ref, count_ref, halo_ref, nodes_ref, out_ref, low_ref, high_ref, live_ref):
    slots = rows_ref.shape[1]
    patches = count_ref.shape[1]
    width = nodes_ref.shape[0]
    owner = lax.broadcasted_iota(I32, (patches, slots), 0)
    place = lax.broadcasted_iota(I32, (patches, slots), 1)
    repeat = jnp.where(place // SLOT == owner, 1.0, 0.0).astype(BF)
    counts = jnp.broadcast_to(count_ref[...].astype(F32), (8, patches)).astype(BF)
    spread = dot(counts, repeat)[:1].astype(I32)
    slot = lax.broadcasted_iota(I32, (1, slots), 1) % SLOT
    live = jnp.where(slot < spread, rows_ref[...], -1)
    live_ref[...] = live
    nodes = nodes_ref[...]
    depth = low_ref.shape[0]
    halo = dot(pick(column(halo_ref[...]), width), nodes).astype(BF)
    low_ref[...] = halo[:depth]
    high_ref[...] = halo[depth:]
    col = column(live)
    for r in tiles(slots):
        out_ref[r] = dot(pick(col[r], width), nodes).astype(BF)


def edge_kernel(
    src_ref, dst_ref, nodes_ref, low_ref, high_ref, edges_ref, w_ref, slope_ref, agg_ref, msg_ref, hid_ref
):
    count, width = nodes_ref.shape
    inner = edges_ref.shape[0] - edges_ref.shape[0] // 4
    src = column(src_ref[...])
    dst = column(dst_ref[...])
    nodes = nodes_ref[...]
    halo = jnp.concatenate([low_ref[...], high_ref[...]], axis=0)
    for r in tiles(edges_ref.shape[0]):
        if r.stop <= inner:
            feat = dot(pick(src[r], count), nodes).astype(BF)
        else:
            feat = dot(pick(src[r] - float(count), halo.shape[0]), halo).astype(BF)
        own = dot(pick(dst[r], count), nodes).astype(BF)
        pre = (
            dot(feat, w_ref[:width])
            + dot(own, w_ref[width : 2 * width])
            + dot(edges_ref[r], w_ref[2 * width : 3 * width])
        )
        sigma = jax.nn.sigmoid(pre)
        hid_ref[r] = (pre * sigma).astype(BF)
        slope_ref[r] = (sigma * (1.0 + pre * (1.0 - sigma))).astype(BF)
    for r in tiles(count):
        agg = dot(pick_t(dst_ref[...], r.start, TILE), hid_ref[...]).astype(BF)
        agg_ref[r] = agg
        msg_ref[r] = dot(agg, w_ref[3 * width : 4 * width])


def node_kernel(
    target_ref, margin_ref, nodes_ref, cot_ref, msg_ref, recv_ref, w_ref,
    new_ref, pooled_ref, hid_ref, gpre_ref, gpool_ref, part_ref, ret_ref,
):
    count, width = nodes_ref.shape
    node_a = w_ref[4 * width : 5 * width]
    node_b = w_ref[5 * width : 6 * width]
    second = w_ref[6 * width :]
    target, margin = target_ref[...], margin_ref[...]
    for r in tiles(count):
        coupled = dot(pick_t(target, r.start, TILE, margin), recv_ref[...])
        pooled = (msg_ref[r] + coupled).astype(BF)
        pooled_ref[r] = pooled
        nodes = nodes_ref[r]
        pre = dot(nodes, node_a) + dot(pooled, node_b)
        sigma = jax.nn.sigmoid(pre)
        hidden = (pre * sigma).astype(BF)
        hid_ref[r] = hidden
        slope = sigma * (1.0 + pre * (1.0 - sigma))
        cot = cot_ref[r]
        gpre = (dot_nt(cot, second) * slope).astype(BF)
        gpre_ref[r] = gpre
        gpool_ref[r] = dot_nt(gpre, node_b).astype(BF)
        new_ref[r] = (nodes.astype(F32) + dot(hidden, second)).astype(BF)
        part_ref[r] = cot.astype(F32) + dot_nt(gpre, node_a)
    col, weight = column(target), column(margin)
    gpool = gpool_ref[...]
    for r in tiles(recv_ref.shape[0]):
        ret_ref[r] = dot(pick(col[r], count, weight[r]), gpool).astype(BF)


def put(own_ref, send_ref, index, value, first):
    half = value.shape[1] // 2
    planes, fine = own_ref.shape[0], own_ref.shape[2]
    value = value.reshape(planes, fine, 2 * half)
    left, right = value[:, :, :half], value[:, :, half:]
    own_ref[:, index] = jnp.where(first, left, right).astype(BF)
    send_ref[:, index] = jnp.where(first, right, left).astype(BF)


def node_grad_kernel(
    side_ref, agg_ref, nodes_ref, pooled_ref, hid_ref, gpre_ref, gpool_ref, cot_ref, own_ref, send_ref,
    *, patches, scale
):
    order = row_order(nodes_ref.shape[1], patches)
    first = side_ref[0] == 0
    pairs = [(agg_ref, gpool_ref), (nodes_ref, gpre_ref), (pooled_ref, gpre_ref), (hid_ref, cot_ref)]
    for index, (left, right) in enumerate(pairs):
        turned = dot_nt(order, left[...]).astype(BF)
        put(own_ref, send_ref, index, dot(turned, right[...]) * scale, first)


def edge_grad_kernel(
    side_ref, src_ref, dst_ref, nodes_ref, low_ref, high_ref, edges_ref, slope_ref, gpool_ref, w_ref,
    own_ref, send_ref, gpre_ref, bysrc_ref, bydst_ref, glow_ref, ghigh_ref,
    *, patches, scale
):
    count, width = nodes_ref.shape
    inner = edges_ref.shape[0] - edges_ref.shape[0] // 4
    depth = low_ref.shape[0]
    first = side_ref[0] == 0
    gpool = gpool_ref[...]
    second = w_ref[3 * width : 4 * width]
    dst_row, src_row = dst_ref[...], src_ref[...]
    dst = column(dst_row)
    for r in tiles(edges_ref.shape[0]):
        message = dot(pick(dst[r], count), gpool).astype(BF)
        gpre_ref[r] = (dot_nt(message, second) * slope_ref[r].astype(F32)).astype(BF)
    order = row_order(width, patches)
    turned = dot_nt(order, edges_ref[...]).astype(BF)
    put(own_ref, send_ref, 2, dot(turned, gpre_ref[...]) * scale, first)
    for r in tiles(count):
        bydst_ref[r] = dot(pick_t(dst_row, r.start, TILE), gpre_ref[...]).astype(BF)
        bysrc_ref[r] = dot(pick_t(src_row[:, :inner], r.start, TILE), gpre_ref[:inner]).astype(BF)
    halo = dot(pick_t(src_row[:, inner:], count, 2 * depth), gpre_ref[inner:]).astype(BF)
    turned = dot_nt(order, nodes_ref[...]).astype(BF)
    put(own_ref, send_ref, 1, dot(turned, bydst_ref[...]) * scale, first)
    rim = dot_nt(order, jnp.concatenate([low_ref[...], high_ref[...]], axis=0)).astype(BF)
    put(own_ref, send_ref, 0, (dot(turned, bysrc_ref[...]) + dot(rim, halo)) * scale, first)
    back = dot_nt(halo, w_ref[:width]).astype(BF)
    glow_ref[...] = back[:depth]
    ghigh_ref[...] = back[depth:]


def edge_rest_kernel(gpre_ref, bysrc_ref, bydst_ref, part_ref, w_ref, edge_ref, total_ref):
    count, width = bysrc_ref.shape
    for r in tiles(gpre_ref.shape[0]):
        edge_ref[r] = dot_nt(gpre_ref[r], w_ref[2 * width : 3 * width]).astype(BF)
    for r in tiles(count):
        total_ref[r] = (
            part_ref[r]
            + dot_nt(bysrc_ref[r], w_ref[:width])
            + dot_nt(bydst_ref[r], w_ref[width : 2 * width])
        )


def last_kernel(live_ref, halo_ref, total_ref, low_ref, high_ref, back_ref, out_ref):
    halo_back = jnp.concatenate([low_ref[...], high_ref[...]], axis=0)
    for r in tiles(total_ref.shape[0]):
        out_ref[r] = (
            total_ref[r]
            + dot(pick_t(halo_ref[...], r.start, TILE), halo_back)
            + dot(pick_t(live_ref[...], r.start, TILE), back_ref[...])
        ).astype(BF)


def from_partner(value):
    return lax.ppermute(value, "mesh", [(0, 1), (1, 0)])


def shift(value, step):
    count = lax.axis_size("patch")
    return lax.ppermute(value, "patch", [(i, (i + step) % count) for i in range(count)])


def route(buffer):
    rows, width = buffer.shape
    patches = lax.axis_size("patch")
    crossed = from_partner(buffer).reshape(patches, rows // patches, width)
    routed = lax.all_to_all(crossed, "patch", split_axis=0, concat_axis=0, tiled=True)
    return routed.reshape(rows, width)


def reduce_blocks(own, send):
    planes, count, rest, half = own.shape
    patches = lax.axis_size("patch")
    depth = patches // PLANE
    fine = rest // depth
    paired = (own.astype(F32) + from_partner(send).astype(F32)).astype(BF)
    groups = [[z * PLANE + i for i in range(PLANE)] for z in range(depth)]
    spread = lax.all_to_all(
        paired, "patch", split_axis=0, concat_axis=0, axis_index_groups=groups, tiled=True
    )
    part = jnp.sum(spread.astype(F32), axis=0).astype(BF)
    part = part.reshape(count, depth, fine, half).transpose(1, 0, 2, 3)
    columns = [
        [m * patches + z * PLANE + i for m in range(2) for z in range(depth)] for i in range(PLANE)
    ]
    both = lax.all_to_all(
        jnp.concatenate([part, part], axis=0),
        ("mesh", "patch"),
        split_axis=0,
        concat_axis=0,
        axis_index_groups=columns,
        tiled=True,
    )
    total = jnp.sum(both.reshape(2, depth, count, fine, half).astype(F32), axis=1)
    return total.transpose(1, 2, 0, 3).reshape(count, fine * 2 * half)


def shards(
    nodes,
    edges,
    cot_nodes,
    weights,
    edge_src,
    edge_dst,
    halo_rows,
    couple_rows,
    couple_count,
    couple_target,
    couple_weight,
):
    nodes_own = nodes[0]
    edges_own = edges[0]
    cotangent = cot_nodes[0]
    count, width = nodes_own.shape
    edge_count = edges_own.shape[0]
    depth = halo_rows.shape[1] // 2
    patches = lax.axis_size("patch")
    slots = couple_rows.shape[2]
    scale = 1.0 / math.sqrt(2 * patches * edge_count)
    side = lax.axis_index("mesh").astype(I32).reshape(1)
    target, margin = couple_target[0], couple_weight[0]
    unit = 2 * width * width

    outgoing, low_out, high_out, live = call(
        send_kernel,
        (couple_rows[0], couple_count[0], halo_rows, nodes_own),
        (shape(BF, slots, width), shape(BF, depth, width), shape(BF, depth, width), shape(I32, 1, slots)),
        flops=(slots + 2 * depth) * unit,
    )
    low, high = shift(high_out, 1), shift(low_out, -1)
    received = route(outgoing)
    slope, agg, message = call(
        edge_kernel,
        (edge_src, edge_dst, nodes_own, low, high, edges_own, weights),
        (shape(BF, edge_count, width), shape(BF, count, width), shape(F32, count, width)),
        scratch=(pltpu.VMEM((edge_count, width), BF),),
        flops=edge_count * 6 * unit,
    )
    square = shape(BF, count, width)
    new_nodes, pooled, hidden, grad_pre, grad_pooled, part, returned = call(
        node_kernel,
        (target, margin, nodes_own, cotangent, message, received, weights),
        (square, square, square, square, square, shape(F32, count, width), shape(BF, slots, width)),
        flops=count * 10 * unit,
    )
    couple_back = route(returned)
    grad_shape = lambda blocks: shape(BF, PLANE, blocks, width // PLANE, width // 2)
    own, send = call(
        lambda *refs: node_grad_kernel(*refs, patches=patches, scale=scale),
        (side, agg, nodes_own, pooled, hidden, grad_pre, grad_pooled, cotangent),
        (grad_shape(4), grad_shape(4)),
        specs=[SMEM] + [VMEM] * 7,
        flops=count * 8 * unit,
    )
    late = reduce_blocks(own, send)
    own, send, grad_edge_pre, by_source, by_target, grad_low, grad_high = call(
        lambda *refs: edge_grad_kernel(*refs, patches=patches, scale=scale),
        (side, edge_src, edge_dst, nodes_own, low, high, edges_own, slope, grad_pooled, weights),
        (
            grad_shape(3), grad_shape(3), shape(BF, edge_count, width), square, square,
            shape(BF, depth, width), shape(BF, depth, width),
        ),
        specs=[SMEM] + [VMEM] * 9,
        flops=edge_count * 8 * unit,
    )
    early = reduce_blocks(own, send)
    back_low, back_high = shift(grad_high, 1), shift(grad_low, -1)
    edge_grads, total = call(
        edge_rest_kernel,
        (grad_edge_pre, by_source, by_target, part, weights),
        (shape(BF, edge_count, width), shape(F32, count, width)),
        flops=edge_count * 2 * unit,
    )
    (node_grads,) = call(
        last_kernel,
        (live, halo_rows, total, back_low, back_high, couple_back),
        (square,),
        flops=count * 2 * unit,
    )
    summed = jnp.concatenate([early, late], axis=0)
    return (new_nodes[None], node_grads[None], edge_grads[None], summed)


def solution(mesh):
    return jax.shard_map(
        shards,
        mesh=mesh,
        in_specs=(
            P("mesh", "patch", None),
            P("mesh", "patch", None),
            P("mesh", "patch", None),
            P(),
            P("mesh", "patch"),
            P("mesh", "patch"),
            P("mesh", "patch"),
            P("mesh", "patch", None),
            P("mesh", "patch", None),
            P("mesh", "patch", None),
            P("mesh", "patch", None),
        ),
        out_specs=(
            P("mesh", "patch", None),
            P("mesh", "patch", None),
            P("mesh", "patch", None),
            P(None, "patch"),
        ),
        check_vma=False,
    )
```

time: 199 us -> 188 us (0.945)
  matrix products: 64.9 us -> 0 us
  Pallas kernels: 0 us -> 20.5 us
  waiting for transfers between devices: 58.3 us -> 75.7 us
  local copies, waits for them, and re-layouts: 7.15 us -> 21.8 us
  starting transfers between devices: 56.5 us -> 61.3 us
  other arithmetic: 8.56 us -> 6.25 us
    dot_general x30 -> x0, matrix products: 64.9 us -> none  [the longest x17 39.6 us: dot(): return jnp.dot(a, b, preferred_element_type=F32)]
    ppermute x4, waiting for transfers between devices: 0.19 us -> 37 us  [shift(): lax.ppermute(value, 'patch', [(i, (i + step) % count) for i in range(coun...]
    all_to_all x2, waiting for transfers between devices: 22.7 us -> 0.01 us  [route(): lax.all_to_all(crossed, 'patch', split_axis=0, concat_axis=0, tiled=True)]
    pallas_call x0 -> x7, Pallas kernels: none -> 20.5 us  [call(): pl.pallas_call(kernel, out_shape=tuple(outs), in_specs=specs or [VMEM] *...]
    unnamed x68, local copies, waits for them, and re-layouts: 2.79 us -> 20.2 us
    all_to_all x2, starting transfers between devices: 13.6 us -> 20.3 us  [route(): lax.all_to_all(crossed, 'patch', split_axis=0, concat_axis=0, tiled=True)]
    convert_element_type x2, other arithmetic: 1.91 us -> 3.94 us  [reduce_blocks(): paired = (own.astype(F32) + from_partner(send).astype(F32)).astype(BF)]
    reshape x4 -> x2, local copies, waits for them, and re-layouts: 2.09 us -> 0.07 us  [reduce_blocks(): return total.transpose(1, 2, 0, 3).reshape(count, fine * 2 * half)]
  transfers between devices with their start and end apart: 14 -> 14, of which waited for: 8 -> 7; matrix products, arithmetic and copies ran while one was open for 20% -> 4% of each run, Pallas kernels for 0% -> 5%
where the time goes in v2:
time: 188 us; the launch traced here: 186 us
  waiting for transfers between devices  75.7 us (40%)
  starting transfers between devices  61.3 us (33%)
  local copies, waits for them, and re-layouts  21.8 us (12%)
  Pallas kernels  20.5 us (11%)
  other arithmetic  6.25 us (3%)
    ppermute x4, waiting for transfers between devices, shift(): lax.ppermute(value, 'patch', [(i, (i + step) % count) for i in range(coun...  37 us
    all_to_all x2, waiting for transfers between devices, reduce_blocks(): lax.all_to_all(paired, 'patch', split_axis=0, concat_axis=0, axis_index_g...  22.6 us
    pallas_call x7, Pallas kernels, call(): pl.pallas_call(kernel, out_shape=tuple(outs), in_specs=specs or [VMEM] *...  20.5 us
    all_to_all x2, starting transfers between devices, route(): lax.all_to_all(crossed, 'patch', split_axis=0, concat_axis=0, tiled=True)  20.3 us
    unnamed x68, local copies, waits for them, and re-layouts  20.2 us
    ppermute x4, starting transfers between devices, shift(): lax.ppermute(value, 'patch', [(i, (i + step) % count) for i in range(coun...  14.1 us
    all_to_all x2, waiting for transfers between devices, reduce_blocks(): lax.all_to_all(jnp.concatenate([part, part], axis=0), ('mesh', 'patch'),...  13.7 us
    all_to_all x2, starting transfers between devices, reduce_blocks(): lax.all_to_all(jnp.concatenate([part, part], axis=0), ('mesh', 'patch'),...  11.8 us
  transfers between devices with their start and end apart: 14, of which 7 were waited for; matrix products, arithmetic and copies ran while one was open for 4% of the time, Pallas kernels for 5%

profile of v2, /device:TPU:1, one launch (start us, length us, event | category | flops | bytes accessed | tf_op | source)
XLA Modules:
  0.0 186.4 jit_solution(16757213650074589852)
XLA Ops:
  4.6 3.3 %collective-permute-start.2 = (bf16[1024,512]{1,0:T(8,128)(2,1)S(1)}, bf16[1024,512]{1,0:T(8,128)(2,1)}, u32[]{:S(2)}, u32[]{:S(2)}) collective-permute-start(bf16[1024,512]{1,0:T(8,128)(2,1)S(1)} %get-tuple-element.32), channel_id=1, source_target_pairs={{0,128},{128,0},{1,129},{129,1},{2,130},{130,2},{3,131},{131,3},{4... | collective-permute-start | bytes 3145736 | tf_op jit(solution)/shard_map/ppermute | solution.py:234
  8.0 2.4 %collective-permute-done.2 = bf16[1024,512]{1,0:T(8,128)(2,1)} collective-permute-done((bf16[1024,512]{1,0:T(8,128)(2,1)S(1)}, bf16[1024,512]{1,0:T(8,128)(2,1)}, u32[]{:S(2)}, u32[]{:S(2)}) %collective-permute-start.2) | collective-permute-done | bytes 1048608 | tf_op jit(solution)/shard_map/ppermute | solution.py:234
  10.4 13.8 %all-to-all-start = ((bf16[128,8,512]{2,1,0:T(8,128)(2,1)}), bf16[128,8,512]{2,1,0:T(8,128)(2,1)S(1)}, u32[]{:S(2)}, u32[]{:S(2)}) async-start(bf16[128,8,512]{2,1,0:T(8,128)(2,1)} %bitcast.7), calls=%async_computation | async-start | bytes 2097152 | tf_op jit(solution)/shard_map/all_to_all | solution.py:246
  24.8 6.4 %collective-permute-start.1 = (bf16[64,512]{1,0:T(8,128)(2,1)S(1)}, bf16[64,512]{1,0:T(8,128)(2,1)S(1)}, u32[]{:S(2)}, u32[]{:S(2)}) collective-permute-start(bf16[64,512]{1,0:T(8,128)(2,1)S(1)} %get-tuple-element.30), channel_id=1, source_target_pairs={{0,127},{1,0},{2,1},{3,2},{4,3},{5,4},{6,5},{7,6},{8,7},{9,8},{10,... | collective-permute-start | bytes 196616 | tf_op jit(solution)/shard_map/ppermute | solution.py:239
  31.3 22.6 %collective-permute-done.low_ref.refs_4_ = bf16[64,512]{1,0:T(8,128)(2,1)S(1)} collective-permute-done((bf16[64,512]{1,0:T(8,128)(2,1)S(1)}, bf16[64,512]{1,0:T(8,128)(2,1)S(1)}, u32[]{:S(2)}, u32[]{:S(2)}) %collective-permute-start) | collective-permute-done | bytes 65568 | tf_op jit(solution)/shard_map/ppermute | solution.py:239
  55.9 4.4 %shard_map.139 = (bf16[1024,512]{1,0:T(8,128)(2,1)S(1)}, bf16[512,512]{1,0:T(8,128)(2,1)S(1)}, f32[512,512]{1,0:T(8,128)S(1)}) custom-call(s32[1,1024]{1,0:T(1,128)S(1)} %copy-done.23, s32[1,1024]{1,0:T(1,128)S(1)} %copy-done.24, bf16[512,512]{1,0:T(8,128)(2,1)S(1)} %bitcast.32, bf16[64,512]{1,0:T(8,128)(2,1)S(1)} %collective-permute-done.low_ref.refs_4_, ...), custom_call_target="tpu_custom_call" | custom-call | flops 3221225472 | bytes 8003584 | tf_op jit(solution)/shard_map/pallas_call | solution.py:61
  68.5 3.4 %shard_map.140 = (bf16[512,512]{1,0:T(8,128)(2,1)}, bf16[512,512]{1,0:T(8,128)(2,1)S(1)}, bf16[512,512]{1,0:T(8,128)(2,1)S(1)}, bf16[512,512]{1,0:T(8,128)(2,1)S...) custom-call(s32[1,1024]{1,0:T(1,128)S(1)} %bitcast.39, ...), custom_call_target="tpu_custom_call" | custom-call | flops 2684354560 | bytes 11542528 | tf_op jit(solution)/shard_map/pallas_call | solution.py:61
  72.9 5.7 %shard_map.141 = (bf16[16,3,32,256]{3,2,1,0:T(8,128)(2,1)S(1)}, bf16[16,3,32,256]{3,2,1,0:T(8,128)(2,1)S(1)}, bf16[1024,512]{1,0:T(8,128)(2,1)S(1)}, bf16[512,51...) custom-call(s32[1]{0:T(128)} %bitcast.10.refs_0_, ...), custom_call_target="tpu_custom_call" | custom-call | flops 4294967296 | bytes 10756100 | tf_op jit(solution)/shard_map/pallas_call | solution.py:61
  78.7 2.0 %collective-permute-start.6 = (bf16[16,3,32,256]{3,2,1,0:T(8,128)(2,1)S(1)}, bf16[16,3,32,256]{3,2,1,0:T(8,128)(2,1)S(1)}, u32[]{:S(2)}, u32[]{:S(2)}) collective-permute-start(bf16[16,3,32,256]{3,2,1,0:T(8,128)(2,1)S(1)} %get-tuple-element.47), channel_id=1, source_target_pairs={{0,128},{128,0},{1,129},{129,1},{2,130},{130,2},{3,131},{131,3},{4... | collective-permute-start | bytes 2359304 | tf_op jit(solution)/shard_map/ppermute | solution.py:234
  80.7 2.4 %shard_map.144 = (bf16[16,4,32,256]{3,2,1,0:T(8,128)(2,1)S(1)}, bf16[16,4,32,256]{3,2,1,0:T(8,128)(2,1)S(1)}) custom-call(s32[1]{0:T(128)} %bitcast.10.refs_0_, bf16[512,512]{1,0:T(8,128)(2,1)S(1)} %copy-done.29, bf16[512,512]{1,0:T(8,128)(2,1)S(1)} %bitcast.35, bf16[512,512]{1,0:T(8,128)(2,1)S(1)} %get-tuple-element.49.refs_3_, ...), custom_call_target="tpu_custom_call" | custom-call | flops 2147483648 | bytes 5767172 | tf_op jit(solution)/shard_map/pallas_call | solution.py:61
  84.5 4.3 %all-to-all-start.2 = ((bf16[16,3,32,256]{3,2,1,0:T(8,128)(2,1)}), bf16[16,3,32,256]{3,2,1,0:T(8,128)(2,1)}, u32[]{:S(2)}, u32[]{:S(2)}) async-start(bf16[16,3,32,256]{3,2,1,0:T(8,128)(2,1)} %add_convert_fusion.1), calls=%async_computation.2 | async-start | bytes 1572864 | tf_op jit(solution)/shard_map/all_to_all | solution.py:257
  88.8 2.7 %add_convert_fusion = bf16[16,4,32,256]{3,2,1,0:T(8,128)(2,1)} fusion(bf16[16,4,32,256]{3,2,1,0:T(8,128)(2,1)} %collective-permute-done.7, bf16[16,4,32,256]{3,2,1,0:T(8,128)(2,1)S(1)} %get-tuple-element.52), kind=kLoop, calls=%fused_computation | loop fusion | flops 2097152 | bytes 3145728 | tf_op jit(solution)/shard_map/convert_element_type | solution.py:255
  91.5 10.9 %all-to-all-done.2 = bf16[16,3,32,256]{3,2,1,0:T(8,128)(2,1)} async-done(((bf16[16,3,32,256]{3,2,1,0:T(8,128)(2,1)}), bf16[16,3,32,256]{3,2,1,0:T(8,128)(2,1)}, u32[]{:S(2)}, u32[]{:S(2)}) %all-to-all-start.2) | async-done | bytes 786464 | tf_op jit(solution)/shard_map/all_to_all | solution.py:257
  102.4 3.7 %all-to-all-start.4 = ((bf16[16,4,32,256]{3,2,1,0:T(8,128)(2,1)}), bf16[16,4,32,256]{3,2,1,0:T(8,128)(2,1)S(1)}, u32[]{:S(2)}, u32[]{:S(2)}) async-start(bf16[16,4,32,256]{3,2,1,0:T(8,128)(2,1)} %add_convert_fusion), calls=%async_computation.4 | async-start | bytes 2097152 | tf_op jit(solution)/shard_map/all_to_all | solution.py:257
  109.8 11.6 %all-to-all-done.4 = bf16[16,4,32,256]{3,2,1,0:T(8,128)(2,1)S(1)} async-done(((bf16[16,4,32,256]{3,2,1,0:T(8,128)(2,1)}), bf16[16,4,32,256]{3,2,1,0:T(8,128)(2,1)S(1)}, u32[]{:S(2)}, u32[]{:S(2)}) %all-to-all-start.4) | async-done | bytes 1048608 | tf_op jit(solution)/shard_map/all_to_all | solution.py:257
  121.5 7.3 %all-to-all-start.3 = ((bf16[16,3,4,256]{3,2,1,0:T(4,128)(2,1)}), bf16[16,3,4,256]{3,2,1,0:T(4,128)(2,1)S(1)}, u32[]{:S(2)}, u32[]{:S(2)}) async-start(bf16[16,3,4,256]{3,2,1,0:T(4,128)(2,1)} %copy.20), calls=%async_computation.3 | async-start | bytes 196608 | tf_op jit(solution)/shard_map/all_to_all | solution.py:265
  129.8 6.3 %all-to-all-done.3 = bf16[16,3,4,256]{3,2,1,0:T(4,128)(2,1)S(1)} async-done(((bf16[16,3,4,256]{3,2,1,0:T(4,128)(2,1)}), bf16[16,3,4,256]{3,2,1,0:T(4,128)(2,1)S(1)}, u32[]{:S(2)}, u32[]{:S(2)}) %all-to-all-start.3) | async-done | bytes 98336 | tf_op jit(solution)/shard_map/all_to_all | solution.py:265
  136.8 4.4 %all-to-all-start.5 = ((bf16[16,4,4,256]{3,2,1,0:T(4,128)(2,1)}), bf16[16,4,4,256]{3,2,1,0:T(4,128)(2,1)S(1)}, u32[]{:S(2)}, u32[]{:S(2)}) async-start(bf16[16,4,4,256]{3,2,1,0:T(4,128)(2,1)} %copy.23), calls=%async_computation.5 | async-start | bytes 262144 | tf_op jit(solution)/shard_map/all_to_all | solution.py:265
  141.2 7.4 %all-to-all-done.5 = bf16[16,4,4,256]{3,2,1,0:T(4,128)(2,1)S(1)} async-done(((bf16[16,4,4,256]{3,2,1,0:T(4,128)(2,1)}), bf16[16,4,4,256]{3,2,1,0:T(4,128)(2,1)S(1)}, u32[]{:S(2)}, u32[]{:S(2)}) %all-to-all-start.5) | async-done | bytes 131104 | tf_op jit(solution)/shard_map/all_to_all | solution.py:265
  148.6 6.5 %all-to-all-start.1 = ((bf16[128,8,512]{2,1,0:T(8,128)(2,1)}), bf16[128,8,512]{2,1,0:T(8,128)(2,1)S(1)}, u32[]{:S(2)}, u32[]{:S(2)}) async-start(bf16[128,8,512]{2,1,0:T(8,128)(2,1)} %bitcast.11), calls=%async_computation.1 | async-start | bytes 2097152 | tf_op jit(solution)/shard_map/all_to_all | solution.py:246
  155.8 6.3 %collective-permute-start.4 = (bf16[64,512]{1,0:T(8,128)(2,1)S(1)}, bf16[64,512]{1,0:T(8,128)(2,1)S(1)}, u32[]{:S(2)}, u32[]{:S(2)}) collective-permute-start(bf16[64,512]{1,0:T(8,128)(2,1)S(1)} %get-tuple-element.43), channel_id=1, source_target_pairs={{0,127},{1,0},{2,1},{3,2},{4,3},{5,4},{6,5},{7,6},{8,7},{9,8},{10,... | collective-permute-start | bytes 196616 | tf_op jit(solution)/shard_map/ppermute | solution.py:239
  162.1 2.0 %copy-done.3 = bf16[3584,512]{1,0:T(8,128)(2,1)S(1)} copy-done((bf16[3584,512]{1,0:T(8,128)(2,1)S(1)}, bf16[3584,512]{1,0:T(8,128)(2,1)}, u32[]{:S(2)}) %copy-start.3) | copy-done | bytes 3670040
  167.5 2.0 %shard_map.142 = (bf16[1024,512]{1,0:T(8,128)(2,1)}, f32[512,512]{1,0:T(8,128)S(1)}) custom-call(bf16[1024,512]{1,0:T(8,128)(2,1)S(1)} %copy-done.5, bf16[512,512]{1,0:T(8,128)(2,1)S(1)} %copy-done.7, bf16[512,512]{1,0:T(8,128)(2,1)S(1)} %copy-done.9, f32[512,512]{1,0:T(8,128)S(1)} %get-tuple-element.40.part_ref, bf16[3584,512]{1,0:T(8,128)(2,1)S(1)} %copy-done.3), custom_call_target="tpu_custom_call" | custom-call | flops 1073741824 | bytes 8912896 | tf_op jit(solution)/shard_map/pallas_call | solution.py:61
  170.4 14.4 %collective-permute-done.3.low_ref = bf16[64,512]{1,0:T(8,128)(2,1)S(1)} collective-permute-done((bf16[64,512]{1,0:T(8,128)(2,1)S(1)}, bf16[64,512]{1,0:T(8,128)(2,1)S(1)}, u32[]{:S(2)}, u32[]{:S(2)}) %collective-permute-start.3) | collective-permute-done | bytes 65568 | tf_op jit(solution)/shard_map/ppermute | solution.py:239
  (96 shorter events, 29.0 us)
Async XLA Ops:
  3.7 50.2 %copy-start.12 = (bf16[1,1024,512]{2,1,0:T(8,128)(2,1)S(1)}, bf16[1,1024,512]{2,1,0:T(8,128)(2,1)}, u32[]{:S(2)}) copy-start(bf16[1,1024,512]{2,1,0:T(8,128)(2,1)} %param.12) | copy-start | bytes 3145732
  3.7 50.2 %copy-start.16 = (bf16[1,512,512]{2,1,0:T(8,128)(2,1)S(1)}, bf16[1,512,512]{2,1,0:T(8,128)(2,1)}, u32[]{:S(2)}) copy-start(bf16[1,512,512]{2,1,0:T(8,128)(2,1)} %param.11) | copy-start | bytes 1572868
  3.7 50.2 %copy-start.23 = (s32[1,1024]{1,0:T(1,128)S(1)}, s32[1,1024]{1,0:T(1,128)}, u32[]{:S(2)}) copy-start(s32[1,1024]{1,0:T(1,128)} %refs_1_.1) | copy-start | bytes 12292
  3.7 50.2 %copy-start.24 = (s32[1,1024]{1,0:T(1,128)S(1)}, s32[1,1024]{1,0:T(1,128)}, u32[]{:S(2)}) copy-start(s32[1,1024]{1,0:T(1,128)} %refs_2_.1) | copy-start | bytes 12292
  4.6 5.8 %collective-permute-start.2 = (bf16[1024,512]{1,0:T(8,128)(2,1)S(1)}, bf16[1024,512]{1,0:T(8,128)(2,1)}, u32[]{:S(2)}, u32[]{:S(2)}) collective-permute-start(bf16[1024,512]{1,0:T(8,128)(2,1)S(1)} %get-tuple-element.32), channel_id=1, source_target_pairs={{0,128},{128,0},{1,129},{129,1},{2,130},{130,2},{3,131},{131,3},{4... | collective-permute-start | bytes 3145736 | tf_op jit(solution)/shard_map/ppermute | solution.py:234
  10.4 52.7 %all-to-all-start = ((bf16[128,8,512]{2,1,0:T(8,128)(2,1)}), bf16[128,8,512]{2,1,0:T(8,128)(2,1)S(1)}, u32[]{:S(2)}, u32[]{:S(2)}) async-start(bf16[128,8,512]{2,1,0:T(8,128)(2,1)} %bitcast.7), calls=%async_computation | async-start | bytes 2097152 | tf_op jit(solution)/shard_map/all_to_all | solution.py:246
  24.2 29.7 %collective-permute-start = (bf16[64,512]{1,0:T(8,128)(2,1)S(1)}, bf16[64,512]{1,0:T(8,128)(2,1)S(1)}, u32[]{:S(2)}, u32[]{:S(2)}) collective-permute-start(bf16[64,512]{1,0:T(8,128)(2,1)S(1)} %get-tuple-element.29), channel_id=1, source_target_pairs={{0,1},{1,2},{2,3},{3,4},{4,5},{5,6},{6,7},{7,8},{8,9},{9,10},{10,1... | collective-permute-start | bytes 196616 | tf_op jit(solution)/shard_map/ppermute | solution.py:239
  24.8 29.1 %collective-permute-start.1 = (bf16[64,512]{1,0:T(8,128)(2,1)S(1)}, bf16[64,512]{1,0:T(8,128)(2,1)S(1)}, u32[]{:S(2)}, u32[]{:S(2)}) collective-permute-start(bf16[64,512]{1,0:T(8,128)(2,1)S(1)} %get-tuple-element.30), channel_id=1, source_target_pairs={{0,127},{1,0},{2,1},{3,2},{4,3},{5,4},{6,5},{7,6},{8,7},{9,8},{10,... | collective-permute-start | bytes 196616 | tf_op jit(solution)/shard_map/ppermute | solution.py:239
  55.9 7.2 %copy-start.21 = (s32[1,1,1024]{2,1,0:T(1,128)S(1)}, s32[1,1,1024]{2,1,0:T(1,128)}, u32[]{:S(2)}) copy-start(s32[1,1,1024]{2,1,0:T(1,128)} %param.20) | copy-start | bytes 12292
  55.9 7.2 %copy-start.22 = (f32[1,1,1024]{2,1,0:T(1,128)S(1)}, f32[1,1,1024]{2,1,0:T(1,128)}, u32[]{:S(2)}) copy-start(f32[1,1,1024]{2,1,0:T(1,128)} %param.21) | copy-start | bytes 12292
  72.9 7.8 %copy-start.19 = (bf16[1,512,512]{2,1,0:T(8,128)(2,1)S(1)}, bf16[1,512,512]{2,1,0:T(8,128)(2,1)}, u32[]{:S(2)}) copy-start(bf16[1,512,512]{2,1,0:T(8,128)(2,1)} %param.13) | copy-start | bytes 1572868
  72.9 7.8 %copy-start.29 = (bf16[512,512]{1,0:T(8,128)(2,1)S(1)}, bf16[512,512]{1,0:T(8,128)(2,1)}, u32[]{:S(2)}) copy-start(bf16[512,512]{1,0:T(8,128)(2,1)} %copy-done.28) | copy-start | bytes 1572868
  78.7 4.6 %collective-permute-start.6 = (bf16[16,3,32,256]{3,2,1,0:T(8,128)(2,1)S(1)}, bf16[16,3,32,256]{3,2,1,0:T(8,128)(2,1)S(1)}, u32[]{:S(2)}, u32[]{:S(2)}) collective-permute-start(bf16[16,3,32,256]{3,2,1,0:T(8,128)(2,1)S(1)} %get-tuple-element.47), channel_id=1, source_target_pairs={{0,128},{128,0},{1,129},{129,1},{2,130},{130,2},{3,131},{131,3},{4... | collective-permute-start | bytes 2359304 | tf_op jit(solution)/shard_map/ppermute | solution.py:234
  83.1 5.6 %collective-permute-start.7 = (bf16[16,4,32,256]{3,2,1,0:T(8,128)(2,1)S(1)}, bf16[16,4,32,256]{3,2,1,0:T(8,128)(2,1)}, u32[]{:S(2)}, u32[]{:S(2)}) collective-permute-start(bf16[16,4,32,256]{3,2,1,0:T(8,128)(2,1)S(1)} %get-tuple-element.53), channel_id=1, source_target_pairs={{0,128},{128,0},{1,129},{129,1},{2,130},{130,2},{3,131},{131,3},{4... | collective-permute-start | bytes 3145736 | tf_op jit(solution)/shard_map/ppermute | solution.py:234
  84.5 18.0 %all-to-all-start.2 = ((bf16[16,3,32,256]{3,2,1,0:T(8,128)(2,1)}), bf16[16,3,32,256]{3,2,1,0:T(8,128)(2,1)}, u32[]{:S(2)}, u32[]{:S(2)}) async-start(bf16[16,3,32,256]{3,2,1,0:T(8,128)(2,1)} %add_convert_fusion.1), calls=%async_computation.2 | async-start | bytes 1572864 | tf_op jit(solution)/shard_map/all_to_all | solution.py:257
  88.8 17.4 %copy-start.14 = (bf16[1024,512]{1,0:T(8,128)(2,1)S(1)}, bf16[1024,512]{1,0:T(8,128)(2,1)}, u32[]{:S(2)}) copy-start(bf16[1024,512]{1,0:T(8,128)(2,1)} %copy-done.13) | copy-start | bytes 3145732
  102.4 19.0 %all-to-all-start.4 = ((bf16[16,4,32,256]{3,2,1,0:T(8,128)(2,1)}), bf16[16,4,32,256]{3,2,1,0:T(8,128)(2,1)S(1)}, u32[]{:S(2)}, u32[]{:S(2)}) async-start(bf16[16,4,32,256]{3,2,1,0:T(8,128)(2,1)} %add_convert_fusion), calls=%async_computation.4 | async-start | bytes 2097152 | tf_op jit(solution)/shard_map/all_to_all | solution.py:257
  106.1 35.1 %collective-permute-start.5 = (bf16[1024,512]{1,0:T(8,128)(2,1)S(1)}, bf16[1024,512]{1,0:T(8,128)(2,1)}, u32[]{:S(2)}, u32[]{:S(2)}) collective-permute-start(bf16[1024,512]{1,0:T(8,128)(2,1)S(1)} %copy-done.14), channel_id=1, source_target_pairs={{0,128},{128,0},{1,129},{129,1},{2,130},{130,2},{3,131},{131,3},{4... | collective-permute-start | bytes 3145736 | tf_op jit(solution)/shard_map/ppermute | solution.py:234
  121.5 14.7 %all-to-all-start.3 = ((bf16[16,3,4,256]{3,2,1,0:T(4,128)(2,1)}), bf16[16,3,4,256]{3,2,1,0:T(4,128)(2,1)S(1)}, u32[]{:S(2)}, u32[]{:S(2)}) async-start(bf16[16,3,4,256]{3,2,1,0:T(4,128)(2,1)} %copy.20), calls=%async_computation.3 | async-start | bytes 196608 | tf_op jit(solution)/shard_map/all_to_all | solution.py:265
  136.8 11.8 %all-to-all-start.5 = ((bf16[16,4,4,256]{3,2,1,0:T(4,128)(2,1)}), bf16[16,4,4,256]{3,2,1,0:T(4,128)(2,1)S(1)}, u32[]{:S(2)}, u32[]{:S(2)}) async-start(bf16[16,4,4,256]{3,2,1,0:T(4,128)(2,1)} %copy.23), calls=%async_computation.5 | async-start | bytes 262144 | tf_op jit(solution)/shard_map/all_to_all | solution.py:265
  148.6 36.2 %all-to-all-start.1 = ((bf16[128,8,512]{2,1,0:T(8,128)(2,1)}), bf16[128,8,512]{2,1,0:T(8,128)(2,1)S(1)}, u32[]{:S(2)}, u32[]{:S(2)}) async-start(bf16[128,8,512]{2,1,0:T(8,128)(2,1)} %bitcast.11), calls=%async_computation.1 | async-start | bytes 2097152 | tf_op jit(solution)/shard_map/all_to_all | solution.py:246
  155.1 29.7 %collective-permute-start.3 = (bf16[64,512]{1,0:T(8,128)(2,1)S(1)}, bf16[64,512]{1,0:T(8,128)(2,1)S(1)}, u32[]{:S(2)}, u32[]{:S(2)}) collective-permute-start(bf16[64,512]{1,0:T(8,128)(2,1)S(1)} %get-tuple-element.42), channel_id=1, source_target_pairs={{0,1},{1,2},{2,3},{3,4},{4,5},{5,6},{6,7},{7,8},{8,9},{9,10},{10,1... | collective-permute-start | bytes 196616 | tf_op jit(solution)/shard_map/ppermute | solution.py:239
  155.8 29.0 %collective-permute-start.4 = (bf16[64,512]{1,0:T(8,128)(2,1)S(1)}, bf16[64,512]{1,0:T(8,128)(2,1)S(1)}, u32[]{:S(2)}, u32[]{:S(2)}) collective-permute-start(bf16[64,512]{1,0:T(8,128)(2,1)S(1)} %get-tuple-element.43), channel_id=1, source_target_pairs={{0,127},{1,0},{2,1},{3,2},{4,3},{5,4},{6,5},{7,6},{8,7},{9,8},{10,... | collective-permute-start | bytes 196616 | tf_op jit(solution)/shard_map/ppermute | solution.py:239
  167.5 17.3 %copy-start.11 = (s32[1,128]{1,0:T(1,128)S(1)}, s32[1,128]{1,0:T(1,128)}, u32[]{:S(2)}) copy-start(s32[1,128]{1,0:T(1,128)} %halo_ref.3) | copy-start | bytes 1540
  (24 other events, 44.6 us)

commit v3 on v2

v3 whole, which is shorter than its diff:
```python
import math

import jax
import jax.numpy as jnp
from jax import lax
from jax.experimental import pallas as pl
from jax.experimental.pallas import tpu as pltpu
from jax.sharding import PartitionSpec as P

SLOT = 8
RING = 4
PLANE = RING * RING
TILE = 256
BF = jnp.bfloat16
F32 = jnp.float32
I32 = jnp.int32
VMEM = pl.BlockSpec(memory_space=pltpu.VMEM)
SMEM = pl.BlockSpec(memory_space=pltpu.SMEM)


def dot(a, b):
    return jnp.dot(a, b, preferred_element_type=F32)


def dot_nt(a, b):
    return lax.dot_general(a, b, (((1,), (1,)), ((), ())), preferred_element_type=F32)


def column(row):
    return jnp.transpose(jnp.broadcast_to(row.astype(F32), (128, row.shape[1])))


def pick(col, count, value=None):
    base = lax.broadcasted_iota(I32, (col.shape[0], 128), 1).astype(F32)
    one = jnp.ones_like(base) if value is None else value
    parts = [jnp.where(col == base + float(k), one, 0.0).astype(BF) for k in range(0, count, 128)]
    return parts[0] if len(parts) == 1 else jnp.concatenate(parts, axis=1)


def pick_t(row, start, size, value=None):
    base = lax.broadcasted_iota(I32, (size, row.shape[1]), 0) + start
    one = jnp.ones(base.shape, F32) if value is None else jnp.broadcast_to(value, base.shape)
    return jnp.where(base == row, one, 0.0).astype(BF)


def row_order(place, width, patches):
    fine = width // patches
    depth = patches // PLANE
    row = lax.broadcasted_iota(I32, (width, width), 0)
    col = lax.broadcasted_iota(I32, (width, width), 1)
    dx, dy = row // (width // RING), (row // (width // PLANE)) % RING
    dz, offset = (row // fine) % depth, row % fine
    x, y = place % RING, (place // RING) % RING
    patch = dz * PLANE + (y + dy) % RING * RING + (x + dx) % RING
    return jnp.where(col == patch * fine + offset, 1.0, 0.0).astype(BF)


def tiles(count):
    return [slice(i, i + TILE) for i in range(0, count, TILE)]


class Far:
    def __init__(self, array, start=0, size=None):
        self.array = array
        self.start = start
        self.size = array.shape[0] if size is None else size


class Fetched:
    def __init__(self, copy, buffer):
        self.copy, self.buffer, self.waited = copy, buffer, False
        self.shape = buffer.shape

    def __getitem__(self, index):
        if not self.waited:
            self.copy.wait()
            self.waited = True
        return self.buffer[index]


def call(kernel, args, outs, scratch=(), flops=0):
    far = [i for i, a in enumerate(args) if isinstance(a, Far)]
    arrays = [a.array if isinstance(a, Far) else a for a in args]
    buffers = [
        pltpu.VMEM((args[i].size,) + args[i].array.shape[1:], args[i].array.dtype) for i in far
    ]
    specs = [
        pl.BlockSpec(memory_space=pl.ANY)
        if isinstance(a, Far)
        else (SMEM if a.dtype == I32 and a.ndim == 1 else VMEM)
        for a in args
    ]
    ins, made = len(args), len(args) + len(outs)

    def body(*refs):
        held = refs[made : made + len(far)]
        refs_in = list(refs[:ins])
        if far:
            sems = refs[made + len(far)]
        for k, i in enumerate(far):
            source = refs_in[i].at[args[i].start : args[i].start + args[i].size]
            copy = pltpu.make_async_copy(source, held[k], sems.at[k])
            copy.start()
            refs_in[i] = Fetched(copy, held[k])
        kernel(*refs_in, *refs[ins:made], *refs[made + len(far) + (1 if far else 0) :])
        for i in far:
            if not refs_in[i].waited:
                refs_in[i].copy.wait()

    size = sum(math.prod(a.shape) * a.dtype.itemsize for a in arrays + list(outs))
    extra = buffers + ([pltpu.SemaphoreType.DMA((len(far),))] if far else [])
    return pl.pallas_call(
        body,
        out_shape=tuple(outs),
        in_specs=specs,
        out_specs=tuple([VMEM] * len(outs)),
        scratch_shapes=extra + list(scratch),
        compiler_params=pltpu.CompilerParams(vmem_limit_bytes=16 * 2**20),
        cost_estimate=pl.CostEstimate(flops=flops, bytes_accessed=size, transcendentals=0),
    )(*arrays)


def shape(dtype, *dims):
    return jax.ShapeDtypeStruct(dims, dtype)


def send_kernel(rows_ref, count_ref, halo_ref, nodes_ref, out_ref, low_ref, high_ref, live_ref):
    slots = rows_ref.shape[1]
    patches = count_ref.shape[1]
    width = nodes_ref.shape[0]
    owner = lax.broadcasted_iota(I32, (patches, slots), 0)
    place = lax.broadcasted_iota(I32, (patches, slots), 1)
    repeat = jnp.where(place // SLOT == owner, 1.0, 0.0).astype(BF)
    counts = jnp.broadcast_to(count_ref[...].astype(F32), (8, patches)).astype(BF)
    spread = dot(counts, repeat)[:1].astype(I32)
    slot = lax.broadcasted_iota(I32, (1, slots), 1) % SLOT
    live = jnp.where(slot < spread, rows_ref[...], -1)
    live_ref[...] = live
    nodes = nodes_ref[...]
    depth = low_ref.shape[0]
    halo = dot(pick(column(halo_ref[...]), width), nodes).astype(BF)
    low_ref[...] = halo[:depth]
    high_ref[...] = halo[depth:]
    col = column(live)
    for r in tiles(slots):
        out_ref[r] = dot(pick(col[r], width), nodes).astype(BF)


def edge_kernel(
    dst_ref, nodes_ref, wb_ref, src_ref, low_ref, high_ref, wa_ref, edges_ref, wc_ref, second_ref,
    slope_ref, agg_ref, msg_ref, hid_ref,
):
    count, width = nodes_ref.shape
    inner = edges_ref.shape[0] - edges_ref.shape[0] // 4
    dst = column(dst_ref[...])
    nodes = nodes_ref[...]
    src = column(src_ref[...])
    halo = jnp.concatenate([low_ref[...], high_ref[...]], axis=0)
    for r in tiles(edges_ref.shape[0]):
        if r.stop <= inner:
            feat = dot(pick(src[r], count), nodes).astype(BF)
        else:
            feat = dot(pick(src[r] - float(count), halo.shape[0]), halo).astype(BF)
        own = dot(pick(dst[r], count), nodes).astype(BF)
        pre = dot(own, wb_ref[...]) + dot(feat, wa_ref[...]) + dot(edges_ref[r], wc_ref[...])
        sigma = jax.nn.sigmoid(pre)
        hid_ref[r] = (pre * sigma).astype(BF)
        slope_ref[r] = (sigma * (1.0 + pre * (1.0 - sigma))).astype(BF)
    for r in tiles(count):
        agg = dot(pick_t(dst_ref[...], r.start, TILE), hid_ref[...]).astype(BF)
        agg_ref[r] = agg
        msg_ref[r] = dot(agg, second_ref[...])


def node_kernel(
    target_ref, margin_ref, nodes_ref, a_ref, b_ref, cot_ref, second_ref, msg_ref, recv_ref,
    new_ref, pooled_ref, hid_ref, gpre_ref, gpool_ref, part_ref, ret_ref,
):
    count, width = nodes_ref.shape
    target, margin = target_ref[...], margin_ref[...]
    for r in tiles(count):
        coupled = dot(pick_t(target, r.start, TILE, margin), recv_ref[...])
        pooled = (msg_ref[r] + coupled).astype(BF)
        pooled_ref[r] = pooled
        nodes = nodes_ref[r]
        pre = dot(nodes, a_ref[...]) + dot(pooled, b_ref[...])
        sigma = jax.nn.sigmoid(pre)
        hidden = (pre * sigma).astype(BF)
        hid_ref[r] = hidden
        slope = sigma * (1.0 + pre * (1.0 - sigma))
        cot = cot_ref[r]
        gpre = (dot_nt(cot, second_ref[...]) * slope).astype(BF)
        gpre_ref[r] = gpre
        gpool_ref[r] = dot_nt(gpre, b_ref[...]).astype(BF)
        new_ref[r] = (nodes.astype(F32) + dot(hidden, second_ref[...])).astype(BF)
        part_ref[r] = cot.astype(F32) + dot_nt(gpre, a_ref[...])
    col, weight = column(target), column(margin)
    gpool = gpool_ref[...]
    for r in tiles(recv_ref.shape[0]):
        ret_ref[r] = dot(pick(col[r], count, weight[r]), gpool).astype(BF)


def put(own_ref, send_ref, index, value, first):
    half = value.shape[1] // 2
    lane = half // 2
    step = value.shape[0] // RING
    fine = step // RING
    own = jnp.where(first, value[:, :half], value[:, half:]).astype(BF)
    send = jnp.where(first, value[:, half:], value[:, :half]).astype(BF)
    for ref, part in ((own_ref, own), (send_ref, send)):
        for i in range(RING):
            ref[0, i, index] = part[i * step : (i + 1) * step, :lane]
            for j in range(RING):
                start = i * step + j * fine
                ref[1, j, index, i * fine : (i + 1) * fine] = part[start : start + fine, lane:]


def node_grad_kernel(
    side_ref, agg_ref, nodes_ref, pooled_ref, hid_ref, gpre_ref, gpool_ref, cot_ref, own_ref, send_ref,
    *, patches, scale
):
    order = row_order(side_ref[1], nodes_ref.shape[1], patches)
    first = side_ref[0] == 0
    pairs = [(agg_ref, gpool_ref), (nodes_ref, gpre_ref), (pooled_ref, gpre_ref), (hid_ref, cot_ref)]
    for index, (left, right) in enumerate(pairs):
        turned = dot_nt(order, left[...]).astype(BF)
        put(own_ref, send_ref, index, dot(turned, right[...]) * scale, first)


def edge_grad_kernel(
    side_ref, dst_ref, second_ref, edges_ref, src_ref, nodes_ref, wa_ref, low_ref, high_ref, slope_ref, gpool_ref,
    own_ref, send_ref, gpre_ref, bysrc_ref, bydst_ref, glow_ref, ghigh_ref,
    *, patches, scale
):
    count, width = nodes_ref.shape
    inner = edges_ref.shape[0] - edges_ref.shape[0] // 4
    depth = low_ref.shape[0]
    first = side_ref[0] == 0
    gpool = gpool_ref[...]
    second = second_ref[...]
    dst_row, src_row = dst_ref[...], src_ref[...]
    dst = column(dst_row)
    for r in tiles(edges_ref.shape[0]):
        message = dot(pick(dst[r], count), gpool).astype(BF)
        gpre_ref[r] = (dot_nt(message, second) * slope_ref[r].astype(F32)).astype(BF)
    order = row_order(side_ref[1], width, patches)
    turned = dot_nt(order, edges_ref[...]).astype(BF)
    put(own_ref, send_ref, 2, dot(turned, gpre_ref[...]) * scale, first)
    for r in tiles(count):
        bydst_ref[r] = dot(pick_t(dst_row, r.start, TILE), gpre_ref[...]).astype(BF)
        bysrc_ref[r] = dot(pick_t(src_row[:, :inner], r.start, TILE), gpre_ref[:inner]).astype(BF)
    halo = dot(pick_t(src_row[:, inner:], count, 2 * depth), gpre_ref[inner:]).astype(BF)
    turned = dot_nt(order, nodes_ref[...]).astype(BF)
    put(own_ref, send_ref, 1, dot(turned, bydst_ref[...]) * scale, first)
    rim = dot_nt(order, jnp.concatenate([low_ref[...], high_ref[...]], axis=0)).astype(BF)
    put(own_ref, send_ref, 0, (dot(turned, bysrc_ref[...]) + dot(rim, halo)) * scale, first)
    back = dot_nt(halo, wa_ref[...]).astype(BF)
    glow_ref[...] = back[:depth]
    ghigh_ref[...] = back[depth:]


def edge_rest_kernel(
    wc_ref, wa_ref, wb_ref, gpre_ref, bysrc_ref, bydst_ref, part_ref, edge_ref, total_ref
):
    count, width = bysrc_ref.shape
    for r in tiles(gpre_ref.shape[0]):
        edge_ref[r] = dot_nt(gpre_ref[r], wc_ref[...]).astype(BF)
    for r in tiles(count):
        total_ref[r] = (
            part_ref[r]
            + dot_nt(bysrc_ref[r], wa_ref[...])
            + dot_nt(bydst_ref[r], wb_ref[...])
        )


def last_kernel(live_ref, halo_ref, total_ref, low_ref, high_ref, back_ref, out_ref):
    halo_back = jnp.concatenate([low_ref[...], high_ref[...]], axis=0)
    for r in tiles(total_ref.shape[0]):
        out_ref[r] = (
            total_ref[r]
            + dot(pick_t(halo_ref[...], r.start, TILE), halo_back)
            + dot(pick_t(live_ref[...], r.start, TILE), back_ref[...])
        ).astype(BF)


def from_partner(value):
    return lax.ppermute(value, "mesh", [(0, 1), (1, 0)])


def shift(value, step):
    count = lax.axis_size("patch")
    return lax.ppermute(value, "patch", [(i, (i + step) % count) for i in range(count)])


def route(crossed):
    rows, width = crossed.shape
    patches = lax.axis_size("patch")
    crossed = crossed.reshape(patches, rows // patches, width)
    routed = lax.all_to_all(crossed, "patch", split_axis=0, concat_axis=0, tiled=True)
    return routed.reshape(rows, width)


def hop(value, dy=0, dx=0):
    pairs = []
    for p in range(lax.axis_size("patch")):
        z, y, x = p // PLANE, p // RING % RING, p % RING
        pairs.append((p, z * PLANE + (y + dy) % RING * RING + (x + dx) % RING))
    return lax.ppermute(value, "patch", pairs)


def join_kernel(own_a, other_a, own_b, other_b, *outs):
    for index, out in enumerate(outs):
        c, d = index // RING, index % RING
        base = 0
        for own, other in ((own_a, other_a), (own_b, other_b)):
            blocks = own.shape[2]
            joined = own[c, d].astype(F32) + other[c, d].astype(F32)
            out[base : base + blocks] = joined.astype(BF)
            base += blocks


def total_of(refs):
    total = refs[0][...].astype(F32)
    for ref in refs[1:]:
        total = total + ref[...].astype(F32)
    return total


def plane_kernel(*refs):
    for c in range(2):
        total = total_of(refs[c * RING : (c + 1) * RING])
        fine = total.shape[1] // RING
        for d in range(RING):
            refs[(2 + c) * RING + d][...] = total[:, d * fine : (d + 1) * fine].astype(BF)


def depth_kernel(*refs):
    ins, (out, hold) = refs[: 2 * RING], refs[2 * RING :]
    depth = hold.shape[0]
    hold[...] = jnp.zeros(hold.shape, F32)
    for c in range(2):
        total = total_of(ins[c * RING : (c + 1) * RING])
        blocks, rows, lane = total.shape
        fine = rows // depth
        for block in range(blocks):
            for d in range(depth):
                hold[d, block * fine : (block + 1) * fine, c * lane : (c + 1) * lane] = total[
                    block, d * fine : (d + 1) * fine
                ]
    value = hold[...].astype(BF)
    out[:depth] = value
    out[depth:] = value


def finish_kernel(in_ref, out_ref):
    count, _, lane = in_ref.shape
    depth = count // 2
    for side in range(2):
        total = in_ref[side * depth].astype(F32)
        for d in range(1, depth):
            total = total + in_ref[side * depth + d].astype(F32)
        out_ref[:, side * lane : (side + 1) * lane] = total[: out_ref.shape[0]]


def weight_sums(own_a, other_a, own_b, other_b):
    patches = lax.axis_size("patch")
    depth = patches // PLANE
    rows, lane = own_a.shape[3:]
    blocks = own_a.shape[2] + own_b.shape[2]
    fine = rows // RING // depth
    piece = shape(BF, blocks, rows, lane)
    small = shape(BF, blocks, rows // RING, lane)
    pieces = call(join_kernel, (own_a, other_a, own_b, other_b), (piece,) * (2 * RING))
    for kernel, axes in ((plane_kernel, ("dx", "dy")), (None, ("dy", "dx"))):
        pieces = [
            pieces[c * RING + d] if d == 0 else hop(pieces[c * RING + d], **{axis: d})
            for c, axis in enumerate(axes)
            for d in range(RING)
        ]
        if kernel is not None:
            pieces = call(kernel, pieces, (small,) * (2 * RING))
    padded = (blocks * fine + 15) // 16 * 16
    (part,) = call(
        depth_kernel,
        pieces,
        (shape(BF, 2 * depth, padded, 2 * lane),),
        scratch=(pltpu.VMEM((depth, padded, 2 * lane), F32),),
    )
    columns = [
        [m * patches + z * PLANE + i for m in range(2) for z in range(depth)] for i in range(PLANE)
    ]
    both = lax.all_to_all(
        part, ("mesh", "patch"), split_axis=0, concat_axis=0, axis_index_groups=columns, tiled=True
    )
    (total,) = call(finish_kernel, (both,), (shape(F32, blocks * fine, 4 * lane),))
    return total.reshape(blocks, fine * 4 * lane)


def shards(
    nodes,
    edges,
    cot_nodes,
    weights,
    edge_src,
    edge_dst,
    halo_rows,
    couple_rows,
    couple_count,
    couple_target,
    couple_weight,
):
    nodes_own = nodes[0]
    edges_own = edges[0]
    cotangent = cot_nodes[0]
    count, width = nodes_own.shape
    edge_count = edges_own.shape[0]
    depth = halo_rows.shape[1] // 2
    patches = lax.axis_size("patch")
    slots = couple_rows.shape[2]
    scale = 1.0 / math.sqrt(2 * patches * edge_count)
    side = jnp.stack([lax.axis_index("mesh"), lax.axis_index("patch")]).astype(I32)
    target, margin = couple_target[0], couple_weight[0]
    unit = 2 * width * width

    def weight(block):
        return Far(weights, block * width, width)

    outgoing, low_out, high_out, live = call(
        send_kernel,
        (Far(couple_rows[0]), Far(couple_count[0]), Far(halo_rows), Far(nodes_own)),
        (shape(BF, slots, width), shape(BF, depth, width), shape(BF, depth, width), shape(I32, 1, slots)),
        flops=(slots + 2 * depth) * unit,
    )
    crossed = from_partner(outgoing)
    low, high = shift(high_out, 1), shift(low_out, -1)
    crossed, low, high = lax.optimization_barrier((crossed, low, high))
    received = route(crossed)
    slope, agg, message = call(
        edge_kernel,
        (
            Far(edge_dst), Far(nodes_own), weight(1), Far(edge_src), low, high, weight(0),
            Far(edges_own), weight(2), weight(3),
        ),
        (shape(BF, edge_count, width), shape(BF, count, width), shape(F32, count, width)),
        scratch=(pltpu.VMEM((edge_count, width), BF),),
        flops=edge_count * 6 * unit,
    )
    square = shape(BF, count, width)
    new_nodes, pooled, hidden, grad_pre, grad_pooled, part, returned = call(
        node_kernel,
        (
            Far(target), Far(margin), Far(nodes_own), weight(4), weight(5), Far(cotangent), weight(6),
            message, received,
        ),
        (square, square, square, square, square, shape(F32, count, width), shape(BF, slots, width)),
        flops=count * 10 * unit,
    )
    crossed_back = from_partner(returned)
    couple_back = route(crossed_back)
    grad_shape = lambda blocks: shape(BF, 2, RING, blocks, width // RING, width // 4)
    own_b, send_b = call(
        lambda *refs: node_grad_kernel(*refs, patches=patches, scale=scale),
        (side, agg, Far(nodes_own), pooled, hidden, grad_pre, grad_pooled, Far(cotangent)),
        (grad_shape(4), grad_shape(4)),
        flops=count * 8 * unit,
    )
    other_b = from_partner(send_b)
    grad_pooled, other_b = lax.optimization_barrier((grad_pooled, other_b))
    own_a, send_a, grad_edge_pre, by_source, by_target, grad_low, grad_high = call(
        lambda *refs: edge_grad_kernel(*refs, patches=patches, scale=scale),
        (
            side, Far(edge_dst), weight(3), Far(edges_own), Far(edge_src), Far(nodes_own), weight(0),
            low, high, slope, grad_pooled,
        ),
        (
            grad_shape(3), grad_shape(3), shape(BF, edge_count, width), square, square,
            shape(BF, depth, width), shape(BF, depth, width),
        ),
        flops=edge_count * 8 * unit,
    )
    summed = weight_sums(own_a, from_partner(send_a), own_b, other_b)
    back_low, back_high = shift(grad_high, 1), shift(grad_low, -1)
    edge_grads, total = call(
        edge_rest_kernel,
        (weight(2), weight(0), weight(1), grad_edge_pre, by_source, by_target, part),
        (shape(BF, edge_count, width), shape(F32, count, width)),
        flops=edge_count * 2 * unit,
    )
    (node_grads,) = call(
        last_kernel,
        (live, Far(halo_rows), total, back_low, back_high, couple_back),
        (square,),
        flops=count * 2 * unit,
    )
    return (new_nodes[None], node_grads[None], edge_grads[None], summed)


def solution(mesh):
    return jax.shard_map(
        shards,
        mesh=mesh,
        in_specs=(
            P("mesh", "patch", None),
            P("mesh", "patch", None),
            P("mesh", "patch", None),
            P(),
            P("mesh", "patch"),
            P("mesh", "patch"),
            P("mesh", "patch"),
            P("mesh", "patch", None),
            P("mesh", "patch", None),
            P("mesh", "patch", None),
            P("mesh", "patch", None),
        ),
        out_specs=(
            P("mesh", "patch", None),
            P("mesh", "patch", None),
            P("mesh", "patch", None),
            P(None, "patch"),
        ),
        check_vma=False,
    )
```

time: 188 us -> 183 us (0.973)
  Pallas kernels: 20.5 us -> 28.7 us
  waiting for transfers between devices: 75.7 us -> 68 us
  other arithmetic: 6.25 us -> 0.08 us
    all_to_all x4 -> x1, waiting for transfers between devices: 36.3 us -> 9.37 us  [weight_sums(): lax.all_to_all(part, ('mesh', 'patch'), split_axis=0, concat_axis=0, axis...]
    ppermute x4, waiting for transfers between devices: 37 us -> 16.7 us  [shift(): lax.ppermute(value, 'patch', [(i, (i + step) % count) for i in range(coun...]
    ppermute x0 -> x12, waiting for transfers between devices: none -> 20.2 us  [hop(): return lax.ppermute(value, 'patch', pairs)]
    all_to_all x2, waiting for transfers between devices: 0.01 us -> 17.5 us  [route(): lax.all_to_all(crossed, 'patch', split_axis=0, concat_axis=0, tiled=True)]
    all_to_all x4 -> x1, starting transfers between devices: 19.7 us -> 7.55 us  [weight_sums(): lax.all_to_all(part, ('mesh', 'patch'), split_axis=0, concat_axis=0, axis...]
    ppermute x0 -> x12, starting transfers between devices: none -> 9.31 us  [hop(): return lax.ppermute(value, 'patch', pairs)]
    pallas_call x7 -> x11, Pallas kernels: 20.5 us -> 28.7 us  [call(): pl.pallas_call(body, out_shape=tuple(outs), in_specs=specs, out_specs=tup...]
    convert_element_type x2 -> x0, other arithmetic: 3.94 us -> none  [reduce_blocks(): paired = (own.astype(F32) + from_partner(send).astype(F32)).astype(BF)]
  transfers between devices with their start and end apart: 14 -> 23, of which waited for: 7 -> 14; matrix products, arithmetic and copies ran while one was open for 4% -> 0% of each run, Pallas kernels for 5% -> 5%
where the time goes in v3:
time: 183 us; the launch traced here: 182 us
  waiting for transfers between devices  68 us (37%)
  starting transfers between devices  62.7 us (34%)
  Pallas kernels  28.7 us (16%)
  local copies, waits for them, and re-layouts  21.6 us (12%)
    pallas_call x11, Pallas kernels, call(): pl.pallas_call(body, out_shape=tuple(outs), in_specs=specs, out_specs=tup...  28.7 us
    all_to_all x2, starting transfers between devices, route(): lax.all_to_all(crossed, 'patch', split_axis=0, concat_axis=0, tiled=True)  21.2 us
    unnamed x70, local copies, waits for them, and re-layouts  20.9 us
    ppermute x12, waiting for transfers between devices, hop(): return lax.ppermute(value, 'patch', pairs)  20.2 us
    all_to_all x2, waiting for transfers between devices, route(): lax.all_to_all(crossed, 'patch', split_axis=0, concat_axis=0, tiled=True)  17.5 us
    ppermute x4, waiting for transfers between devices, shift(): lax.ppermute(value, 'patch', [(i, (i + step) % count) for i in range(coun...  16.7 us
    ppermute x4, starting transfers between devices, shift(): lax.ppermute(value, 'patch', [(i, (i + step) % count) for i in range(coun...  15.5 us
    all_to_all x1, waiting for transfers between devices, weight_sums(): lax.all_to_all(part, ('mesh', 'patch'), split_axis=0, concat_axis=0, axis...  9.37 us
  transfers between devices with their start and end apart: 23, of which 14 were waited for; matrix products, arithmetic and copies ran while one was open for 0% of the time, Pallas kernels for 5%

profile of v3, /device:TPU:1, one launch (start us, length us, event | category | flops | bytes accessed | tf_op | source)
XLA Modules:
  0.0 182.2 jit_solution(8481402841695249185)
XLA Ops:
  4.8 3.3 %collective-permute-start = (bf16[1024,512]{1,0:T(8,128)(2,1)S(1)}, bf16[1024,512]{1,0:T(8,128)(2,1)S(1)}, u32[]{:S(2)}, u32[]{:S(2)}) collective-permute-start(bf16[1024,512]{1,0:T(8,128)(2,1)S(1)} %get-tuple-element.50), channel_id=1, source_target_pairs={{0,128},{128,0},{1,129},{129,1},{2,130},{130,2},{3,131},{131,3},{4... | collective-permute-start | bytes 3145736 | tf_op jit(solution)/shard_map/ppermute | solution.py:287
  8.2 8.5 %collective-permute-start.2 = (bf16[64,512]{1,0:T(8,128)(2,1)S(1)}, bf16[64,512]{1,0:T(8,128)(2,1)S(1)}, u32[]{:S(2)}, u32[]{:S(2)}) collective-permute-start(bf16[64,512]{1,0:T(8,128)(2,1)S(1)} %get-tuple-element.52), channel_id=1, source_target_pairs={{0,127},{1,0},{2,1},{3,2},{4,3},{5,4},{6,5},{7,6},{8,7},{9,8},{10,... | collective-permute-start | bytes 196616 | tf_op jit(solution)/shard_map/ppermute | solution.py:292
  16.7 2.4 %collective-permute-done.1.refs_4_.refs_7_ = bf16[64,512]{1,0:T(8,128)(2,1)S(1)} collective-permute-done((bf16[64,512]{1,0:T(8,128)(2,1)S(1)}, bf16[64,512]{1,0:T(8,128)(2,1)S(1)}, u32[]{:S(2)}, u32[]{:S(2)}) %collective-permute-start.1) | collective-permute-done | bytes 65568 | tf_op jit(solution)/shard_map/ppermute | solution.py:292
  20.1 11.1 %all-to-all-start = ((bf16[128,8,512]{2,1,0:T(8,128)(2,1)}), bf16[128,8,512]{2,1,0:T(8,128)(2,1)S(1)}, u32[]{:S(2)}, u32[]{:S(2)}) async-start(bf16[128,8,512]{2,1,0:T(8,128)(2,1)} %bitcast.32), calls=%async_computation | async-start | bytes 2097152 | tf_op jit(solution)/shard_map/all_to_all | solution.py:299
  33.3 5.0 %shard_map.139 = (bf16[1024,512]{1,0:T(8,128)(2,1)S(1)}, bf16[512,512]{1,0:T(8,128)(2,1)S(1)}, f32[512,512]{1,0:T(8,128)S(1)}) custom-call(s32[1,1024]{1,0:T(1,128)S(1)} %copy-done.22, bf16[512,512]{1,0:T(8,128)(2,1)S(1)} %bitcast.19, bf16[3584,512]{1,0:T(8,128)(2,1)S(1)} %copy-done, s32[1,1024]{1,0:T(1,128)S(1)} %copy-done.23, ...), custom_call_target="tpu_custom_call" | custom-call | flops 3221225472 | bytes 19013632 | tf_op jit(solution)/shard_map/pallas_call | solution.py:112
  41.0 17.5 %all-to-all-done = bf16[128,8,512]{2,1,0:T(8,128)(2,1)S(1)} async-done(((bf16[128,8,512]{2,1,0:T(8,128)(2,1)}), bf16[128,8,512]{2,1,0:T(8,128)(2,1)S(1)}, u32[]{:S(2)}, u32[]{:S(2)}) %all-to-all-start) | async-done | bytes 1048608 | tf_op jit(solution)/shard_map/all_to_all | solution.py:299
  61.9 5.0 %shard_map.140 = (bf16[512,512]{1,0:T(8,128)(2,1)}, bf16[512,512]{1,0:T(8,128)(2,1)S(1)}, bf16[512,512]{1,0:T(8,128)(2,1)S(1)}, bf16[512,512]{1,0:T(8,128)(2,1)S...) custom-call(s32[1,1024]{1,0:T(1,128)S(1)} %bitcast.27, ...), custom_call_target="tpu_custom_call" | custom-call | flops 2684354560 | bytes 18882560 | tf_op jit(solution)/shard_map/pallas_call | solution.py:112
  66.9 3.6 %shard_map.141 = (bf16[2,4,4,128,128]{4,3,2,1,0:T(8,128)(2,1)S(1)}, bf16[2,4,4,128,128]{4,3,2,1,0:T(8,128)(2,1)S(1)}) custom-call(s32[2]{0:T(128)S(1)} %pad_add_fusion.refs_0_, bf16[512,512]{1,0:T(8,128)(2,1)S(1)} %copy-done.29, bf16[512,512]{1,0:T(8,128)(2,1)S(1)} %bitcast.21, bf16[512,512]{1,0:T(8,128)(2,1)S(1)} %get-tuple-element.62.refs_3_, ...), custom_call_target="tpu_custom_call" | custom-call | flops 2147483648 | bytes 5767176 | tf_op jit(solution)/shard_map/pallas_call | solution.py:112
  70.5 4.9 %collective-permute-start.3 = (bf16[2,4,4,128,128]{4,3,2,1,0:T(8,128)(2,1)S(1)}, bf16[2,4,4,128,128]{4,3,2,1,0:T(8,128)(2,1)S(1)}, u32[]{:S(2)}, u32[]{:S(2)}) collective-permute-start(bf16[2,4,4,128,128]{4,3,2,1,0:T(8,128)(2,1)S(1)} %get-tuple-element.65), channel_id=1, source_target_pairs={{0,128},{128,0},{1,129},{129,1},{2,130},{130,2},{3,131},{131,3},{4... | collective-permute-start | bytes 3145736 | tf_op jit(solution)/shard_map/ppermute | solution.py:287
  75.4 2.3 %collective-permute-done.3.refs_3_ = bf16[2,4,4,128,128]{4,3,2,1,0:T(8,128)(2,1)S(1)} collective-permute-done((bf16[2,4,4,128,128]{4,3,2,1,0:T(8,128)(2,1)S(1)}, bf16[2,4,4,128,128]{4,3,2,1,0:T(8,128)(2,1)S(1)}, u32[]{:S(2)}, u32[]{:S(2)}) %collective-permute-start.3) | collective-permute-done | bytes 1048608 | tf_op jit(solution)/shard_map/ppermute | solution.py:287
  77.7 8.3 %shard_map.142 = (bf16[2,4,3,128,128]{4,3,2,1,0:T(8,128)(2,1)S(1)}, bf16[2,4,3,128,128]{4,3,2,1,0:T(8,128)(2,1)S(1)}, bf16[1024,512]{1,0:T(8,128)(2,1)S(1)}, bf1...) custom-call(s32[2]{0:T(128)S(1)} %pad_add_fusion.refs_0_, ...), custom_call_target="tpu_custom_call" | custom-call | flops 4294967296 | bytes 14426120 | tf_op jit(solution)/shard_map/pallas_call | solution.py:112
  95.7 2.2 %collective-permute-done.10.refs_3_ = bf16[7,128,128]{2,1,0:T(8,128)(2,1)S(1)} collective-permute-done((bf16[7,128,128]{2,1,0:T(8,128)(2,1)S(1)}, bf16[7,128,128]{2,1,0:T(8,128)(2,1)S(1)}, u32[]{:S(2)}, u32[]{:S(2)}) %collective-permute-start.10) | collective-permute-done | bytes 229408 | tf_op jit(solution)/shard_map/ppermute | solution.py:308
  98.3 6.5 %collective-permute-done.11.refs_5_ = bf16[7,128,128]{2,1,0:T(8,128)(2,1)S(1)} collective-permute-done((bf16[7,128,128]{2,1,0:T(8,128)(2,1)S(1)}, bf16[7,128,128]{2,1,0:T(8,128)(2,1)S(1)}, u32[]{:S(2)}, u32[]{:S(2)}) %collective-permute-start.11) | collective-permute-done | bytes 229408 | tf_op jit(solution)/shard_map/ppermute | solution.py:308
  104.8 2.3 %collective-permute-done.13.refs_7_ = bf16[7,128,128]{2,1,0:T(8,128)(2,1)S(1)} collective-permute-done((bf16[7,128,128]{2,1,0:T(8,128)(2,1)S(1)}, bf16[7,128,128]{2,1,0:T(8,128)(2,1)S(1)}, u32[]{:S(2)}, u32[]{:S(2)}) %collective-permute-start.13) | collective-permute-done | bytes 229408 | tf_op jit(solution)/shard_map/ppermute | solution.py:308
  107.0 4.8 %collective-permute-done.9.refs_2_ = bf16[7,128,128]{2,1,0:T(8,128)(2,1)S(1)} collective-permute-done((bf16[7,128,128]{2,1,0:T(8,128)(2,1)S(1)}, bf16[7,128,128]{2,1,0:T(8,128)(2,1)S(1)}, u32[]{:S(2)}, u32[]{:S(2)}) %collective-permute-start.9) | collective-permute-done | bytes 229408 | tf_op jit(solution)/shard_map/ppermute | solution.py:308
  112.5 2.3 %collective-permute-start.16 = (bf16[7,32,128]{2,1,0:T(8,128)(2,1)S(1)}, bf16[7,32,128]{2,1,0:T(8,128)(2,1)S(1)}, u32[]{:S(2)}, u32[]{:S(2)}) collective-permute-start(bf16[7,32,128]{2,1,0:T(8,128)(2,1)S(1)} %get-tuple-element.91), channel_id=1, source_target_pairs={{0,12},{1,13},{2,14},{3,15},{4,0},{5,1},{6,2},{7,3},{8,4},{9,5},{1... | collective-permute-start | bytes 172040 | tf_op jit(solution)/shard_map/ppermute | solution.py:308
  119.4 2.1 %collective-permute-done.18.refs_6_ = bf16[7,32,128]{2,1,0:T(8,128)(2,1)S(1)} collective-permute-done((bf16[7,32,128]{2,1,0:T(8,128)(2,1)S(1)}, bf16[7,32,128]{2,1,0:T(8,128)(2,1)S(1)}, u32[]{:S(2)}, u32[]{:S(2)}) %collective-permute-start.18) | collective-permute-done | bytes 57376 | tf_op jit(solution)/shard_map/ppermute | solution.py:308
  122.3 7.5 %all-to-all-start.2 = ((bf16[16,32,256]{2,1,0:T(8,128)(2,1)}), bf16[16,32,256]{2,1,0:T(8,128)(2,1)S(1)}, u32[]{:S(2)}, u32[]{:S(2)}) async-start(bf16[16,32,256]{2,1,0:T(8,128)(2,1)} %shard_map.147), calls=%async_computation.2 | async-start | bytes 524288 | tf_op jit(solution)/shard_map/all_to_all | solution.py:392
  129.9 9.4 %all-to-all-done.2.refs_0_ = bf16[16,32,256]{2,1,0:T(8,128)(2,1)S(1)} async-done(((bf16[16,32,256]{2,1,0:T(8,128)(2,1)}), bf16[16,32,256]{2,1,0:T(8,128)(2,1)S(1)}, u32[]{:S(2)}, u32[]{:S(2)}) %all-to-all-start.2) | async-done | bytes 262176 | tf_op jit(solution)/shard_map/all_to_all | solution.py:392
  139.2 10.1 %all-to-all-start.1 = ((bf16[128,8,512]{2,1,0:T(8,128)(2,1)}), bf16[128,8,512]{2,1,0:T(8,128)(2,1)S(1)}, u32[]{:S(2)}, u32[]{:S(2)}) async-start(bf16[128,8,512]{2,1,0:T(8,128)(2,1)} %bitcast.31), calls=%async_computation.1 | async-start | bytes 2097152 | tf_op jit(solution)/shard_map/all_to_all | solution.py:299
  150.0 6.3 %collective-permute-start.5 = (bf16[64,512]{1,0:T(8,128)(2,1)}, bf16[64,512]{1,0:T(8,128)(2,1)S(1)}, u32[]{:S(2)}, u32[]{:S(2)}) collective-permute-start(bf16[64,512]{1,0:T(8,128)(2,1)} %copy-done.30), channel_id=1, source_target_pairs={{0,127},{1,0},{2,1},{3,2},{4,3},{5,4},{6,5},{7,6},{8,7},{9,8},{10,... | collective-permute-start | bytes 196616 | tf_op jit(solution)/shard_map/ppermute | solution.py:292
  156.4 2.0 %copy-done.3 = bf16[3584,512]{1,0:T(8,128)(2,1)S(1)} copy-done((bf16[3584,512]{1,0:T(8,128)(2,1)S(1)}, bf16[3584,512]{1,0:T(8,128)(2,1)}, u32[]{:S(2)}) %copy-start.3) | copy-done | bytes 3670040
  160.5 2.5 %shard_map.143 = (bf16[1024,512]{1,0:T(8,128)(2,1)}, f32[512,512]{1,0:T(8,128)S(1)}) custom-call(bf16[3584,512]{1,0:T(8,128)(2,1)S(1)} %copy-done.3, bf16[3584,512]{1,0:T(8,128)(2,1)S(1)} %copy-done.3, bf16[3584,512]{1,0:T(8,128)(2,1)S(1)} %copy-done.3, bf16[1024,512]{1,0:T(8,128)(2,1)S(1)} %copy-done.10, bf16[512,512]{1,0:T(8,128)(2,1)S(1)} %copy-done.16, ...), custom_call_target="tpu_custom_call" | custom-call | flops 1073741824 | bytes 16252928 | tf_op jit(solution)/shard_map/pallas_call | solution.py:112
  164.8 14.3 %collective-permute-done.4.refs_3_ = bf16[64,512]{1,0:T(8,128)(2,1)S(1)} collective-permute-done((bf16[64,512]{1,0:T(8,128)(2,1)}, bf16[64,512]{1,0:T(8,128)(2,1)S(1)}, u32[]{:S(2)}, u32[]{:S(2)}) %collective-permute-start.4) | collective-permute-done | bytes 65568 | tf_op jit(solution)/shard_map/ppermute | solution.py:292
  (105 shorter events, 36.8 us)
Async XLA Ops:
  4.8 14.2 %collective-permute-start = (bf16[1024,512]{1,0:T(8,128)(2,1)S(1)}, bf16[1024,512]{1,0:T(8,128)(2,1)S(1)}, u32[]{:S(2)}, u32[]{:S(2)}) collective-permute-start(bf16[1024,512]{1,0:T(8,128)(2,1)S(1)} %get-tuple-element.50), channel_id=1, source_target_pairs={{0,128},{128,0},{1,129},{129,1},{2,130},{130,2},{3,131},{131,3},{4... | collective-permute-start | bytes 3145736 | tf_op jit(solution)/shard_map/ppermute | solution.py:287
  8.2 10.9 %collective-permute-start.1 = (bf16[64,512]{1,0:T(8,128)(2,1)S(1)}, bf16[64,512]{1,0:T(8,128)(2,1)S(1)}, u32[]{:S(2)}, u32[]{:S(2)}) collective-permute-start(bf16[64,512]{1,0:T(8,128)(2,1)S(1)} %get-tuple-element.51), channel_id=1, source_target_pairs={{0,1},{1,2},{2,3},{3,4},{4,5},{5,6},{6,7},{7,8},{8,9},{9,10},{10,1... | collective-permute-start | bytes 196616 | tf_op jit(solution)/shard_map/ppermute | solution.py:292
  8.2 10.9 %collective-permute-start.2 = (bf16[64,512]{1,0:T(8,128)(2,1)S(1)}, bf16[64,512]{1,0:T(8,128)(2,1)S(1)}, u32[]{:S(2)}, u32[]{:S(2)}) collective-permute-start(bf16[64,512]{1,0:T(8,128)(2,1)S(1)} %get-tuple-element.52), channel_id=1, source_target_pairs={{0,127},{1,0},{2,1},{3,2},{4,3},{5,4},{6,5},{7,6},{8,7},{9,8},{10,... | collective-permute-start | bytes 196616 | tf_op jit(solution)/shard_map/ppermute | solution.py:292
  20.1 38.5 %all-to-all-start = ((bf16[128,8,512]{2,1,0:T(8,128)(2,1)}), bf16[128,8,512]{2,1,0:T(8,128)(2,1)S(1)}, u32[]{:S(2)}, u32[]{:S(2)}) async-start(bf16[128,8,512]{2,1,0:T(8,128)(2,1)} %bitcast.32), calls=%async_computation | async-start | bytes 2097152 | tf_op jit(solution)/shard_map/all_to_all | solution.py:299
  70.5 7.2 %collective-permute-start.3 = (bf16[2,4,4,128,128]{4,3,2,1,0:T(8,128)(2,1)S(1)}, bf16[2,4,4,128,128]{4,3,2,1,0:T(8,128)(2,1)S(1)}, u32[]{:S(2)}, u32[]{:S(2)}) collective-permute-start(bf16[2,4,4,128,128]{4,3,2,1,0:T(8,128)(2,1)S(1)} %get-tuple-element.65), channel_id=1, source_target_pairs={{0,128},{128,0},{1,129},{129,1},{2,130},{130,2},{3,131},{131,3},{4... | collective-permute-start | bytes 3145736 | tf_op jit(solution)/shard_map/ppermute | solution.py:287
  88.4 2.3 %collective-permute-start.7 = (bf16[2,4,3,128,128]{4,3,2,1,0:T(8,128)(2,1)S(1)}, bf16[2,4,3,128,128]{4,3,2,1,0:T(8,128)(2,1)S(1)}, u32[]{:S(2)}, u32[]{:S(2)}) collective-permute-start(bf16[2,4,3,128,128]{4,3,2,1,0:T(8,128)(2,1)S(1)} %get-tuple-element.77), channel_id=1, source_target_pairs={{0,128},{128,0},{1,129},{129,1},{2,130},{130,2},{3,131},{131,3},{4... | collective-permute-start | bytes 2359304 | tf_op jit(solution)/shard_map/ppermute | solution.py:287
  90.7 65.7 %copy-start.10 = (bf16[1024,512]{1,0:T(8,128)(2,1)S(1)}, bf16[1024,512]{1,0:T(8,128)(2,1)}, u32[]{:S(2)}) copy-start(bf16[1024,512]{1,0:T(8,128)(2,1)} %copy-done.9) | copy-start | bytes 3145732
  91.1 6.9 %collective-permute-start.10 = (bf16[7,128,128]{2,1,0:T(8,128)(2,1)S(1)}, bf16[7,128,128]{2,1,0:T(8,128)(2,1)S(1)}, u32[]{:S(2)}, u32[]{:S(2)}) collective-permute-start(bf16[7,128,128]{2,1,0:T(8,128)(2,1)S(1)} %get-tuple-element.83), channel_id=1, source_target_pairs={{0,3},{1,0},{2,1},{3,2},{4,7},{5,4},{6,5},{7,6},{8,11},{9,8},{10,9... | collective-permute-start | bytes 688136 | tf_op jit(solution)/shard_map/ppermute | solution.py:308
  92.1 12.6 %collective-permute-start.11 = (bf16[7,128,128]{2,1,0:T(8,128)(2,1)S(1)}, bf16[7,128,128]{2,1,0:T(8,128)(2,1)S(1)}, u32[]{:S(2)}, u32[]{:S(2)}) collective-permute-start(bf16[7,128,128]{2,1,0:T(8,128)(2,1)S(1)} %get-tuple-element.85), channel_id=1, source_target_pairs={{0,4},{1,5},{2,6},{3,7},{4,8},{5,9},{6,10},{7,11},{8,12},{9,13},{1... | collective-permute-start | bytes 688136 | tf_op jit(solution)/shard_map/ppermute | solution.py:308
  92.1 37.7 %collective-permute-start.6 = (bf16[1024,512]{1,0:T(8,128)(2,1)}, bf16[1024,512]{1,0:T(8,128)(2,1)S(1)}, u32[]{:S(2)}, u32[]{:S(2)}) collective-permute-start(bf16[1024,512]{1,0:T(8,128)(2,1)} %get-tuple-element.74), channel_id=1, source_target_pairs={{0,128},{128,0},{1,129},{129,1},{2,130},{130,2},{3,131},{131,3},{4... | collective-permute-start | bytes 3145736 | tf_op jit(solution)/shard_map/ppermute | solution.py:287
  92.8 12.0 %collective-permute-start.12 = (bf16[7,128,128]{2,1,0:T(8,128)(2,1)S(1)}, bf16[7,128,128]{2,1,0:T(8,128)(2,1)S(1)}, u32[]{:S(2)}, u32[]{:S(2)}) collective-permute-start(bf16[7,128,128]{2,1,0:T(8,128)(2,1)S(1)} %get-tuple-element.86), channel_id=1, source_target_pairs={{0,8},{1,9},{2,10},{3,11},{4,12},{5,13},{6,14},{7,15},{8,0},{9,1},... | collective-permute-start | bytes 688136 | tf_op jit(solution)/shard_map/ppermute | solution.py:308
  94.0 13.0 %collective-permute-start.13 = (bf16[7,128,128]{2,1,0:T(8,128)(2,1)S(1)}, bf16[7,128,128]{2,1,0:T(8,128)(2,1)S(1)}, u32[]{:S(2)}, u32[]{:S(2)}) collective-permute-start(bf16[7,128,128]{2,1,0:T(8,128)(2,1)S(1)} %get-tuple-element.87), channel_id=1, source_target_pairs={{0,12},{1,13},{2,14},{3,15},{4,0},{5,1},{6,2},{7,3},{8,4},{9,5},{1... | collective-permute-start | bytes 688136 | tf_op jit(solution)/shard_map/ppermute | solution.py:308
  98.0 9.1 %collective-permute-start.8 = (bf16[7,128,128]{2,1,0:T(8,128)(2,1)S(1)}, bf16[7,128,128]{2,1,0:T(8,128)(2,1)S(1)}, u32[]{:S(2)}, u32[]{:S(2)}) collective-permute-start(bf16[7,128,128]{2,1,0:T(8,128)(2,1)S(1)} %get-tuple-element.81), channel_id=1, source_target_pairs={{0,1},{1,2},{2,3},{3,0},{4,5},{5,6},{6,7},{7,4},{8,9},{9,10},{10,1... | collective-permute-start | bytes 688136 | tf_op jit(solution)/shard_map/ppermute | solution.py:308
  104.8 7.1 %collective-permute-start.9 = (bf16[7,128,128]{2,1,0:T(8,128)(2,1)S(1)}, bf16[7,128,128]{2,1,0:T(8,128)(2,1)S(1)}, u32[]{:S(2)}, u32[]{:S(2)}) collective-permute-start(bf16[7,128,128]{2,1,0:T(8,128)(2,1)S(1)} %get-tuple-element.82), channel_id=1, source_target_pairs={{0,2},{1,3},{2,0},{3,1},{4,6},{5,7},{6,4},{7,5},{8,10},{9,11},{10,... | collective-permute-start | bytes 688136 | tf_op jit(solution)/shard_map/ppermute | solution.py:308
  112.1 4.3 %collective-permute-start.14 = (bf16[7,32,128]{2,1,0:T(8,128)(2,1)S(1)}, bf16[7,32,128]{2,1,0:T(8,128)(2,1)S(1)}, u32[]{:S(2)}, u32[]{:S(2)}) collective-permute-start(bf16[7,32,128]{2,1,0:T(8,128)(2,1)S(1)} %get-tuple-element.89), channel_id=1, source_target_pairs={{0,4},{1,5},{2,6},{3,7},{4,8},{5,9},{6,10},{7,11},{8,12},{9,13},{1... | collective-permute-start | bytes 172040 | tf_op jit(solution)/shard_map/ppermute | solution.py:308
  112.2 5.4 %collective-permute-start.15 = (bf16[7,32,128]{2,1,0:T(8,128)(2,1)S(1)}, bf16[7,32,128]{2,1,0:T(8,128)(2,1)S(1)}, u32[]{:S(2)}, u32[]{:S(2)}) collective-permute-start(bf16[7,32,128]{2,1,0:T(8,128)(2,1)S(1)} %get-tuple-element.90), channel_id=1, source_target_pairs={{0,8},{1,9},{2,10},{3,11},{4,12},{5,13},{6,14},{7,15},{8,0},{9,1},... | collective-permute-start | bytes 172040 | tf_op jit(solution)/shard_map/ppermute | solution.py:308
  112.5 6.8 %collective-permute-start.16 = (bf16[7,32,128]{2,1,0:T(8,128)(2,1)S(1)}, bf16[7,32,128]{2,1,0:T(8,128)(2,1)S(1)}, u32[]{:S(2)}, u32[]{:S(2)}) collective-permute-start(bf16[7,32,128]{2,1,0:T(8,128)(2,1)S(1)} %get-tuple-element.91), channel_id=1, source_target_pairs={{0,12},{1,13},{2,14},{3,15},{4,0},{5,1},{6,2},{7,3},{8,4},{9,5},{1... | collective-permute-start | bytes 172040 | tf_op jit(solution)/shard_map/ppermute | solution.py:308
  114.8 4.5 %collective-permute-start.17 = (bf16[7,32,128]{2,1,0:T(8,128)(2,1)S(1)}, bf16[7,32,128]{2,1,0:T(8,128)(2,1)S(1)}, u32[]{:S(2)}, u32[]{:S(2)}) collective-permute-start(bf16[7,32,128]{2,1,0:T(8,128)(2,1)S(1)} %get-tuple-element.93), channel_id=1, source_target_pairs={{0,1},{1,2},{2,3},{3,0},{4,5},{5,6},{6,7},{7,4},{8,9},{9,10},{10,1... | collective-permute-start | bytes 172040 | tf_op jit(solution)/shard_map/ppermute | solution.py:308
  116.4 5.1 %collective-permute-start.18 = (bf16[7,32,128]{2,1,0:T(8,128)(2,1)S(1)}, bf16[7,32,128]{2,1,0:T(8,128)(2,1)S(1)}, u32[]{:S(2)}, u32[]{:S(2)}) collective-permute-start(bf16[7,32,128]{2,1,0:T(8,128)(2,1)S(1)} %get-tuple-element.94), channel_id=1, source_target_pairs={{0,2},{1,3},{2,0},{3,1},{4,6},{5,7},{6,4},{7,5},{8,10},{9,11},{10,... | collective-permute-start | bytes 172040 | tf_op jit(solution)/shard_map/ppermute | solution.py:308
  117.5 4.0 %collective-permute-start.19 = (bf16[7,32,128]{2,1,0:T(8,128)(2,1)S(1)}, bf16[7,32,128]{2,1,0:T(8,128)(2,1)S(1)}, u32[]{:S(2)}, u32[]{:S(2)}) collective-permute-start(bf16[7,32,128]{2,1,0:T(8,128)(2,1)S(1)} %get-tuple-element.95), channel_id=1, source_target_pairs={{0,3},{1,0},{2,1},{3,2},{4,7},{5,4},{6,5},{7,6},{8,11},{9,8},{10,9... | collective-permute-start | bytes 172040 | tf_op jit(solution)/shard_map/ppermute | solution.py:308
  122.3 16.9 %all-to-all-start.2 = ((bf16[16,32,256]{2,1,0:T(8,128)(2,1)}), bf16[16,32,256]{2,1,0:T(8,128)(2,1)S(1)}, u32[]{:S(2)}, u32[]{:S(2)}) async-start(bf16[16,32,256]{2,1,0:T(8,128)(2,1)} %shard_map.147), calls=%async_computation.2 | async-start | bytes 524288 | tf_op jit(solution)/shard_map/all_to_all | solution.py:392
  139.2 39.8 %all-to-all-start.1 = ((bf16[128,8,512]{2,1,0:T(8,128)(2,1)}), bf16[128,8,512]{2,1,0:T(8,128)(2,1)S(1)}, u32[]{:S(2)}, u32[]{:S(2)}) async-start(bf16[128,8,512]{2,1,0:T(8,128)(2,1)} %bitcast.31), calls=%async_computation.1 | async-start | bytes 2097152 | tf_op jit(solution)/shard_map/all_to_all | solution.py:299
  149.4 29.7 %collective-permute-start.4 = (bf16[64,512]{1,0:T(8,128)(2,1)}, bf16[64,512]{1,0:T(8,128)(2,1)S(1)}, u32[]{:S(2)}, u32[]{:S(2)}) collective-permute-start(bf16[64,512]{1,0:T(8,128)(2,1)} %get-tuple-element.72), channel_id=1, source_target_pairs={{0,1},{1,2},{2,3},{3,4},{4,5},{5,6},{6,7},{7,8},{8,9},{9,10},{10,1... | collective-permute-start | bytes 196616 | tf_op jit(solution)/shard_map/ppermute | solution.py:292
  150.0 29.0 %collective-permute-start.5 = (bf16[64,512]{1,0:T(8,128)(2,1)}, bf16[64,512]{1,0:T(8,128)(2,1)S(1)}, u32[]{:S(2)}, u32[]{:S(2)}) collective-permute-start(bf16[64,512]{1,0:T(8,128)(2,1)} %copy-done.30), channel_id=1, source_target_pairs={{0,127},{1,0},{2,1},{3,2},{4,3},{5,4},{6,5},{7,6},{8,7},{9,8},{10,... | collective-permute-start | bytes 196616 | tf_op jit(solution)/shard_map/ppermute | solution.py:292
  (34 other events, 336.6 us)

commit v4 on v3

--- a/solution.py
+++ b/solution.py
@@ -11,6 +11,7 @@
 RING = 4
 PLANE = RING * RING
 TILE = 256
+LIMIT = 61 * 2**20 - 2**16
 BF = jnp.bfloat16
 F32 = jnp.float32
 I32 = jnp.int32
@@ -71,52 +72,91 @@
         self.copy, self.buffer, self.waited = copy, buffer, False
         self.shape = buffer.shape
 
-    def __getitem__(self, index):
+    def wait(self):
         if not self.waited:
             self.copy.wait()
             self.waited = True
+
+    def __getitem__(self, index):
+        self.wait()
         return self.buffer[index]
 
 
-def call(kernel, args, outs, scratch=(), flops=0):
+class Staged:
+    def __init__(self, copy, buffer):
+        self.copy, self.buffer, self.sent = copy, buffer, False
+        self.shape = buffer.shape
+
+    def __getitem__(self, index):
+        return self.buffer[index]
+
+    def __setitem__(self, index, value):
+        self.buffer[index] = value
+
+    def flush(self):
+        if not self.sent:
+            self.copy.start()
+            self.sent = True
+
+
+def flush(*refs):
+    for ref in refs:
+        ref.flush()
+
+
+def cost(arrays, flops):
+    size = sum(math.prod(a.shape) * a.dtype.itemsize for a in arrays)
+    return pl.CostEstimate(flops=flops, bytes_accessed=size, transcendentals=0)
+
+
+def call(kernel, args, outs):
+    return pl.pallas_call(
+        kernel,
+        out_shape=tuple(outs),
+        in_specs=[VMEM] * len(args),
+        out_specs=tuple([VMEM] * len(outs)),
+        compiler_params=pltpu.CompilerParams(vmem_limit_bytes=14 * 2**20),
+        cost_estimate=cost(list(args) + list(outs), 0),
+    )(*args)
+
+
+def stream(kernel, args, outs, scratch=(), flops=0):
+    args = [a if isinstance(a, Far) or a.ndim == 1 else Far(a) for a in args]
     far = [i for i, a in enumerate(args) if isinstance(a, Far)]
     arrays = [a.array if isinstance(a, Far) else a for a in args]
-    buffers = [
+    held = [
         pltpu.VMEM((args[i].size,) + args[i].array.shape[1:], args[i].array.dtype) for i in far
     ]
-    specs = [
-        pl.BlockSpec(memory_space=pl.ANY)
-        if isinstance(a, Far)
-        else (SMEM if a.dtype == I32 and a.ndim == 1 else VMEM)
-        for a in args
-    ]
-    ins, made = len(args), len(args) + len(outs)
+    held += [pltpu.VMEM(o.shape, o.dtype) for o in outs]
+    hbm = pl.BlockSpec(memory_space=pltpu.HBM)
+    ins, made, moved = len(args), len(args) + len(outs), len(far) + len(outs)
 
     def body(*refs):
-        held = refs[made : made + len(far)]
-        refs_in = list(refs[:ins])
-        if far:
-            sems = refs[made + len(far)]
+        buffers, sems, rest = refs[made : made + moved], refs[made + moved], refs[made + moved + 1 :]
+        reads = list(refs[:ins])
         for k, i in enumerate(far):
-            source = refs_in[i].at[args[i].start : args[i].start + args[i].size]
-            copy = pltpu.make_async_copy(source, held[k], sems.at[k])
+            source = reads[i].at[args[i].start : args[i].start + args[i].size]
+            copy = pltpu.make_async_copy(source, buffers[k], sems.at[k])
             copy.start()
-            refs_in[i] = Fetched(copy, held[k])
-        kernel(*refs_in, *refs[ins:made], *refs[made + len(far) + (1 if far else 0) :])
+            reads[i] = Fetched(copy, buffers[k])
+        writes = []
+        for k, out in enumerate(refs[ins:made], len(far)):
+            writes.append(Staged(pltpu.make_async_copy(buffers[k], out, sems.at[k]), buffers[k]))
+        kernel(*reads, *writes, *rest)
+        flush(*writes)
         for i in far:
-            if not refs_in[i].waited:
-                refs_in[i].copy.wait()
-
-    size = sum(math.prod(a.shape) * a.dtype.itemsize for a in arrays + list(outs))
-    extra = buffers + ([pltpu.SemaphoreType.DMA((len(far),))] if far else [])
+            reads[i].wait()
+        for write in writes:
+            write.copy.wait()
+
     return pl.pallas_call(
         body,
         out_shape=tuple(outs),
-        in_specs=specs,
-        out_specs=tuple([VMEM] * len(outs)),
-        scratch_shapes=extra + list(scratch),
-        compiler_params=pltpu.CompilerParams(vmem_limit_bytes=16 * 2**20),
-        cost_estimate=pl.CostEstimate(flops=flops, bytes_accessed=size, transcendentals=0),
+        in_specs=[hbm if isinstance(a, Far) else SMEM for a in args],
+        out_specs=tuple([hbm] * len(outs)),
+        scratch_shapes=held + [pltpu.SemaphoreType.DMA((moved,))] + list(scratch),
+        compiler_params=pltpu.CompilerParams(vmem_limit_bytes=LIMIT),
+        cost_estimate=cost(arrays + list(outs), flops),
     )(*arrays)
 
 
@@ -141,6 +181,7 @@
     halo = dot(pick(column(halo_ref[...]), width), nodes).astype(BF)
     low_ref[...] = halo[:depth]
     high_ref[...] = halo[depth:]
+    flush(low_ref, high_ref, live_ref)
     col = column(live)
     for r in tiles(slots):
         out_ref[r] = dot(pick(col[r], width), nodes).astype(BF)
@@ -166,6 +207,7 @@
         sigma = jax.nn.sigmoid(pre)
         hid_ref[r] = (pre * sigma).astype(BF)
         slope_ref[r] = (sigma * (1.0 + pre * (1.0 - sigma))).astype(BF)
+    flush(slope_ref)
     for r in tiles(count):
         agg = dot(pick_t(dst_ref[...], r.start, TILE), hid_ref[...]).astype(BF)
         agg_ref[r] = agg
@@ -173,7 +215,7 @@
 
 
 def node_kernel(
-    target_ref, margin_ref, nodes_ref, a_ref, b_ref, cot_ref, second_ref, msg_ref, recv_ref,
+    target_ref, margin_ref, recv_ref, msg_ref, nodes_ref, a_ref, b_ref, cot_ref, second_ref,
     new_ref, pooled_ref, hid_ref, gpre_ref, gpool_ref, part_ref, ret_ref,
 ):
     count, width = nodes_ref.shape
@@ -194,6 +236,7 @@
         gpool_ref[r] = dot_nt(gpre, b_ref[...]).astype(BF)
         new_ref[r] = (nodes.astype(F32) + dot(hidden, second_ref[...])).astype(BF)
         part_ref[r] = cot.astype(F32) + dot_nt(gpre, a_ref[...])
+    flush(new_ref, pooled_ref, hid_ref, gpre_ref, gpool_ref, part_ref)
     col, weight = column(target), column(margin)
     gpool = gpool_ref[...]
     for r in tiles(recv_ref.shape[0]):
@@ -216,7 +259,7 @@
 
 
 def node_grad_kernel(
-    side_ref, agg_ref, nodes_ref, pooled_ref, hid_ref, gpre_ref, gpool_ref, cot_ref, own_ref, send_ref,
+    side_ref, agg_ref, gpool_ref, nodes_ref, gpre_ref, pooled_ref, hid_ref, cot_ref, own_ref, send_ref,
     *, patches, scale
 ):
     order = row_order(side_ref[1], nodes_ref.shape[1], patches)
@@ -228,7 +271,7 @@
 
 
 def edge_grad_kernel(
-    side_ref, dst_ref, second_ref, edges_ref, src_ref, nodes_ref, wa_ref, low_ref, high_ref, slope_ref, gpool_ref,
+    side_ref, dst_ref, gpool_ref, second_ref, slope_ref, edges_ref, src_ref, nodes_ref, low_ref, high_ref, wa_ref,
     own_ref, send_ref, gpre_ref, bysrc_ref, bydst_ref, glow_ref, ghigh_ref,
     *, patches, scale
 ):
@@ -243,12 +286,14 @@
     for r in tiles(edges_ref.shape[0]):
         message = dot(pick(dst[r], count), gpool).astype(BF)
         gpre_ref[r] = (dot_nt(message, second) * slope_ref[r].astype(F32)).astype(BF)
+    flush(gpre_ref)
     order = row_order(side_ref[1], width, patches)
     turned = dot_nt(order, edges_ref[...]).astype(BF)
     put(own_ref, send_ref, 2, dot(turned, gpre_ref[...]) * scale, first)
     for r in tiles(count):
         bydst_ref[r] = dot(pick_t(dst_row, r.start, TILE), gpre_ref[...]).astype(BF)
         bysrc_ref[r] = dot(pick_t(src_row[:, :inner], r.start, TILE), gpre_ref[:inner]).astype(BF)
+    flush(bysrc_ref, bydst_ref)
     halo = dot(pick_t(src_row[:, inner:], count, 2 * depth), gpre_ref[inner:]).astype(BF)
     turned = dot_nt(order, nodes_ref[...]).astype(BF)
     put(own_ref, send_ref, 1, dot(turned, bydst_ref[...]) * scale, first)
@@ -260,11 +305,12 @@
 
 
 def edge_rest_kernel(
-    wc_ref, wa_ref, wb_ref, gpre_ref, bysrc_ref, bydst_ref, part_ref, edge_ref, total_ref
+    gpre_ref, wc_ref, bysrc_ref, wa_ref, bydst_ref, wb_ref, part_ref, edge_ref, total_ref
 ):
     count, width = bysrc_ref.shape
     for r in tiles(gpre_ref.shape[0]):
         edge_ref[r] = dot_nt(gpre_ref[r], wc_ref[...]).astype(BF)
+    flush(edge_ref)
     for r in tiles(count):
         total_ref[r] = (
             part_ref[r]
@@ -300,11 +346,12 @@
     return routed.reshape(rows, width)
 
 
-def hop(value, dy=0, dx=0):
+def hop(value, dz=0, dy=0, dx=0):
+    depth = lax.axis_size("patch") // PLANE
     pairs = []
-    for p in range(lax.axis_size("patch")):
+    for p in range(depth * PLANE):
         z, y, x = p // PLANE, p // RING % RING, p % RING
-        pairs.append((p, z * PLANE + (y + dy) % RING * RING + (x + dx) % RING))
+        pairs.append((p, (z + dz) % depth * PLANE + (y + dy) % RING * RING + (x + dx) % RING))
     return lax.ppermute(value, "patch", pairs)
 
 
@@ -362,7 +409,7 @@
         out_ref[:, side * lane : (side + 1) * lane] = total[: out_ref.shape[0]]
 
 
-def weight_sums(own_a, other_a, own_b, other_b):
+def weight_sums(own_a, other_a, own_b, other_b, couple_back, total):
     patches = lax.axis_size("patch")
     depth = patches // PLANE
     rows, lane = own_a.shape[3:]
@@ -380,20 +427,22 @@
         if kernel is not None:
             pieces = call(kernel, pieces, (small,) * (2 * RING))
     padded = (blocks * fine + 15) // 16 * 16
-    (part,) = call(
+    (part,) = pl.pallas_call(
         depth_kernel,
-        pieces,
-        (shape(BF, 2 * depth, padded, 2 * lane),),
-        scratch=(pltpu.VMEM((depth, padded, 2 * lane), F32),),
-    )
+        out_shape=(shape(BF, 2 * depth, padded, 2 * lane),),
+        in_specs=[VMEM] * len(pieces),
+        out_specs=(VMEM,),
+        scratch_shapes=[pltpu.VMEM((depth, padded, 2 * lane), F32)],
+    )(*pieces)
+    part, couple_back, total = lax.optimization_barrier((part, couple_back, total))
     columns = [
         [m * patches + z * PLANE + i for m in range(2) for z in range(depth)] for i in range(PLANE)
     ]
     both = lax.all_to_all(
         part, ("mesh", "patch"), split_axis=0, concat_axis=0, axis_index_groups=columns, tiled=True
     )
-    (total,) = call(finish_kernel, (both,), (shape(F32, blocks * fine, 4 * lane),))
-    return total.reshape(blocks, fine * 4 * lane)
+    (result,) = call(finish_kernel, (both,), (shape(F32, blocks * fine, 4 * lane),))
+    return result.reshape(blocks, fine * 4 * lane), couple_back, total
 
 
 def shards(
@@ -425,9 +474,12 @@
     def weight(block):
         return Far(weights, block * width, width)
 
-    outgoing, low_out, high_out, live = call(
+    def weight(block):
+        return Far(weights, block * width, width)
+
+    outgoing, low_out, high_out, live = stream(
         send_kernel,
-        (Far(couple_rows[0]), Far(couple_count[0]), Far(halo_rows), Far(nodes_own)),
+        (couple_rows[0], couple_count[0], halo_rows, nodes_own),
         (shape(BF, slots, width), shape(BF, depth, width), shape(BF, depth, width), shape(I32, 1, slots)),
         flops=(slots + 2 * depth) * unit,
     )
@@ -435,42 +487,39 @@
     low, high = shift(high_out, 1), shift(low_out, -1)
     crossed, low, high = lax.optimization_barrier((crossed, low, high))
     received = route(crossed)
-    slope, agg, message = call(
+    slope, agg, message = stream(
         edge_kernel,
         (
-            Far(edge_dst), Far(nodes_own), weight(1), Far(edge_src), low, high, weight(0),
-            Far(edges_own), weight(2), weight(3),
+            edge_dst, nodes_own, weight(1), edge_src, low, high, weight(0), edges_own, weight(2),
+            weight(3),
         ),
         (shape(BF, edge_count, width), shape(BF, count, width), shape(F32, count, width)),
         scratch=(pltpu.VMEM((edge_count, width), BF),),
         flops=edge_count * 6 * unit,
     )
     square = shape(BF, count, width)
-    new_nodes, pooled, hidden, grad_pre, grad_pooled, part, returned = call(
+    new_nodes, pooled, hidden, grad_pre, grad_pooled, part, returned = stream(
         node_kernel,
-        (
-            Far(target), Far(margin), Far(nodes_own), weight(4), weight(5), Far(cotangent), weight(6),
-            message, received,
-        ),
+        (target, margin, received, message, nodes_own, weight(4), weight(5), cotangent, weight(6)),
         (square, square, square, square, square, shape(F32, count, width), shape(BF, slots, width)),
         flops=count * 10 * unit,
     )
     crossed_back = from_partner(returned)
     couple_back = route(crossed_back)
     grad_shape = lambda blocks: shape(BF, 2, RING, blocks, width // RING, width // 4)
-    own_b, send_b = call(
+    own_b, send_b = stream(
         lambda *refs: node_grad_kernel(*refs, patches=patches, scale=scale),
-        (side, agg, Far(nodes_own), pooled, hidden, grad_pre, grad_pooled, Far(cotangent)),
+        (side, agg, grad_pooled, nodes_own, grad_pre, pooled, hidden, cotangent),
         (grad_shape(4), grad_shape(4)),
         flops=count * 8 * unit,
     )
     other_b = from_partner(send_b)
-    grad_pooled, other_b = lax.optimization_barrier((grad_pooled, other_b))
-    own_a, send_a, grad_edge_pre, by_source, by_target, grad_low, grad_high = call(
+    grad_pooled, other_b, crossed_back = lax.optimization_barrier((grad_pooled, other_b, crossed_back))
+    own_a, send_a, grad_edge_pre, by_source, by_target, grad_low, grad_high = stream(
         lambda *refs: edge_grad_kernel(*refs, patches=patches, scale=scale),
         (
-            side, Far(edge_dst), weight(3), Far(edges_own), Far(edge_src), Far(nodes_own), weight(0),
-            low, high, slope, grad_pooled,
+            side, edge_dst, grad_pooled, weight(3), slope, edges_own, edge_src, nodes_own, low, high,
+            weight(0),
         ),
         (
             grad_shape(3), grad_shape(3), shape(BF, edge_count, width), square, square,
@@ -478,17 +527,18 @@
         ),
         flops=edge_count * 8 * unit,
     )
-    summed = weight_sums(own_a, from_partner(send_a), own_b, other_b)
-    back_low, back_high = shift(grad_high, 1), shift(grad_low, -1)
-    edge_grads, total = call(
+    edge_grads, total = stream(
         edge_rest_kernel,
-        (weight(2), weight(0), weight(1), grad_edge_pre, by_source, by_target, part),
+        (grad_edge_pre, weight(2), by_source, weight(0), by_target, weight(1), part),
         (shape(BF, edge_count, width), shape(F32, count, width)),
         flops=edge_count * 2 * unit,
     )
-    (node_grads,) = call(
+    back_low, back_high = shift(grad_high, 1), shift(grad_low, -1)
+    other_a = from_partner(send_a)
+    summed, couple_back, total = weight_sums(own_a, other_a, own_b, other_b, couple_back, total)
+    (node_grads,) = stream(
         last_kernel,
-        (live, Far(halo_rows), total, back_low, back_high, couple_back),
+        (live, halo_rows, total, back_low, back_high, couple_back),
         (square,),
         flops=count * 2 * unit,
     )

time: 183 us -> 161 us (0.88)
  waiting for transfers between devices: 68 us -> 38.6 us
  local copies, waits for them, and re-layouts: 21.6 us -> 5.26 us
  Pallas kernels: 28.7 us -> 43.9 us
  starting transfers between devices: 62.7 us -> 70.9 us
    unnamed x70 -> x36, local copies, waits for them, and re-layouts: 20.9 us -> 4.6 us
    pallas_call x11, Pallas kernels: 28.7 us -> 43.9 us  [the longest x7 41.4 us: stream(): pl.pallas_call(body, out_shape=tuple(outs), in_specs=[hbm if isinstance(a...]
    ppermute x12, waiting for transfers between devices: 20.2 us -> 8.87 us  [hop(): return lax.ppermute(value, 'patch', pairs)]
    ppermute x4, waiting for transfers between devices: 16.7 us -> 6.76 us  [shift(): lax.ppermute(value, 'patch', [(i, (i + step) % count) for i in range(coun...]
    all_to_all x1, waiting for transfers between devices: 9.37 us -> 0.01 us  [weight_sums(): lax.all_to_all(part, ('mesh', 'patch'), split_axis=0, concat_axis=0, axis...]
    ppermute x12, starting transfers between devices: 9.31 us -> 18.4 us  [hop(): return lax.ppermute(value, 'patch', pairs)]
    all_to_all x2, starting transfers between devices: 21.2 us -> 17.1 us  [route(): lax.all_to_all(crossed, 'patch', split_axis=0, concat_axis=0, tiled=True)]
    all_to_all x1, starting transfers between devices: 7.55 us -> 11.2 us  [weight_sums(): lax.all_to_all(part, ('mesh', 'patch'), split_axis=0, concat_axis=0, axis...]
  transfers between devices with their start and end apart: 23 -> 23, of which waited for: 14 -> 8; matrix products, arithmetic and copies ran while one was open for 0% -> 0% of each run, Pallas kernels for 5% -> 21%
where the time goes in v4:
time: 161 us; the launch traced here: 160 us
  starting transfers between devices  70.9 us (44%)
  Pallas kernels  43.9 us (27%)
  waiting for transfers between devices  38.6 us (24%)
  local copies, waits for them, and re-layouts  5.26 us (3%)
    pallas_call x7, Pallas kernels, stream(): pl.pallas_call(body, out_shape=tuple(outs), in_specs=[hbm if isinstance(a...  41.4 us
    all_to_all x2, waiting for transfers between devices, route(): lax.all_to_all(crossed, 'patch', split_axis=0, concat_axis=0, tiled=True)  20.8 us
    ppermute x12, starting transfers between devices, hop(): return lax.ppermute(value, 'patch', pairs)  18.4 us
    all_to_all x2, starting transfers between devices, route(): lax.all_to_all(crossed, 'patch', split_axis=0, concat_axis=0, tiled=True)  17.1 us
    ppermute x4, starting transfers between devices, shift(): lax.ppermute(value, 'patch', [(i, (i + step) % count) for i in range(coun...  15.5 us
    all_to_all x1, starting transfers between devices, weight_sums(): lax.all_to_all(part, ('mesh', 'patch'), split_axis=0, concat_axis=0, axis...  11.2 us
    ppermute x12, waiting for transfers between devices, hop(): return lax.ppermute(value, 'patch', pairs)  8.87 us
    ppermute x4, starting transfers between devices, from_partner(): return lax.ppermute(value, 'mesh', [(0, 1), (1, 0)])  8.81 us
  transfers between devices with their start and end apart: 23, of which 8 were waited for; matrix products, arithmetic and copies ran while one was open for 0% of the time, Pallas kernels for 21%

profile of v4, /device:TPU:1, one launch (start us, length us, event | category | flops | bytes accessed | tf_op | source)
XLA Modules:
  0.0 160.3 jit_solution(14700278814005843085)
XLA Ops:
  0.6 3.0 %shard_map.138 = (bf16[1024,512]{1,0:T(8,128)(2,1)}, bf16[64,512]{1,0:T(8,128)(2,1)}, bf16[64,512]{1,0:T(8,128)(2,1)}, s32[1,1024]{1,0:T(1,128)}) custom-call(s32[1,1024]{1,0:T(1,128)} %bitcast.32, s32[1,128]{1,0:T(1,128)} %bitcast.33, s32[1,128]{1,0:T(1,128)} %refs_1_.5, bf16[512,512]{1,0:T(8,128)(2,1)} %bitcast.18), custom_call_target="tpu_custom_call" | custom-call | flops 603979776 | bytes 1713152 | tf_op jit(solution)/shard_map/pallas_call | solution.py:152
  3.7 3.3 %collective-permute-start = (bf16[1024,512]{1,0:T(8,128)(2,1)}, bf16[1024,512]{1,0:T(8,128)(2,1)}, u32[]{:S(2)}, u32[]{:S(2)}) collective-permute-start(bf16[1024,512]{1,0:T(8,128)(2,1)} %get-tuple-element.53), channel_id=1, source_target_pairs={{0,128},{128,0},{1,129},{129,1},{2,130},{130,2},{3,131},{131,3},{4... | collective-permute-start | bytes 3145736 | tf_op jit(solution)/shard_map/ppermute | solution.py:333
  7.0 8.5 %collective-permute-start.2 = (bf16[64,512]{1,0:T(8,128)(2,1)}, bf16[64,512]{1,0:T(8,128)(2,1)S(1)}, u32[]{:S(2)}, u32[]{:S(2)}) collective-permute-start(bf16[64,512]{1,0:T(8,128)(2,1)} %get-tuple-element.55), channel_id=1, source_target_pairs={{0,127},{1,0},{2,1},{3,2},{4,3},{5,4},{6,5},{7,6},{8,7},{9,8},{10,... | collective-permute-start | bytes 196616 | tf_op jit(solution)/shard_map/ppermute | solution.py:338
  15.5 2.6 %collective-permute-done.1.refs_4_.refs_8_ = bf16[64,512]{1,0:T(8,128)(2,1)S(1)} collective-permute-done((bf16[64,512]{1,0:T(8,128)(2,1)}, bf16[64,512]{1,0:T(8,128)(2,1)S(1)}, u32[]{:S(2)}, u32[]{:S(2)}) %collective-permute-start.1) | collective-permute-done | bytes 65568 | tf_op jit(solution)/shard_map/ppermute | solution.py:338
  18.1 10.9 %all-to-all-start = ((bf16[128,8,512]{2,1,0:T(8,128)(2,1)}), bf16[128,8,512]{2,1,0:T(8,128)(2,1)S(1)}, u32[]{:S(2)}, u32[]{:S(2)}) async-start(bf16[128,8,512]{2,1,0:T(8,128)(2,1)} %bitcast.5), calls=%async_computation | async-start | bytes 2097152 | tf_op jit(solution)/shard_map/all_to_all | solution.py:345
  29.0 6.8 %shard_map.139 = (bf16[1024,512]{1,0:T(8,128)(2,1)}, bf16[512,512]{1,0:T(8,128)(2,1)}, f32[512,512]{1,0:T(8,128)}) custom-call(s32[1,1024]{1,0:T(1,128)} %refs_1_.3, bf16[512,512]{1,0:T(8,128)(2,1)} %bitcast.19, bf16[3584,512]{1,0:T(8,128)(2,1)} %refs_5_.3, s32[1,1024]{1,0:T(1,128)} %refs_6_.5, bf16[64,512]{1,0:T(8,128)(2,1)} %copy-done.6, ...), custom_call_target="tpu_custom_call" | custom-call | flops 3221225472 | bytes 19013632 | tf_op jit(solution)/shard_map/pallas_call | solution.py:152
  35.8 20.8 %all-to-all-done = bf16[128,8,512]{2,1,0:T(8,128)(2,1)S(1)} async-done(((bf16[128,8,512]{2,1,0:T(8,128)(2,1)}), bf16[128,8,512]{2,1,0:T(8,128)(2,1)S(1)}, u32[]{:S(2)}, u32[]{:S(2)}) %all-to-all-start) | async-done | bytes 1048608 | tf_op jit(solution)/shard_map/all_to_all | solution.py:345
  57.6 6.9 %shard_map.140 = (bf16[512,512]{1,0:T(8,128)(2,1)}, bf16[512,512]{1,0:T(8,128)(2,1)}, bf16[512,512]{1,0:T(8,128)(2,1)}, bf16[512,512]{1,0:T(8,128)(2,1)}, bf16[5...) custom-call(s32[1,1024]{1,0:T(1,128)} %bitcast.28, f32[1,1024]{1,0:T(1,128)} %bitcast.29, ...), custom_call_target="tpu_custom_call" | custom-call | flops 2684354560 | bytes 18882560 | tf_op jit(solution)/shard_map/pallas_call | solution.py:152
  64.5 4.8 %collective-permute-start.4 = (bf16[1024,512]{1,0:T(8,128)(2,1)}, bf16[1024,512]{1,0:T(8,128)(2,1)}, u32[]{:S(2)}, u32[]{:S(2)}) collective-permute-start(bf16[1024,512]{1,0:T(8,128)(2,1)} %get-tuple-element.68), channel_id=1, source_target_pairs={{0,128},{128,0},{1,129},{129,1},{2,130},{130,2},{3,131},{131,3},{4... | collective-permute-start | bytes 3145736 | tf_op jit(solution)/shard_map/ppermute | solution.py:333
  70.0 6.6 %shard_map.141 = (bf16[2,4,4,128,128]{4,3,2,1,0:T(8,128)(2,1)}, bf16[2,4,4,128,128]{4,3,2,1,0:T(8,128)(2,1)}) custom-call(s32[2]{0:T(128)} %pad_add_fusion.refs_0_, bf16[512,512]{1,0:T(8,128)(2,1)} %get-tuple-element.63.refs_1_, bf16[512,512]{1,0:T(8,128)(2,1)} %get-tuple-element.69.refs_2_, bf16[512,512]{1,0:T(8,128)(2,1)} %bitcast.21, ...), custom_call_target="tpu_custom_call" | custom-call | flops 2147483648 | bytes 5767176 | tf_op jit(solution)/shard_map/pallas_call | solution.py:152
  76.7 6.2 %all-to-all-start.1 = ((bf16[128,8,512]{2,1,0:T(8,128)(2,1)}), bf16[128,8,512]{2,1,0:T(8,128)(2,1)S(1)}, u32[]{:S(2)}, u32[]{:S(2)}) async-start(bf16[128,8,512]{2,1,0:T(8,128)(2,1)} %bitcast.12), calls=%async_computation.1 | async-start | bytes 2097152 | tf_op jit(solution)/shard_map/all_to_all | solution.py:345
  82.9 10.6 %shard_map.142 = (bf16[2,4,3,128,128]{4,3,2,1,0:T(8,128)(2,1)}, bf16[2,4,3,128,128]{4,3,2,1,0:T(8,128)(2,1)}, bf16[1024,512]{1,0:T(8,128)(2,1)}, bf16[512,512]{1...) custom-call(s32[2]{0:T(128)} %pad_add_fusion.refs_0_, ...), custom_call_target="tpu_custom_call" | custom-call | flops 4294967296 | bytes 14426120 | tf_op jit(solution)/shard_map/pallas_call | solution.py:152
  94.1 2.1 %collective-permute-done.5.other_a = bf16[2,4,3,128,128]{4,3,2,1,0:T(8,128)(2,1)S(1)} collective-permute-done((bf16[2,4,3,128,128]{4,3,2,1,0:T(8,128)(2,1)}, bf16[2,4,3,128,128]{4,3,2,1,0:T(8,128)(2,1)S(1)}, u32[]{:S(2)}, u32[]{:S(2)}) %collective-permute-start.5) | collective-permute-done | bytes 786464 | tf_op jit(solution)/shard_map/ppermute | solution.py:333
  98.6 2.4 %collective-permute-start.7 = (bf16[7,128,128]{2,1,0:T(8,128)(2,1)S(1)}, bf16[7,128,128]{2,1,0:T(8,128)(2,1)S(1)}, u32[]{:S(2)}, u32[]{:S(2)}) collective-permute-start(bf16[7,128,128]{2,1,0:T(8,128)(2,1)S(1)} %get-tuple-element.77), channel_id=1, source_target_pairs={{0,2},{1,3},{2,0},{3,1},{4,6},{5,7},{6,4},{7,5},{8,10},{9,11},{10,... | collective-permute-start | bytes 688136 | tf_op jit(solution)/shard_map/ppermute | solution.py:355
  103.4 2.5 %collective-permute-start.10 = (bf16[7,128,128]{2,1,0:T(8,128)(2,1)S(1)}, bf16[7,128,128]{2,1,0:T(8,128)(2,1)S(1)}, u32[]{:S(2)}, u32[]{:S(2)}) collective-permute-start(bf16[7,128,128]{2,1,0:T(8,128)(2,1)S(1)} %get-tuple-element.81), channel_id=1, source_target_pairs={{0,8},{1,9},{2,10},{3,11},{4,12},{5,13},{6,14},{7,15},{8,0},{9,1},... | collective-permute-start | bytes 688136 | tf_op jit(solution)/shard_map/ppermute | solution.py:355
  105.8 3.3 %collective-permute-done.6.refs_1_ = bf16[7,128,128]{2,1,0:T(8,128)(2,1)S(1)} collective-permute-done((bf16[7,128,128]{2,1,0:T(8,128)(2,1)S(1)}, bf16[7,128,128]{2,1,0:T(8,128)(2,1)S(1)}, u32[]{:S(2)}, u32[]{:S(2)}) %collective-permute-start.6) | collective-permute-done | bytes 229408 | tf_op jit(solution)/shard_map/ppermute | solution.py:355
  109.1 2.5 %collective-permute-start.11 = (bf16[7,128,128]{2,1,0:T(8,128)(2,1)S(1)}, bf16[7,128,128]{2,1,0:T(8,128)(2,1)S(1)}, u32[]{:S(2)}, u32[]{:S(2)}) collective-permute-start(bf16[7,128,128]{2,1,0:T(8,128)(2,1)S(1)} %get-tuple-element.82), channel_id=1, source_target_pairs={{0,12},{1,13},{2,14},{3,15},{4,0},{5,1},{6,2},{7,3},{8,4},{9,5},{1... | collective-permute-start | bytes 688136 | tf_op jit(solution)/shard_map/ppermute | solution.py:355
  111.6 3.7 %collective-permute-done.7.refs_2_ = bf16[7,128,128]{2,1,0:T(8,128)(2,1)S(1)} collective-permute-done((bf16[7,128,128]{2,1,0:T(8,128)(2,1)S(1)}, bf16[7,128,128]{2,1,0:T(8,128)(2,1)S(1)}, u32[]{:S(2)}, u32[]{:S(2)}) %collective-permute-start.7) | collective-permute-done | bytes 229408 | tf_op jit(solution)/shard_map/ppermute | solution.py:355
  118.6 2.3 %collective-permute-start.12 = (bf16[7,32,128]{2,1,0:T(8,128)(2,1)S(1)}, bf16[7,32,128]{2,1,0:T(8,128)(2,1)S(1)}, u32[]{:S(2)}, u32[]{:S(2)}) collective-permute-start(bf16[7,32,128]{2,1,0:T(8,128)(2,1)S(1)} %get-tuple-element.84), channel_id=1, source_target_pairs={{0,4},{1,5},{2,6},{3,7},{4,8},{5,9},{6,10},{7,11},{8,12},{9,13},{1... | collective-permute-start | bytes 172040 | tf_op jit(solution)/shard_map/ppermute | solution.py:355
  126.5 4.3 %shard_map.146 = (bf16[1024,512]{1,0:T(8,128)(2,1)}, f32[512,512]{1,0:T(8,128)}) custom-call(bf16[1024,512]{1,0:T(8,128)(2,1)} %get-tuple-element.91.refs_0_, bf16[3584,512]{1,0:T(8,128)(2,1)} %refs_5_.3, bf16[512,512]{1,0:T(8,128)(2,1)} %get-tuple-element.92.refs_2_, bf16[3584,512]{1,0:T(8,128)(2,1)} %refs_5_.3, ...), custom_call_target="tpu_custom_call" | custom-call | flops 1073741824 | bytes 16252928 | tf_op jit(solution)/shard_map/pallas_call | solution.py:152
  133.3 11.2 %all-to-all-start.2 = ((bf16[16,32,256]{2,1,0:T(8,128)(2,1)}), bf16[16,32,256]{2,1,0:T(8,128)(2,1)S(1)}, u32[]{:S(2)}, u32[]{:S(2)}) async-start(bf16[16,32,256]{2,1,0:T(8,128)(2,1)} %shard_map.145), calls=%async_computation.2 | async-start | bytes 524288 | tf_op jit(solution)/shard_map/all_to_all | solution.py:441
  144.6 6.9 %collective-permute-start.19 = (bf16[64,512]{1,0:T(8,128)(2,1)S(1)}, bf16[64,512]{1,0:T(8,128)(2,1)S(1)}, u32[]{:S(2)}, u32[]{:S(2)}) collective-permute-start(bf16[64,512]{1,0:T(8,128)(2,1)S(1)} %copy-done.16), channel_id=1, source_target_pairs={{0,127},{1,0},{2,1},{3,2},{4,3},{5,4},{6,5},{7,6},{8,7},{9,8},{10,... | collective-permute-start | bytes 196616 | tf_op jit(solution)/shard_map/ppermute | solution.py:338
  151.5 4.2 %collective-permute-done.18.refs_3_ = bf16[64,512]{1,0:T(8,128)(2,1)S(1)} collective-permute-done((bf16[64,512]{1,0:T(8,128)(2,1)S(1)}, bf16[64,512]{1,0:T(8,128)(2,1)S(1)}, u32[]{:S(2)}, u32[]{:S(2)}) %collective-permute-start.18) | collective-permute-done | bytes 65568 | tf_op jit(solution)/shard_map/ppermute | solution.py:338
  156.3 3.2 %shard_map.147 = bf16[512,512]{1,0:T(8,128)(2,1)} custom-call(s32[1,1024]{1,0:T(1,128)} %get-tuple-element.61.refs_0_, s32[1,128]{1,0:T(1,128)} %refs_1_.5, f32[512,512]{1,0:T(8,128)} %get-tuple-element.96.refs_2_, bf16[64,512]{1,0:T(8,128)(2,1)} %copy-done.8, bf16[64,512]{1,0:T(8,128)(2,1)} %copy-done.9, bf16[1024,512]{1,0:T(8,128)(2,1)} %bitcast.17), custom_call_target="tpu_custom_call" | custom-call | flops 536870912 | bytes 2757120 | tf_op jit(solution)/shard_map/pallas_call | solution.py:152
  (71 shorter events, 19.8 us)
Async XLA Ops:
  3.7 14.4 %collective-permute-start = (bf16[1024,512]{1,0:T(8,128)(2,1)}, bf16[1024,512]{1,0:T(8,128)(2,1)}, u32[]{:S(2)}, u32[]{:S(2)}) collective-permute-start(bf16[1024,512]{1,0:T(8,128)(2,1)} %get-tuple-element.53), channel_id=1, source_target_pairs={{0,128},{128,0},{1,129},{129,1},{2,130},{130,2},{3,131},{131,3},{4... | collective-permute-start | bytes 3145736 | tf_op jit(solution)/shard_map/ppermute | solution.py:333
  7.0 11.1 %collective-permute-start.1 = (bf16[64,512]{1,0:T(8,128)(2,1)}, bf16[64,512]{1,0:T(8,128)(2,1)S(1)}, u32[]{:S(2)}, u32[]{:S(2)}) collective-permute-start(bf16[64,512]{1,0:T(8,128)(2,1)} %get-tuple-element.54), channel_id=1, source_target_pairs={{0,1},{1,2},{2,3},{3,4},{4,5},{5,6},{6,7},{7,8},{8,9},{9,10},{10,1... | collective-permute-start | bytes 196616 | tf_op jit(solution)/shard_map/ppermute | solution.py:338
  7.0 11.1 %collective-permute-start.2 = (bf16[64,512]{1,0:T(8,128)(2,1)}, bf16[64,512]{1,0:T(8,128)(2,1)S(1)}, u32[]{:S(2)}, u32[]{:S(2)}) collective-permute-start(bf16[64,512]{1,0:T(8,128)(2,1)} %get-tuple-element.55), channel_id=1, source_target_pairs={{0,127},{1,0},{2,1},{3,2},{4,3},{5,4},{6,5},{7,6},{8,7},{9,8},{10,... | collective-permute-start | bytes 196616 | tf_op jit(solution)/shard_map/ppermute | solution.py:338
  18.1 38.5 %all-to-all-start = ((bf16[128,8,512]{2,1,0:T(8,128)(2,1)}), bf16[128,8,512]{2,1,0:T(8,128)(2,1)S(1)}, u32[]{:S(2)}, u32[]{:S(2)}) async-start(bf16[128,8,512]{2,1,0:T(8,128)(2,1)} %bitcast.5), calls=%async_computation | async-start | bytes 2097152 | tf_op jit(solution)/shard_map/all_to_all | solution.py:345
  64.5 12.2 %collective-permute-start.4 = (bf16[1024,512]{1,0:T(8,128)(2,1)}, bf16[1024,512]{1,0:T(8,128)(2,1)}, u32[]{:S(2)}, u32[]{:S(2)}) collective-permute-start(bf16[1024,512]{1,0:T(8,128)(2,1)} %get-tuple-element.68), channel_id=1, source_target_pairs={{0,128},{128,0},{1,129},{129,1},{2,130},{130,2},{3,131},{131,3},{4... | collective-permute-start | bytes 3145736 | tf_op jit(solution)/shard_map/ppermute | solution.py:333
  76.6 6.3 %collective-permute-start.3 = (bf16[2,4,4,128,128]{4,3,2,1,0:T(8,128)(2,1)}, bf16[2,4,4,128,128]{4,3,2,1,0:T(8,128)(2,1)S(1)}, u32[]{:S(2)}, u32[]{:S(2)}) collective-permute-start(bf16[2,4,4,128,128]{4,3,2,1,0:T(8,128)(2,1)} %get-tuple-element.67), channel_id=1, source_target_pairs={{0,128},{128,0},{1,129},{129,1},{2,130},{130,2},{3,131},{131,3},{4... | collective-permute-start | bytes 3145736 | tf_op jit(solution)/shard_map/ppermute | solution.py:333
  76.7 56.6 %all-to-all-start.1 = ((bf16[128,8,512]{2,1,0:T(8,128)(2,1)}), bf16[128,8,512]{2,1,0:T(8,128)(2,1)S(1)}, u32[]{:S(2)}, u32[]{:S(2)}) async-start(bf16[128,8,512]{2,1,0:T(8,128)(2,1)} %bitcast.12), calls=%async_computation.1 | async-start | bytes 2097152 | tf_op jit(solution)/shard_map/all_to_all | solution.py:345
  93.5 2.7 %collective-permute-start.5 = (bf16[2,4,3,128,128]{4,3,2,1,0:T(8,128)(2,1)}, bf16[2,4,3,128,128]{4,3,2,1,0:T(8,128)(2,1)S(1)}, u32[]{:S(2)}, u32[]{:S(2)}) collective-permute-start(bf16[2,4,3,128,128]{4,3,2,1,0:T(8,128)(2,1)} %get-tuple-element.72), channel_id=1, source_target_pairs={{0,128},{128,0},{1,129},{129,1},{2,130},{130,2},{3,131},{131,3},{4... | collective-permute-start | bytes 2359304 | tf_op jit(solution)/shard_map/ppermute | solution.py:333
  97.7 11.4 %collective-permute-start.6 = (bf16[7,128,128]{2,1,0:T(8,128)(2,1)S(1)}, bf16[7,128,128]{2,1,0:T(8,128)(2,1)S(1)}, u32[]{:S(2)}, u32[]{:S(2)}) collective-permute-start(bf16[7,128,128]{2,1,0:T(8,128)(2,1)S(1)} %get-tuple-element.76), channel_id=1, source_target_pairs={{0,1},{1,2},{2,3},{3,0},{4,5},{5,6},{6,7},{7,4},{8,9},{9,10},{10,1... | collective-permute-start | bytes 688136 | tf_op jit(solution)/shard_map/ppermute | solution.py:355
  98.6 16.7 %collective-permute-start.7 = (bf16[7,128,128]{2,1,0:T(8,128)(2,1)S(1)}, bf16[7,128,128]{2,1,0:T(8,128)(2,1)S(1)}, u32[]{:S(2)}, u32[]{:S(2)}) collective-permute-start(bf16[7,128,128]{2,1,0:T(8,128)(2,1)S(1)} %get-tuple-element.77), channel_id=1, source_target_pairs={{0,2},{1,3},{2,0},{3,1},{4,6},{5,7},{6,4},{7,5},{8,10},{9,11},{10,... | collective-permute-start | bytes 688136 | tf_op jit(solution)/shard_map/ppermute | solution.py:355
  101.0 14.3 %collective-permute-start.8 = (bf16[7,128,128]{2,1,0:T(8,128)(2,1)S(1)}, bf16[7,128,128]{2,1,0:T(8,128)(2,1)S(1)}, u32[]{:S(2)}, u32[]{:S(2)}) collective-permute-start(bf16[7,128,128]{2,1,0:T(8,128)(2,1)S(1)} %get-tuple-element.78), channel_id=1, source_target_pairs={{0,3},{1,0},{2,1},{3,2},{4,7},{5,4},{6,5},{7,6},{8,11},{9,8},{10,9... | collective-permute-start | bytes 688136 | tf_op jit(solution)/shard_map/ppermute | solution.py:355
  102.2 13.1 %collective-permute-start.9 = (bf16[7,128,128]{2,1,0:T(8,128)(2,1)S(1)}, bf16[7,128,128]{2,1,0:T(8,128)(2,1)S(1)}, u32[]{:S(2)}, u32[]{:S(2)}) collective-permute-start(bf16[7,128,128]{2,1,0:T(8,128)(2,1)S(1)} %get-tuple-element.80), channel_id=1, source_target_pairs={{0,4},{1,5},{2,6},{3,7},{4,8},{5,9},{6,10},{7,11},{8,12},{9,13},{1... | collective-permute-start | bytes 688136 | tf_op jit(solution)/shard_map/ppermute | solution.py:355
  103.4 13.5 %collective-permute-start.10 = (bf16[7,128,128]{2,1,0:T(8,128)(2,1)S(1)}, bf16[7,128,128]{2,1,0:T(8,128)(2,1)S(1)}, u32[]{:S(2)}, u32[]{:S(2)}) collective-permute-start(bf16[7,128,128]{2,1,0:T(8,128)(2,1)S(1)} %get-tuple-element.81), channel_id=1, source_target_pairs={{0,8},{1,9},{2,10},{3,11},{4,12},{5,13},{6,14},{7,15},{8,0},{9,1},... | collective-permute-start | bytes 688136 | tf_op jit(solution)/shard_map/ppermute | solution.py:355
  109.1 8.1 %collective-permute-start.11 = (bf16[7,128,128]{2,1,0:T(8,128)(2,1)S(1)}, bf16[7,128,128]{2,1,0:T(8,128)(2,1)S(1)}, u32[]{:S(2)}, u32[]{:S(2)}) collective-permute-start(bf16[7,128,128]{2,1,0:T(8,128)(2,1)S(1)} %get-tuple-element.82), channel_id=1, source_target_pairs={{0,12},{1,13},{2,14},{3,15},{4,0},{5,1},{6,2},{7,3},{8,4},{9,5},{1... | collective-permute-start | bytes 688136 | tf_op jit(solution)/shard_map/ppermute | solution.py:355
  118.6 6.2 %collective-permute-start.12 = (bf16[7,32,128]{2,1,0:T(8,128)(2,1)S(1)}, bf16[7,32,128]{2,1,0:T(8,128)(2,1)S(1)}, u32[]{:S(2)}, u32[]{:S(2)}) collective-permute-start(bf16[7,32,128]{2,1,0:T(8,128)(2,1)S(1)} %get-tuple-element.84), channel_id=1, source_target_pairs={{0,4},{1,5},{2,6},{3,7},{4,8},{5,9},{6,10},{7,11},{8,12},{9,13},{1... | collective-permute-start | bytes 172040 | tf_op jit(solution)/shard_map/ppermute | solution.py:355
  121.0 9.8 %collective-permute-start.13 = (bf16[7,32,128]{2,1,0:T(8,128)(2,1)S(1)}, bf16[7,32,128]{2,1,0:T(8,128)(2,1)S(1)}, u32[]{:S(2)}, u32[]{:S(2)}) collective-permute-start(bf16[7,32,128]{2,1,0:T(8,128)(2,1)S(1)} %get-tuple-element.85), channel_id=1, source_target_pairs={{0,8},{1,9},{2,10},{3,11},{4,12},{5,13},{6,14},{7,15},{8,0},{9,1},... | collective-permute-start | bytes 172040 | tf_op jit(solution)/shard_map/ppermute | solution.py:355
  122.8 8.0 %collective-permute-start.14 = (bf16[7,32,128]{2,1,0:T(8,128)(2,1)S(1)}, bf16[7,32,128]{2,1,0:T(8,128)(2,1)S(1)}, u32[]{:S(2)}, u32[]{:S(2)}) collective-permute-start(bf16[7,32,128]{2,1,0:T(8,128)(2,1)S(1)} %get-tuple-element.86), channel_id=1, source_target_pairs={{0,12},{1,13},{2,14},{3,15},{4,0},{5,1},{6,2},{7,3},{8,4},{9,5},{1... | collective-permute-start | bytes 172040 | tf_op jit(solution)/shard_map/ppermute | solution.py:355
  123.4 7.5 %collective-permute-start.15 = (bf16[7,32,128]{2,1,0:T(8,128)(2,1)S(1)}, bf16[7,32,128]{2,1,0:T(8,128)(2,1)S(1)}, u32[]{:S(2)}, u32[]{:S(2)}) collective-permute-start(bf16[7,32,128]{2,1,0:T(8,128)(2,1)S(1)} %get-tuple-element.88), channel_id=1, source_target_pairs={{0,1},{1,2},{2,3},{3,0},{4,5},{5,6},{6,7},{7,4},{8,9},{9,10},{10,1... | collective-permute-start | bytes 172040 | tf_op jit(solution)/shard_map/ppermute | solution.py:355
  124.1 6.8 %collective-permute-start.16 = (bf16[7,32,128]{2,1,0:T(8,128)(2,1)S(1)}, bf16[7,32,128]{2,1,0:T(8,128)(2,1)S(1)}, u32[]{:S(2)}, u32[]{:S(2)}) collective-permute-start(bf16[7,32,128]{2,1,0:T(8,128)(2,1)S(1)} %get-tuple-element.89), channel_id=1, source_target_pairs={{0,2},{1,3},{2,0},{3,1},{4,6},{5,7},{6,4},{7,5},{8,10},{9,11},{10,... | collective-permute-start | bytes 172040 | tf_op jit(solution)/shard_map/ppermute | solution.py:355
  124.8 6.1 %collective-permute-start.17 = (bf16[7,32,128]{2,1,0:T(8,128)(2,1)S(1)}, bf16[7,32,128]{2,1,0:T(8,128)(2,1)S(1)}, u32[]{:S(2)}, u32[]{:S(2)}) collective-permute-start(bf16[7,32,128]{2,1,0:T(8,128)(2,1)S(1)} %get-tuple-element.90), channel_id=1, source_target_pairs={{0,3},{1,0},{2,1},{3,2},{4,7},{5,4},{6,5},{7,6},{8,11},{9,8},{10,9... | collective-permute-start | bytes 172040 | tf_op jit(solution)/shard_map/ppermute | solution.py:355
  133.3 22.4 %copy-start.5 = (bf16[128,8,512]{2,1,0:T(8,128)(2,1)}, bf16[128,8,512]{2,1,0:T(8,128)(2,1)S(1)}, u32[]{:S(2)}) copy-start(bf16[128,8,512]{2,1,0:T(8,128)(2,1)S(1)} %all-to-all-done.1) | copy-start | bytes 3145732
  133.3 26.3 %all-to-all-start.2 = ((bf16[16,32,256]{2,1,0:T(8,128)(2,1)}), bf16[16,32,256]{2,1,0:T(8,128)(2,1)S(1)}, u32[]{:S(2)}, u32[]{:S(2)}) async-start(bf16[16,32,256]{2,1,0:T(8,128)(2,1)} %shard_map.145), calls=%async_computation.2 | async-start | bytes 524288 | tf_op jit(solution)/shard_map/all_to_all | solution.py:441
  144.5 11.2 %collective-permute-start.18 = (bf16[64,512]{1,0:T(8,128)(2,1)S(1)}, bf16[64,512]{1,0:T(8,128)(2,1)S(1)}, u32[]{:S(2)}, u32[]{:S(2)}) collective-permute-start(bf16[64,512]{1,0:T(8,128)(2,1)S(1)} %copy-done.17), channel_id=1, source_target_pairs={{0,1},{1,2},{2,3},{3,4},{4,5},{5,6},{6,7},{7,8},{8,9},{9,10},{10,1... | collective-permute-start | bytes 196616 | tf_op jit(solution)/shard_map/ppermute | solution.py:338
  144.6 11.1 %collective-permute-start.19 = (bf16[64,512]{1,0:T(8,128)(2,1)S(1)}, bf16[64,512]{1,0:T(8,128)(2,1)S(1)}, u32[]{:S(2)}, u32[]{:S(2)}) collective-permute-start(bf16[64,512]{1,0:T(8,128)(2,1)S(1)} %copy-done.16), channel_id=1, source_target_pairs={{0,127},{1,0},{2,1},{3,2},{4,3},{5,4},{6,5},{7,6},{8,7},{9,8},{10,... | collective-permute-start | bytes 196616 | tf_op jit(solution)/shard_map/ppermute | solution.py:338
  (17 other events, 85.0 us)

commit v5 on v4

--- a/solution.py
+++ b/solution.py
@@ -214,94 +214,85 @@
         msg_ref[r] = dot(agg, second_ref[...])
 
 
-def node_kernel(
-    target_ref, margin_ref, recv_ref, msg_ref, nodes_ref, a_ref, b_ref, cot_ref, second_ref,
-    new_ref, pooled_ref, hid_ref, gpre_ref, gpool_ref, part_ref, ret_ref,
+def put(ref, index, value, first):
+    half = value.shape[1] // 2
+    lane = half // 2
+    step = value.shape[0] // RING
+    fine = step // RING
+    own = jnp.where(first, value[:, :half], value[:, half:]).astype(BF)
+    send = jnp.where(first, value[:, half:], value[:, :half]).astype(BF)
+    for buffer, part in ((ref.own, own), (ref.send, send)):
+        for i in range(RING):
+            buffer[index, 0, i] = part[i * step : (i + 1) * step, :lane]
+            for j in range(RING):
+                start = i * step + j * fine
+                buffer[index, 1, j, i * fine : (i + 1) * fine] = part[start : start + fine, lane:]
+
+
+class Blocks:
+    def __init__(self, own, send):
+        self.own, self.send = own, send
+
+
+def core_kernel(
+    side_ref, target_ref, margin_ref, recv_ref, msg_ref, nodes_ref, na_ref, nb_ref, cot_ref, nsec_ref,
+    dst_ref, esec_ref, slope_ref, agg_ref, edges_ref, src_ref, low_ref, high_ref, wa_ref,
+    send_ref, ret_ref, own_ref, new_ref, part_ref, gedge_ref, bysrc_ref, bydst_ref, glow_ref, ghigh_ref,
+    pooled_ref, hid_ref, gnode_ref, gpool_ref, turned_ref,
+    *, patches, scale
 ):
     count, width = nodes_ref.shape
+    inner = edges_ref.shape[0] - edges_ref.shape[0] // 4
+    depth = low_ref.shape[0]
+    first = side_ref[0] == 0
     target, margin = target_ref[...], margin_ref[...]
     for r in tiles(count):
         coupled = dot(pick_t(target, r.start, TILE, margin), recv_ref[...])
         pooled = (msg_ref[r] + coupled).astype(BF)
         pooled_ref[r] = pooled
         nodes = nodes_ref[r]
-        pre = dot(nodes, a_ref[...]) + dot(pooled, b_ref[...])
+        pre = dot(nodes, na_ref[...]) + dot(pooled, nb_ref[...])
         sigma = jax.nn.sigmoid(pre)
         hidden = (pre * sigma).astype(BF)
         hid_ref[r] = hidden
         slope = sigma * (1.0 + pre * (1.0 - sigma))
-        cot = cot_ref[r]
-        gpre = (dot_nt(cot, second_ref[...]) * slope).astype(BF)
-        gpre_ref[r] = gpre
-        gpool_ref[r] = dot_nt(gpre, b_ref[...]).astype(BF)
-        new_ref[r] = (nodes.astype(F32) + dot(hidden, second_ref[...])).astype(BF)
-        part_ref[r] = cot.astype(F32) + dot_nt(gpre, a_ref[...])
-    flush(new_ref, pooled_ref, hid_ref, gpre_ref, gpool_ref, part_ref)
+        gnode = (dot_nt(cot_ref[r], nsec_ref[...]) * slope).astype(BF)
+        gnode_ref[r] = gnode
+        gpool_ref[r] = dot_nt(gnode, nb_ref[...]).astype(BF)
+        new_ref[r] = (nodes.astype(F32) + dot(hidden, nsec_ref[...])).astype(BF)
+        part_ref[r] = cot_ref[r].astype(F32) + dot_nt(gnode, na_ref[...])
+    flush(new_ref, part_ref)
+    gpool = gpool_ref[...]
     col, weight = column(target), column(margin)
-    gpool = gpool_ref[...]
     for r in tiles(recv_ref.shape[0]):
         ret_ref[r] = dot(pick(col[r], count, weight[r]), gpool).astype(BF)
-
-
-def put(own_ref, send_ref, index, value, first):
-    half = value.shape[1] // 2
-    lane = half // 2
-    step = value.shape[0] // RING
-    fine = step // RING
-    own = jnp.where(first, value[:, :half], value[:, half:]).astype(BF)
-    send = jnp.where(first, value[:, half:], value[:, :half]).astype(BF)
-    for ref, part in ((own_ref, own), (send_ref, send)):
-        for i in range(RING):
-            ref[0, i, index] = part[i * step : (i + 1) * step, :lane]
-            for j in range(RING):
-                start = i * step + j * fine
-                ref[1, j, index, i * fine : (i + 1) * fine] = part[start : start + fine, lane:]
-
-
-def node_grad_kernel(
-    side_ref, agg_ref, gpool_ref, nodes_ref, gpre_ref, pooled_ref, hid_ref, cot_ref, own_ref, send_ref,
-    *, patches, scale
-):
-    order = row_order(side_ref[1], nodes_ref.shape[1], patches)
-    first = side_ref[0] == 0
-    pairs = [(agg_ref, gpool_ref), (nodes_ref, gpre_ref), (pooled_ref, gpre_ref), (hid_ref, cot_ref)]
-    for index, (left, right) in enumerate(pairs):
-        turned = dot_nt(order, left[...]).astype(BF)
-        put(own_ref, send_ref, index, dot(turned, right[...]) * scale, first)
-
-
-def edge_grad_kernel(
-    side_ref, dst_ref, gpool_ref, second_ref, slope_ref, edges_ref, src_ref, nodes_ref, low_ref, high_ref, wa_ref,
-    own_ref, send_ref, gpre_ref, bysrc_ref, bydst_ref, glow_ref, ghigh_ref,
-    *, patches, scale
-):
-    count, width = nodes_ref.shape
-    inner = edges_ref.shape[0] - edges_ref.shape[0] // 4
-    depth = low_ref.shape[0]
-    first = side_ref[0] == 0
-    gpool = gpool_ref[...]
-    second = second_ref[...]
+    flush(ret_ref)
     dst_row, src_row = dst_ref[...], src_ref[...]
     dst = column(dst_row)
     for r in tiles(edges_ref.shape[0]):
         message = dot(pick(dst[r], count), gpool).astype(BF)
-        gpre_ref[r] = (dot_nt(message, second) * slope_ref[r].astype(F32)).astype(BF)
-    flush(gpre_ref)
-    order = row_order(side_ref[1], width, patches)
-    turned = dot_nt(order, edges_ref[...]).astype(BF)
-    put(own_ref, send_ref, 2, dot(turned, gpre_ref[...]) * scale, first)
+        gedge_ref[r] = (dot_nt(message, esec_ref[...]) * slope_ref[r].astype(F32)).astype(BF)
+    flush(gedge_ref)
     for r in tiles(count):
-        bydst_ref[r] = dot(pick_t(dst_row, r.start, TILE), gpre_ref[...]).astype(BF)
-        bysrc_ref[r] = dot(pick_t(src_row[:, :inner], r.start, TILE), gpre_ref[:inner]).astype(BF)
+        bydst_ref[r] = dot(pick_t(dst_row, r.start, TILE), gedge_ref[...]).astype(BF)
+        bysrc_ref[r] = dot(pick_t(src_row[:, :inner], r.start, TILE), gedge_ref[:inner]).astype(BF)
     flush(bysrc_ref, bydst_ref)
-    halo = dot(pick_t(src_row[:, inner:], count, 2 * depth), gpre_ref[inner:]).astype(BF)
-    turned = dot_nt(order, nodes_ref[...]).astype(BF)
-    put(own_ref, send_ref, 1, dot(turned, bydst_ref[...]) * scale, first)
-    rim = dot_nt(order, jnp.concatenate([low_ref[...], high_ref[...]], axis=0)).astype(BF)
-    put(own_ref, send_ref, 0, (dot(turned, bysrc_ref[...]) + dot(rim, halo)) * scale, first)
+    halo = dot(pick_t(src_row[:, inner:], count, 2 * depth), gedge_ref[inner:]).astype(BF)
     back = dot_nt(halo, wa_ref[...]).astype(BF)
     glow_ref[...] = back[:depth]
     ghigh_ref[...] = back[depth:]
+    flush(glow_ref, ghigh_ref)
+    order = row_order(side_ref[1], width, patches)
+    blocks = Blocks(own_ref, send_ref)
+    turned_ref[...] = dot_nt(order, nodes_ref[...]).astype(BF)
+    rim = dot_nt(order, jnp.concatenate([low_ref[...], high_ref[...]], axis=0)).astype(BF)
+    put(blocks, 0, (dot(turned_ref[...], bysrc_ref[...]) + dot(rim, halo)) * scale, first)
+    put(blocks, 1, dot(turned_ref[...], bydst_ref[...]) * scale, first)
+    put(blocks, 4, dot(turned_ref[...], gnode_ref[...]) * scale, first)
+    pairs = ((2, edges_ref, gedge_ref), (3, agg_ref, gpool_ref), (5, pooled_ref, gnode_ref), (6, hid_ref, cot_ref))
+    for index, left, right in pairs:
+        turned = dot_nt(order, left[...]).astype(BF)
+        put(blocks, index, dot(turned, right[...]) * scale, first)
 
 
 def edge_rest_kernel(
@@ -355,15 +346,10 @@
     return lax.ppermute(value, "patch", pairs)
 
 
-def join_kernel(own_a, other_a, own_b, other_b, *outs):
+def join_kernel(own_ref, other_ref, *outs):
     for index, out in enumerate(outs):
         c, d = index // RING, index % RING
-        base = 0
-        for own, other in ((own_a, other_a), (own_b, other_b)):
-            blocks = own.shape[2]
-            joined = own[c, d].astype(F32) + other[c, d].astype(F32)
-            out[base : base + blocks] = joined.astype(BF)
-            base += blocks
+        out[...] = (own_ref[:, c, d].astype(F32) + other_ref[:, c, d].astype(F32)).astype(BF)
 
 
 def total_of(refs):
@@ -381,8 +367,8 @@
             refs[(2 + c) * RING + d][...] = total[:, d * fine : (d + 1) * fine].astype(BF)
 
 
-def depth_kernel(*refs):
-    ins, (out, hold) = refs[: 2 * RING], refs[2 * RING :]
+def depth_kernel(place_ref, *refs):
+    ins, (keep_ref, send_ref, hold) = refs[: 2 * RING], refs[2 * RING :]
     depth = hold.shape[0]
     hold[...] = jnp.zeros(hold.shape, F32)
     for c in range(2):
@@ -394,55 +380,69 @@
                 hold[d, block * fine : (block + 1) * fine, c * lane : (c + 1) * lane] = total[
                     block, d * fine : (d + 1) * fine
                 ]
-    value = hold[...].astype(BF)
-    out[:depth] = value
-    out[depth:] = value
-
-
-def finish_kernel(in_ref, out_ref):
-    count, _, lane = in_ref.shape
-    depth = count // 2
-    for side in range(2):
-        total = in_ref[side * depth].astype(F32)
-        for d in range(1, depth):
-            total = total + in_ref[side * depth + d].astype(F32)
-        out_ref[:, side * lane : (side + 1) * lane] = total[: out_ref.shape[0]]
-
-
-def weight_sums(own_a, other_a, own_b, other_b, couple_back, total):
+    even = (place_ref[1] // PLANE) % 2 == 0
+    for j in range(depth // 2):
+        low, high = hold[2 * j], hold[2 * j + 1]
+        keep_ref[j] = jnp.where(even, low, high)
+        send_ref[j] = jnp.where(even, high, low).astype(BF)
+
+
+def pair_kernel(place_ref, keep_ref, other_ref, *outs):
+    mine = place_ref[1] // PLANE // 2
+    for d, out in enumerate(outs):
+        j = (mine + d) % len(outs)
+        out[...] = keep_ref[j] + other_ref[j].astype(F32)
+
+
+def small_call(kernel, place, args, outs, scratch=()):
+    return pl.pallas_call(
+        kernel,
+        out_shape=tuple(outs),
+        in_specs=[SMEM] + [VMEM] * len(args),
+        out_specs=tuple([VMEM] * len(outs)),
+        scratch_shapes=list(scratch),
+        compiler_params=pltpu.CompilerParams(vmem_limit_bytes=14 * 2**20),
+        cost_estimate=cost(list(args) + list(outs), 0),
+    )(place, *args)
+
+
+def spread(pieces, axes):
+    return [
+        pieces[c * RING + d] if d == 0 else hop(pieces[c * RING + d], **{axis: d})
+        for c, axis in enumerate(axes)
+        for d in range(RING)
+    ]
+
+
+def weight_sums(own, other, place, tied):
     patches = lax.axis_size("patch")
     depth = patches // PLANE
-    rows, lane = own_a.shape[3:]
-    blocks = own_a.shape[2] + own_b.shape[2]
+    blocks, _, _, rows, lane = own.shape
     fine = rows // RING // depth
-    piece = shape(BF, blocks, rows, lane)
-    small = shape(BF, blocks, rows // RING, lane)
-    pieces = call(join_kernel, (own_a, other_a, own_b, other_b), (piece,) * (2 * RING))
-    for kernel, axes in ((plane_kernel, ("dx", "dy")), (None, ("dy", "dx"))):
-        pieces = [
-            pieces[c * RING + d] if d == 0 else hop(pieces[c * RING + d], **{axis: d})
-            for c, axis in enumerate(axes)
-            for d in range(RING)
-        ]
-        if kernel is not None:
-            pieces = call(kernel, pieces, (small,) * (2 * RING))
+    pieces = call(join_kernel, (own, other), (shape(BF, blocks, rows, lane),) * (2 * RING))
+    pieces = spread(pieces, ("dx", "dy"))
+    pieces[1], tied = lax.optimization_barrier((pieces[1], tied))
+    pieces = call(plane_kernel, pieces, (shape(BF, blocks, rows // RING, lane),) * (2 * RING))
+    pieces = spread(pieces, ("dy", "dx"))
     padded = (blocks * fine + 15) // 16 * 16
-    (part,) = pl.pallas_call(
+    half = depth // 2
+    keep, send = small_call(
         depth_kernel,
-        out_shape=(shape(BF, 2 * depth, padded, 2 * lane),),
-        in_specs=[VMEM] * len(pieces),
-        out_specs=(VMEM,),
-        scratch_shapes=[pltpu.VMEM((depth, padded, 2 * lane), F32)],
-    )(*pieces)
-    part, couple_back, total = lax.optimization_barrier((part, couple_back, total))
-    columns = [
-        [m * patches + z * PLANE + i for m in range(2) for z in range(depth)] for i in range(PLANE)
-    ]
-    both = lax.all_to_all(
-        part, ("mesh", "patch"), split_axis=0, concat_axis=0, axis_index_groups=columns, tiled=True
-    )
-    (result,) = call(finish_kernel, (both,), (shape(F32, blocks * fine, 4 * lane),))
-    return result.reshape(blocks, fine * 4 * lane), couple_back, total
+        place,
+        pieces,
+        (shape(F32, half, padded, 2 * lane), shape(BF, half, padded, 2 * lane)),
+        scratch=(pltpu.VMEM((depth, padded, 2 * lane), F32),),
+    )
+    pairs = [(p, (p // PLANE ^ 1) * PLANE + p % PLANE) for p in range(patches)]
+    other = lax.ppermute(send, "patch", pairs)
+    pieces = small_call(pair_kernel, place, (keep, other), (shape(F32, padded, 2 * lane),) * half)
+    own = pieces[0]
+    for d in range(1, half):
+        own = own + hop(pieces[d], dz=2 * d)
+    other = from_partner(own)
+    first = lax.axis_index("mesh") == 0
+    both = jnp.concatenate([jnp.where(first, own, other), jnp.where(first, other, own)], axis=1)
+    return both[: blocks * fine].reshape(blocks, fine * 4 * lane), tied
 
 
 def shards(
@@ -498,44 +498,33 @@
         flops=edge_count * 6 * unit,
     )
     square = shape(BF, count, width)
-    new_nodes, pooled, hidden, grad_pre, grad_pooled, part, returned = stream(
-        node_kernel,
-        (target, margin, received, message, nodes_own, weight(4), weight(5), cotangent, weight(6)),
-        (square, square, square, square, square, shape(F32, count, width), shape(BF, slots, width)),
-        flops=count * 10 * unit,
-    )
+    grads = shape(BF, 7, 2, RING, width // RING, width // 4)
+    rim = shape(BF, depth, width)
+    slot_block = shape(BF, slots, width)
+    edge_block = shape(BF, edge_count, width)
+    total = shape(F32, count, width)
+    send, returned, own, new_nodes, part, grad_edge_pre, by_source, by_target, grad_low, grad_high = stream(
+        lambda *refs: core_kernel(*refs, patches=patches, scale=scale),
+        (
+            side, target, margin, received, message, nodes_own, weight(4), weight(5), cotangent,
+            weight(6), edge_dst, weight(3), slope, agg, edges_own, edge_src, low, high, weight(0),
+        ),
+        (grads, slot_block, grads, square, total, edge_block, square, square, rim, rim),
+        scratch=[pltpu.VMEM((count, width), BF)] * 5,
+        flops=edge_count * 18 * unit,
+    )
+    other = from_partner(send)
     crossed_back = from_partner(returned)
+    back_low, back_high = shift(grad_high, 1), shift(grad_low, -1)
+    summed, tied = weight_sums(own, other, side, (crossed_back, back_low, back_high))
+    crossed_back, back_low, back_high = tied
     couple_back = route(crossed_back)
-    grad_shape = lambda blocks: shape(BF, 2, RING, blocks, width // RING, width // 4)
-    own_b, send_b = stream(
-        lambda *refs: node_grad_kernel(*refs, patches=patches, scale=scale),
-        (side, agg, grad_pooled, nodes_own, grad_pre, pooled, hidden, cotangent),
-        (grad_shape(4), grad_shape(4)),
-        flops=count * 8 * unit,
-    )
-    other_b = from_partner(send_b)
-    grad_pooled, other_b, crossed_back = lax.optimization_barrier((grad_pooled, other_b, crossed_back))
-    own_a, send_a, grad_edge_pre, by_source, by_target, grad_low, grad_high = stream(
-        lambda *refs: edge_grad_kernel(*refs, patches=patches, scale=scale),
-        (
-            side, edge_dst, grad_pooled, weight(3), slope, edges_own, edge_src, nodes_own, low, high,
-            weight(0),
-        ),
-        (
-            grad_shape(3), grad_shape(3), shape(BF, edge_count, width), square, square,
-            shape(BF, depth, width), shape(BF, depth, width),
-        ),
-        flops=edge_count * 8 * unit,
-    )
     edge_grads, total = stream(
         edge_rest_kernel,
         (grad_edge_pre, weight(2), by_source, weight(0), by_target, weight(1), part),
-        (shape(BF, edge_count, width), shape(F32, count, width)),
+        (edge_block, total),
         flops=edge_count * 2 * unit,
     )
-    back_low, back_high = shift(grad_high, 1), shift(grad_low, -1)
-    other_a = from_partner(send_a)
-    summed, couple_back, total = weight_sums(own_a, other_a, own_b, other_b, couple_back, total)
     (node_grads,) = stream(
         last_kernel,
         (live, halo_rows, total, back_low, back_high, couple_back),

time: 161 us -> 170 us (1.056)
  waiting for transfers between devices: 38.6 us -> 48.6 us
  Pallas kernels: 43.9 us -> 35.8 us
  starting transfers between devices: 70.9 us -> 78.7 us
    all_to_all x1 -> x0, starting transfers between devices: 11.2 us -> none  [weight_sums(): lax.all_to_all(part, ('mesh', 'patch'), split_axis=0, concat_axis=0, axis...]
    ppermute x12 -> x15, waiting for transfers between devices: 8.87 us -> 18.7 us  [hop(): return lax.ppermute(value, 'patch', pairs)]
    pallas_call x7 -> x5, Pallas kernels: 41.4 us -> 33.9 us  [stream(): pl.pallas_call(body, out_shape=tuple(outs), in_specs=[hbm if isinstance(a...]
    ppermute x12 -> x15, starting transfers between devices: 18.4 us -> 25.6 us  [hop(): return lax.ppermute(value, 'patch', pairs)]
    ppermute x4, starting transfers between devices: 8.81 us -> 15 us  [from_partner(): return lax.ppermute(value, 'mesh', [(0, 1), (1, 0)])]
    all_to_all x2, starting transfers between devices: 17.1 us -> 21.6 us  [route(): lax.all_to_all(crossed, 'patch', split_axis=0, concat_axis=0, tiled=True)]
    ppermute x4, waiting for transfers between devices: 6.76 us -> 4.23 us  [shift(): lax.ppermute(value, 'patch', [(i, (i + step) % count) for i in range(coun...]
    ppermute x0 -> x1, waiting for transfers between devices: none -> 2.1 us  [weight_sums(): other = lax.ppermute(send, 'patch', pairs)]
  transfers between devices with their start and end apart: 23 -> 26, of which waited for: 8 -> 13; matrix products, arithmetic and copies ran while one was open for 0% -> 1% of each run, Pallas kernels for 21% -> 8%
where the time goes in v5:
time: 170 us
  starting transfers between devices  78.7 us (46%)
  waiting for transfers between devices  48.6 us (29%)
  Pallas kernels  35.8 us (21%)
  local copies, waits for them, and re-layouts  5.19 us (3%)
    pallas_call x5, Pallas kernels, stream(): pl.pallas_call(body, out_shape=tuple(outs), in_specs=[hbm if isinstance(a...  33.9 us
    ppermute x15, starting transfers between devices, hop(): return lax.ppermute(value, 'patch', pairs)  25.6 us
    all_to_all x2, starting transfers between devices, route(): lax.all_to_all(crossed, 'patch', split_axis=0, concat_axis=0, tiled=True)  21.6 us
    all_to_all x2, waiting for transfers between devices, route(): lax.all_to_all(crossed, 'patch', split_axis=0, concat_axis=0, tiled=True)  20 us
    ppermute x15, waiting for transfers between devices, hop(): return lax.ppermute(value, 'patch', pairs)  18.7 us
    ppermute x4, starting transfers between devices, shift(): lax.ppermute(value, 'patch', [(i, (i + step) % count) for i in range(coun...  15.4 us
    ppermute x4, starting transfers between devices, from_partner(): return lax.ppermute(value, 'mesh', [(0, 1), (1, 0)])  15 us
    unnamed x22, local copies, waits for them, and re-layouts  4.53 us
  transfers between devices with their start and end apart: 26, of which 13 were waited for; matrix products, arithmetic and copies ran while one was open for 1% of the time, Pallas kernels for 8%

profile of v5, /device:TPU:1, one launch (start us, length us, event | category | flops | bytes accessed | tf_op | source)
XLA Modules:
  0.0 169.9 jit_solution(5742725860222589196)
XLA Ops:
  0.6 3.0 %shard_map.138 = (bf16[1024,512]{1,0:T(8,128)(2,1)}, bf16[64,512]{1,0:T(8,128)(2,1)}, bf16[64,512]{1,0:T(8,128)(2,1)}, s32[1,1024]{1,0:T(1,128)}) custom-call(s32[1,1024]{1,0:T(1,128)} %bitcast.27, s32[1,128]{1,0:T(1,128)} %bitcast.30, s32[1,128]{1,0:T(1,128)} %refs_1_.3, bf16[512,512]{1,0:T(8,128)(2,1)} %bitcast.21), custom_call_target="tpu_custom_call" | custom-call | flops 603979776 | bytes 1713152 | tf_op jit(solution)/shard_map/pallas_call | solution.py:152
  3.7 3.3 %collective-permute-start = (bf16[1024,512]{1,0:T(8,128)(2,1)}, bf16[1024,512]{1,0:T(8,128)(2,1)}, u32[]{:S(2)}, u32[]{:S(2)}) collective-permute-start(bf16[1024,512]{1,0:T(8,128)(2,1)} %get-tuple-element.52), channel_id=1, source_target_pairs={{0,128},{128,0},{1,129},{129,1},{2,130},{130,2},{3,131},{131,3},{4... | collective-permute-start | bytes 3145736 | tf_op jit(solution)/shard_map/ppermute | solution.py:324
  7.0 8.5 %collective-permute-start.2 = (bf16[64,512]{1,0:T(8,128)(2,1)}, bf16[64,512]{1,0:T(8,128)(2,1)S(1)}, u32[]{:S(2)}, u32[]{:S(2)}) collective-permute-start(bf16[64,512]{1,0:T(8,128)(2,1)} %get-tuple-element.54), channel_id=1, source_target_pairs={{0,127},{1,0},{2,1},{3,2},{4,3},{5,4},{6,5},{7,6},{8,7},{9,8},{10,... | collective-permute-start | bytes 196616 | tf_op jit(solution)/shard_map/ppermute | solution.py:329
  15.5 2.6 %collective-permute-done.1.refs_4_.refs_16_ = bf16[64,512]{1,0:T(8,128)(2,1)S(1)} collective-permute-done((bf16[64,512]{1,0:T(8,128)(2,1)}, bf16[64,512]{1,0:T(8,128)(2,1)S(1)}, u32[]{:S(2)}, u32[]{:S(2)}) %collective-permute-start.1) | collective-permute-done | bytes 65568 | tf_op jit(solution)/shard_map/ppermute | solution.py:329
  18.1 11.1 %all-to-all-start = ((bf16[128,8,512]{2,1,0:T(8,128)(2,1)}), bf16[128,8,512]{2,1,0:T(8,128)(2,1)S(1)}, u32[]{:S(2)}, u32[]{:S(2)}) async-start(bf16[128,8,512]{2,1,0:T(8,128)(2,1)} %bitcast.7), calls=%async_computation | async-start | bytes 2097152 | tf_op jit(solution)/shard_map/all_to_all | solution.py:336
  29.8 6.9 %shard_map.139 = (bf16[1024,512]{1,0:T(8,128)(2,1)}, bf16[512,512]{1,0:T(8,128)(2,1)}, f32[512,512]{1,0:T(8,128)}) custom-call(s32[1,1024]{1,0:T(1,128)} %refs_10_.1, bf16[512,512]{1,0:T(8,128)(2,1)} %bitcast.22, bf16[3584,512]{1,0:T(8,128)(2,1)} %refs_5_.1, s32[1,1024]{1,0:T(1,128)} %refs_15_.1, bf16[64,512]{1,0:T(8,128)(2,1)} %copy-done.5, ...), custom_call_target="tpu_custom_call" | custom-call | flops 3221225472 | bytes 19013632 | tf_op jit(solution)/shard_map/pallas_call | solution.py:152
  36.7 20.0 %all-to-all-done = bf16[128,8,512]{2,1,0:T(8,128)(2,1)S(1)} async-done(((bf16[128,8,512]{2,1,0:T(8,128)(2,1)}), bf16[128,8,512]{2,1,0:T(8,128)(2,1)S(1)}, u32[]{:S(2)}, u32[]{:S(2)}) %all-to-all-start) | async-done | bytes 1048608 | tf_op jit(solution)/shard_map/all_to_all | solution.py:336
  57.6 16.5 %shard_map.140 = (bf16[7,2,4,128,128]{4,3,2,1,0:T(8,128)(2,1)}, bf16[1024,512]{1,0:T(8,128)(2,1)}, bf16[7,2,4,128,128]{4,3,2,1,0:T(8,128)(2,1)}, bf16[512,512]{1...) custom-call(s32[2]{0:T(128)} %pad_add_fusion.refs_0_.place_ref, ...), custom_call_target="tpu_custom_call" | custom-call | flops 9663676416 | bytes 32784392 | tf_op jit(solution)/shard_map/pallas_call | solution.py:152
  74.1 4.7 %collective-permute-start.3 = (bf16[7,2,4,128,128]{4,3,2,1,0:T(8,128)(2,1)}, bf16[7,2,4,128,128]{4,3,2,1,0:T(8,128)(2,1)S(1)}, u32[]{:S(2)}, u32[]{:S(2)}) collective-permute-start(bf16[7,2,4,128,128]{4,3,2,1,0:T(8,128)(2,1)} %get-tuple-element.69), channel_id=1, source_target_pairs={{0,128},{128,0},{1,129},{129,1},{2,130},{130,2},{3,131},{131,3},{4... | collective-permute-start | bytes 5505032 | tf_op jit(solution)/shard_map/ppermute | solution.py:324
  78.8 3.5 %collective-permute-done.3.other_ref = bf16[7,2,4,128,128]{4,3,2,1,0:T(8,128)(2,1)S(1)} collective-permute-done((bf16[7,2,4,128,128]{4,3,2,1,0:T(8,128)(2,1)}, bf16[7,2,4,128,128]{4,3,2,1,0:T(8,128)(2,1)S(1)}, u32[]{:S(2)}, u32[]{:S(2)}) %collective-permute-start.3) | collective-permute-done | bytes 1835040 | tf_op jit(solution)/shard_map/ppermute | solution.py:324
  85.0 6.6 %collective-permute-start.7 = (bf16[64,512]{1,0:T(8,128)(2,1)S(1)}, bf16[64,512]{1,0:T(8,128)(2,1)S(1)}, u32[]{:S(2)}, u32[]{:S(2)}) collective-permute-start(bf16[64,512]{1,0:T(8,128)(2,1)S(1)} %copy-done.9), channel_id=1, source_target_pairs={{0,127},{1,0},{2,1},{3,2},{4,3},{5,4},{6,5},{7,6},{8,7},{9,8},{10,... | collective-permute-start | bytes 196616 | tf_op jit(solution)/shard_map/ppermute | solution.py:329
  94.3 10.5 %all-to-all-start.1 = ((bf16[128,8,512]{2,1,0:T(8,128)(2,1)}), bf16[128,8,512]{2,1,0:T(8,128)(2,1)S(1)}, u32[]{:S(2)}, u32[]{:S(2)}) async-start(bf16[128,8,512]{2,1,0:T(8,128)(2,1)} %bitcast.19), calls=%async_computation.1 | async-start | bytes 2097152 | tf_op jit(solution)/shard_map/all_to_all | solution.py:336
  104.8 2.2 %collective-permute-start.8 = (bf16[7,128,128]{2,1,0:T(8,128)(2,1)S(1)}, bf16[7,128,128]{2,1,0:T(8,128)(2,1)S(1)}, u32[]{:S(2)}, u32[]{:S(2)}) collective-permute-start(bf16[7,128,128]{2,1,0:T(8,128)(2,1)S(1)} %get-tuple-element.80), channel_id=1, source_target_pairs={{0,2},{1,3},{2,0},{3,1},{4,6},{5,7},{6,4},{7,5},{8,10},{9,11},{10,... | collective-permute-start | bytes 688136 | tf_op jit(solution)/shard_map/ppermute | solution.py:346
  109.0 2.4 %collective-permute-start.11 = (bf16[7,128,128]{2,1,0:T(8,128)(2,1)S(1)}, bf16[7,128,128]{2,1,0:T(8,128)(2,1)S(1)}, u32[]{:S(2)}, u32[]{:S(2)}) collective-permute-start(bf16[7,128,128]{2,1,0:T(8,128)(2,1)S(1)} %get-tuple-element.84), channel_id=1, source_target_pairs={{0,8},{1,9},{2,10},{3,11},{4,12},{5,13},{6,14},{7,15},{8,0},{9,1},... | collective-permute-start | bytes 688136 | tf_op jit(solution)/shard_map/ppermute | solution.py:346
  112.6 3.3 %collective-permute-done.8.refs_2_ = bf16[7,128,128]{2,1,0:T(8,128)(2,1)S(1)} collective-permute-done((bf16[7,128,128]{2,1,0:T(8,128)(2,1)S(1)}, bf16[7,128,128]{2,1,0:T(8,128)(2,1)S(1)}, u32[]{:S(2)}, u32[]{:S(2)}) %collective-permute-start.8) | collective-permute-done | bytes 229408 | tf_op jit(solution)/shard_map/ppermute | solution.py:346
  115.9 8.9 %collective-permute-done.9.refs_3_ = bf16[7,128,128]{2,1,0:T(8,128)(2,1)S(1)} collective-permute-done((bf16[7,128,128]{2,1,0:T(8,128)(2,1)S(1)}, bf16[7,128,128]{2,1,0:T(8,128)(2,1)S(1)}, u32[]{:S(2)}, u32[]{:S(2)}) %collective-permute-start.9) | collective-permute-done | bytes 229408 | tf_op jit(solution)/shard_map/ppermute | solution.py:346
  124.8 3.6 %collective-permute-done.11.refs_6_ = bf16[7,128,128]{2,1,0:T(8,128)(2,1)S(1)} collective-permute-done((bf16[7,128,128]{2,1,0:T(8,128)(2,1)S(1)}, bf16[7,128,128]{2,1,0:T(8,128)(2,1)S(1)}, u32[]{:S(2)}, u32[]{:S(2)}) %collective-permute-start.11) | collective-permute-done | bytes 229408 | tf_op jit(solution)/shard_map/ppermute | solution.py:346
  128.6 2.5 %collective-permute-start.13 = (bf16[7,32,128]{2,1,0:T(8,128)(2,1)S(1)}, bf16[7,32,128]{2,1,0:T(8,128)(2,1)S(1)}, u32[]{:S(2)}, u32[]{:S(2)}) collective-permute-start(bf16[7,32,128]{2,1,0:T(8,128)(2,1)S(1)} %get-tuple-element.87), channel_id=1, source_target_pairs={{0,4},{1,5},{2,6},{3,7},{4,8},{5,9},{6,10},{7,11},{8,12},{9,13},{1... | collective-permute-start | bytes 172040 | tf_op jit(solution)/shard_map/ppermute | solution.py:346
  143.8 2.4 %collective-permute-start.20 = (f32[32,256]{1,0:T(8,128)S(1)}, f32[32,256]{1,0:T(8,128)S(1)}, u32[]{:S(2)}, u32[]{:S(2)}) collective-permute-start(f32[32,256]{1,0:T(8,128)S(1)} %get-tuple-element.97), channel_id=1, source_target_pairs={{0,32},{1,33},{2,34},{3,35},{4,36},{5,37},{6,38},{7,39},{8,40},{9,... | collective-permute-start | bytes 98312 | tf_op jit(solution)/shard_map/ppermute | solution.py:346
  146.2 3.2 %collective-permute-start.21 = (f32[32,256]{1,0:T(8,128)S(1)}, f32[32,256]{1,0:T(8,128)S(1)}, u32[]{:S(2)}, u32[]{:S(2)}) collective-permute-start(f32[32,256]{1,0:T(8,128)S(1)} %get-tuple-element.98), channel_id=1, source_target_pairs={{0,64},{1,65},{2,66},{3,67},{4,68},{5,69},{6,70},{7,71},{8,72},{9,... | collective-permute-start | bytes 98312 | tf_op jit(solution)/shard_map/ppermute | solution.py:346
  149.3 3.1 %collective-permute-start.22 = (f32[32,256]{1,0:T(8,128)S(1)}, f32[32,256]{1,0:T(8,128)S(1)}, u32[]{:S(2)}, u32[]{:S(2)}) collective-permute-start(f32[32,256]{1,0:T(8,128)S(1)} %get-tuple-element.99), channel_id=1, source_target_pairs={{0,96},{1,97},{2,98},{3,99},{4,100},{5,101},{6,102},{7,103},{8,104... | collective-permute-start | bytes 98312 | tf_op jit(solution)/shard_map/ppermute | solution.py:346
  153.5 6.9 %collective-permute-start.23 = (f32[32,256]{1,0:T(8,128)S(1)}, f32[32,256]{1,0:T(8,128)S(1)}, u32[]{:S(2)}, u32[]{:S(2)}) collective-permute-start(f32[32,256]{1,0:T(8,128)S(1)} %add_add_fusion), channel_id=1, source_target_pairs={{0,128},{128,0},{1,129},{129,1},{2,130},{130,2},{3,131},{131,3},{4... | collective-permute-start | bytes 98312 | tf_op jit(solution)/shard_map/ppermute | solution.py:324
  160.4 4.3 %shard_map.141 = (bf16[1024,512]{1,0:T(8,128)(2,1)}, f32[512,512]{1,0:T(8,128)}) custom-call(bf16[1024,512]{1,0:T(8,128)(2,1)} %get-tuple-element.63.refs_0_, bf16[3584,512]{1,0:T(8,128)(2,1)} %refs_5_.1, bf16[512,512]{1,0:T(8,128)(2,1)} %get-tuple-element.64.refs_2_, bf16[3584,512]{1,0:T(8,128)(2,1)} %refs_5_.1, ...), custom_call_target="tpu_custom_call" | custom-call | flops 1073741824 | bytes 16252928 | tf_op jit(solution)/shard_map/pallas_call | solution.py:152
  166.4 3.2 %shard_map.143 = bf16[512,512]{1,0:T(8,128)(2,1)} custom-call(s32[1,1024]{1,0:T(1,128)} %get-tuple-element.62.refs_0_, s32[1,128]{1,0:T(1,128)} %refs_1_.3, f32[512,512]{1,0:T(8,128)} %get-tuple-element.67.refs_2_, bf16[64,512]{1,0:T(8,128)(2,1)} %copy-done.7, bf16[64,512]{1,0:T(8,128)(2,1)} %copy-done.8, bf16[1024,512]{1,0:T(8,128)(2,1)} %bitcast.16), custom_call_target="tpu_custom_call" | custom-call | flops 536870912 | bytes 2757120 | tf_op jit(solution)/shard_map/pallas_call | solution.py:152
  (64 shorter events, 25.8 us)
Async XLA Ops:
  3.7 14.4 %collective-permute-start = (bf16[1024,512]{1,0:T(8,128)(2,1)}, bf16[1024,512]{1,0:T(8,128)(2,1)}, u32[]{:S(2)}, u32[]{:S(2)}) collective-permute-start(bf16[1024,512]{1,0:T(8,128)(2,1)} %get-tuple-element.52), channel_id=1, source_target_pairs={{0,128},{128,0},{1,129},{129,1},{2,130},{130,2},{3,131},{131,3},{4... | collective-permute-start | bytes 3145736 | tf_op jit(solution)/shard_map/ppermute | solution.py:324
  7.0 11.1 %collective-permute-start.1 = (bf16[64,512]{1,0:T(8,128)(2,1)}, bf16[64,512]{1,0:T(8,128)(2,1)S(1)}, u32[]{:S(2)}, u32[]{:S(2)}) collective-permute-start(bf16[64,512]{1,0:T(8,128)(2,1)} %get-tuple-element.53), channel_id=1, source_target_pairs={{0,1},{1,2},{2,3},{3,4},{4,5},{5,6},{6,7},{7,8},{8,9},{9,10},{10,1... | collective-permute-start | bytes 196616 | tf_op jit(solution)/shard_map/ppermute | solution.py:329
  7.0 11.1 %collective-permute-start.2 = (bf16[64,512]{1,0:T(8,128)(2,1)}, bf16[64,512]{1,0:T(8,128)(2,1)S(1)}, u32[]{:S(2)}, u32[]{:S(2)}) collective-permute-start(bf16[64,512]{1,0:T(8,128)(2,1)} %get-tuple-element.54), channel_id=1, source_target_pairs={{0,127},{1,0},{2,1},{3,2},{4,3},{5,4},{6,5},{7,6},{8,7},{9,8},{10,... | collective-permute-start | bytes 196616 | tf_op jit(solution)/shard_map/ppermute | solution.py:329
  18.1 38.5 %all-to-all-start = ((bf16[128,8,512]{2,1,0:T(8,128)(2,1)}), bf16[128,8,512]{2,1,0:T(8,128)(2,1)S(1)}, u32[]{:S(2)}, u32[]{:S(2)}) async-start(bf16[128,8,512]{2,1,0:T(8,128)(2,1)} %bitcast.7), calls=%async_computation | async-start | bytes 2097152 | tf_op jit(solution)/shard_map/all_to_all | solution.py:336
  74.1 8.3 %collective-permute-start.3 = (bf16[7,2,4,128,128]{4,3,2,1,0:T(8,128)(2,1)}, bf16[7,2,4,128,128]{4,3,2,1,0:T(8,128)(2,1)S(1)}, u32[]{:S(2)}, u32[]{:S(2)}) collective-permute-start(bf16[7,2,4,128,128]{4,3,2,1,0:T(8,128)(2,1)} %get-tuple-element.69), channel_id=1, source_target_pairs={{0,128},{128,0},{1,129},{129,1},{2,130},{130,2},{3,131},{131,3},{4... | collective-permute-start | bytes 5505032 | tf_op jit(solution)/shard_map/ppermute | solution.py:324
  78.7 14.5 %collective-permute-start.5 = (bf16[1024,512]{1,0:T(8,128)(2,1)}, bf16[1024,512]{1,0:T(8,128)(2,1)S(1)}, u32[]{:S(2)}, u32[]{:S(2)}) collective-permute-start(bf16[1024,512]{1,0:T(8,128)(2,1)} %get-tuple-element.71), channel_id=1, source_target_pairs={{0,128},{128,0},{1,129},{129,1},{2,130},{130,2},{3,131},{131,3},{4... | collective-permute-start | bytes 3145736 | tf_op jit(solution)/shard_map/ppermute | solution.py:324
  84.3 9.0 %collective-permute-start.4 = (bf16[7,128,128]{2,1,0:T(8,128)(2,1)S(1)}, bf16[7,128,128]{2,1,0:T(8,128)(2,1)S(1)}, u32[]{:S(2)}, u32[]{:S(2)}) collective-permute-start(bf16[7,128,128]{2,1,0:T(8,128)(2,1)S(1)} %get-tuple-element.70), channel_id=1, source_target_pairs={{0,1},{1,2},{2,3},{3,0},{4,5},{5,6},{6,7},{7,4},{8,9},{9,10},{10,1... | collective-permute-start | bytes 688136 | tf_op jit(solution)/shard_map/ppermute | solution.py:346
  84.7 8.5 %collective-permute-start.6 = (bf16[64,512]{1,0:T(8,128)(2,1)S(1)}, bf16[64,512]{1,0:T(8,128)(2,1)S(1)}, u32[]{:S(2)}, u32[]{:S(2)}) collective-permute-start(bf16[64,512]{1,0:T(8,128)(2,1)S(1)} %copy-done.10), channel_id=1, source_target_pairs={{0,1},{1,2},{2,3},{3,4},{4,5},{5,6},{6,7},{7,8},{8,9},{9,10},{10,1... | collective-permute-start | bytes 196616 | tf_op jit(solution)/shard_map/ppermute | solution.py:329
  85.0 8.3 %collective-permute-start.7 = (bf16[64,512]{1,0:T(8,128)(2,1)S(1)}, bf16[64,512]{1,0:T(8,128)(2,1)S(1)}, u32[]{:S(2)}, u32[]{:S(2)}) collective-permute-start(bf16[64,512]{1,0:T(8,128)(2,1)S(1)} %copy-done.9), channel_id=1, source_target_pairs={{0,127},{1,0},{2,1},{3,2},{4,3},{5,4},{6,5},{7,6},{8,7},{9,8},{10,... | collective-permute-start | bytes 196616 | tf_op jit(solution)/shard_map/ppermute | solution.py:329
  94.3 71.2 %all-to-all-start.1 = ((bf16[128,8,512]{2,1,0:T(8,128)(2,1)}), bf16[128,8,512]{2,1,0:T(8,128)(2,1)S(1)}, u32[]{:S(2)}, u32[]{:S(2)}) async-start(bf16[128,8,512]{2,1,0:T(8,128)(2,1)} %bitcast.19), calls=%async_computation.1 | async-start | bytes 2097152 | tf_op jit(solution)/shard_map/all_to_all | solution.py:336
  104.8 11.1 %collective-permute-start.8 = (bf16[7,128,128]{2,1,0:T(8,128)(2,1)S(1)}, bf16[7,128,128]{2,1,0:T(8,128)(2,1)S(1)}, u32[]{:S(2)}, u32[]{:S(2)}) collective-permute-start(bf16[7,128,128]{2,1,0:T(8,128)(2,1)S(1)} %get-tuple-element.80), channel_id=1, source_target_pairs={{0,2},{1,3},{2,0},{3,1},{4,6},{5,7},{6,4},{7,5},{8,10},{9,11},{10,... | collective-permute-start | bytes 688136 | tf_op jit(solution)/shard_map/ppermute | solution.py:346
  107.0 17.8 %collective-permute-start.9 = (bf16[7,128,128]{2,1,0:T(8,128)(2,1)S(1)}, bf16[7,128,128]{2,1,0:T(8,128)(2,1)S(1)}, u32[]{:S(2)}, u32[]{:S(2)}) collective-permute-start(bf16[7,128,128]{2,1,0:T(8,128)(2,1)S(1)} %get-tuple-element.81), channel_id=1, source_target_pairs={{0,3},{1,0},{2,1},{3,2},{4,7},{5,4},{6,5},{7,6},{8,11},{9,8},{10,9... | collective-permute-start | bytes 688136 | tf_op jit(solution)/shard_map/ppermute | solution.py:346
  107.9 16.9 %collective-permute-start.10 = (bf16[7,128,128]{2,1,0:T(8,128)(2,1)S(1)}, bf16[7,128,128]{2,1,0:T(8,128)(2,1)S(1)}, u32[]{:S(2)}, u32[]{:S(2)}) collective-permute-start(bf16[7,128,128]{2,1,0:T(8,128)(2,1)S(1)} %get-tuple-element.83), channel_id=1, source_target_pairs={{0,4},{1,5},{2,6},{3,7},{4,8},{5,9},{6,10},{7,11},{8,12},{9,13},{1... | collective-permute-start | bytes 688136 | tf_op jit(solution)/shard_map/ppermute | solution.py:346
  109.0 19.3 %collective-permute-start.11 = (bf16[7,128,128]{2,1,0:T(8,128)(2,1)S(1)}, bf16[7,128,128]{2,1,0:T(8,128)(2,1)S(1)}, u32[]{:S(2)}, u32[]{:S(2)}) collective-permute-start(bf16[7,128,128]{2,1,0:T(8,128)(2,1)S(1)} %get-tuple-element.84), channel_id=1, source_target_pairs={{0,8},{1,9},{2,10},{3,11},{4,12},{5,13},{6,14},{7,15},{8,0},{9,1},... | collective-permute-start | bytes 688136 | tf_op jit(solution)/shard_map/ppermute | solution.py:346
  111.4 16.9 %collective-permute-start.12 = (bf16[7,128,128]{2,1,0:T(8,128)(2,1)S(1)}, bf16[7,128,128]{2,1,0:T(8,128)(2,1)S(1)}, u32[]{:S(2)}, u32[]{:S(2)}) collective-permute-start(bf16[7,128,128]{2,1,0:T(8,128)(2,1)S(1)} %get-tuple-element.85), channel_id=1, source_target_pairs={{0,12},{1,13},{2,14},{3,15},{4,0},{5,1},{6,2},{7,3},{8,4},{9,5},{1... | collective-permute-start | bytes 688136 | tf_op jit(solution)/shard_map/ppermute | solution.py:346
  128.6 6.9 %collective-permute-start.13 = (bf16[7,32,128]{2,1,0:T(8,128)(2,1)S(1)}, bf16[7,32,128]{2,1,0:T(8,128)(2,1)S(1)}, u32[]{:S(2)}, u32[]{:S(2)}) collective-permute-start(bf16[7,32,128]{2,1,0:T(8,128)(2,1)S(1)} %get-tuple-element.87), channel_id=1, source_target_pairs={{0,4},{1,5},{2,6},{3,7},{4,8},{5,9},{6,10},{7,11},{8,12},{9,13},{1... | collective-permute-start | bytes 172040 | tf_op jit(solution)/shard_map/ppermute | solution.py:346
  131.1 6.3 %collective-permute-start.14 = (bf16[7,32,128]{2,1,0:T(8,128)(2,1)S(1)}, bf16[7,32,128]{2,1,0:T(8,128)(2,1)S(1)}, u32[]{:S(2)}, u32[]{:S(2)}) collective-permute-start(bf16[7,32,128]{2,1,0:T(8,128)(2,1)S(1)} %get-tuple-element.88), channel_id=1, source_target_pairs={{0,8},{1,9},{2,10},{3,11},{4,12},{5,13},{6,14},{7,15},{8,0},{9,1},... | collective-permute-start | bytes 172040 | tf_op jit(solution)/shard_map/ppermute | solution.py:346
  133.0 4.4 %collective-permute-start.15 = (bf16[7,32,128]{2,1,0:T(8,128)(2,1)S(1)}, bf16[7,32,128]{2,1,0:T(8,128)(2,1)S(1)}, u32[]{:S(2)}, u32[]{:S(2)}) collective-permute-start(bf16[7,32,128]{2,1,0:T(8,128)(2,1)S(1)} %get-tuple-element.89), channel_id=1, source_target_pairs={{0,12},{1,13},{2,14},{3,15},{4,0},{5,1},{6,2},{7,3},{8,4},{9,5},{1... | collective-permute-start | bytes 172040 | tf_op jit(solution)/shard_map/ppermute | solution.py:346
  133.6 4.5 %collective-permute-start.16 = (bf16[7,32,128]{2,1,0:T(8,128)(2,1)S(1)}, bf16[7,32,128]{2,1,0:T(8,128)(2,1)S(1)}, u32[]{:S(2)}, u32[]{:S(2)}) collective-permute-start(bf16[7,32,128]{2,1,0:T(8,128)(2,1)S(1)} %get-tuple-element.91), channel_id=1, source_target_pairs={{0,1},{1,2},{2,3},{3,0},{4,5},{5,6},{6,7},{7,4},{8,9},{9,10},{10,1... | collective-permute-start | bytes 172040 | tf_op jit(solution)/shard_map/ppermute | solution.py:346
  134.4 4.5 %collective-permute-start.17 = (bf16[7,32,128]{2,1,0:T(8,128)(2,1)S(1)}, bf16[7,32,128]{2,1,0:T(8,128)(2,1)S(1)}, u32[]{:S(2)}, u32[]{:S(2)}) collective-permute-start(bf16[7,32,128]{2,1,0:T(8,128)(2,1)S(1)} %get-tuple-element.92), channel_id=1, source_target_pairs={{0,2},{1,3},{2,0},{3,1},{4,6},{5,7},{6,4},{7,5},{8,10},{9,11},{10,... | collective-permute-start | bytes 172040 | tf_op jit(solution)/shard_map/ppermute | solution.py:346
  143.8 8.7 %collective-permute-start.20 = (f32[32,256]{1,0:T(8,128)S(1)}, f32[32,256]{1,0:T(8,128)S(1)}, u32[]{:S(2)}, u32[]{:S(2)}) collective-permute-start(f32[32,256]{1,0:T(8,128)S(1)} %get-tuple-element.97), channel_id=1, source_target_pairs={{0,32},{1,33},{2,34},{3,35},{4,36},{5,37},{6,38},{7,39},{8,40},{9,... | collective-permute-start | bytes 98312 | tf_op jit(solution)/shard_map/ppermute | solution.py:346
  146.2 7.0 %collective-permute-start.21 = (f32[32,256]{1,0:T(8,128)S(1)}, f32[32,256]{1,0:T(8,128)S(1)}, u32[]{:S(2)}, u32[]{:S(2)}) collective-permute-start(f32[32,256]{1,0:T(8,128)S(1)} %get-tuple-element.98), channel_id=1, source_target_pairs={{0,64},{1,65},{2,66},{3,67},{4,68},{5,69},{6,70},{7,71},{8,72},{9,... | collective-permute-start | bytes 98312 | tf_op jit(solution)/shard_map/ppermute | solution.py:346
  149.3 4.1 %collective-permute-start.22 = (f32[32,256]{1,0:T(8,128)S(1)}, f32[32,256]{1,0:T(8,128)S(1)}, u32[]{:S(2)}, u32[]{:S(2)}) collective-permute-start(f32[32,256]{1,0:T(8,128)S(1)} %get-tuple-element.99), channel_id=1, source_target_pairs={{0,96},{1,97},{2,98},{3,99},{4,100},{5,101},{6,102},{7,103},{8,104... | collective-permute-start | bytes 98312 | tf_op jit(solution)/shard_map/ppermute | solution.py:346
  153.5 11.2 %collective-permute-start.23 = (f32[32,256]{1,0:T(8,128)S(1)}, f32[32,256]{1,0:T(8,128)S(1)}, u32[]{:S(2)}, u32[]{:S(2)}) collective-permute-start(f32[32,256]{1,0:T(8,128)S(1)} %add_add_fusion), channel_id=1, source_target_pairs={{0,128},{128,0},{1,129},{129,1},{2,130},{130,2},{3,131},{131,3},{4... | collective-permute-start | bytes 98312 | tf_op jit(solution)/shard_map/ppermute | solution.py:324
  (13 other events, 224.9 us)

commit v6 on v5

--- a/solution.py
+++ b/solution.py
@@ -234,17 +234,11 @@
         self.own, self.send = own, send
 
 
-def core_kernel(
-    side_ref, target_ref, margin_ref, recv_ref, msg_ref, nodes_ref, na_ref, nb_ref, cot_ref, nsec_ref,
-    dst_ref, esec_ref, slope_ref, agg_ref, edges_ref, src_ref, low_ref, high_ref, wa_ref,
-    send_ref, ret_ref, own_ref, new_ref, part_ref, gedge_ref, bysrc_ref, bydst_ref, glow_ref, ghigh_ref,
-    pooled_ref, hid_ref, gnode_ref, gpool_ref, turned_ref,
-    *, patches, scale
+def node_kernel(
+    target_ref, margin_ref, recv_ref, msg_ref, nodes_ref, na_ref, nb_ref, cot_ref, nsec_ref,
+    ret_ref, gpool_ref, pooled_ref, hid_ref, gnode_ref,
 ):
-    count, width = nodes_ref.shape
-    inner = edges_ref.shape[0] - edges_ref.shape[0] // 4
-    depth = low_ref.shape[0]
-    first = side_ref[0] == 0
+    count = nodes_ref.shape[0]
     target, margin = target_ref[...], margin_ref[...]
     for r in tiles(count):
         coupled = dot(pick_t(target, r.start, TILE, margin), recv_ref[...])
@@ -259,14 +253,24 @@
         gnode = (dot_nt(cot_ref[r], nsec_ref[...]) * slope).astype(BF)
         gnode_ref[r] = gnode
         gpool_ref[r] = dot_nt(gnode, nb_ref[...]).astype(BF)
-        new_ref[r] = (nodes.astype(F32) + dot(hidden, nsec_ref[...])).astype(BF)
-        part_ref[r] = cot_ref[r].astype(F32) + dot_nt(gnode, na_ref[...])
-    flush(new_ref, part_ref)
+    flush(gpool_ref, pooled_ref, hid_ref, gnode_ref)
     gpool = gpool_ref[...]
     col, weight = column(target), column(margin)
     for r in tiles(recv_ref.shape[0]):
         ret_ref[r] = dot(pick(col[r], count, weight[r]), gpool).astype(BF)
-    flush(ret_ref)
+
+
+def grad_kernel(
+    side_ref, dst_ref, gpool_ref, esec_ref, slope_ref, src_ref, nodes_ref, low_ref, high_ref, edges_ref,
+    gnode_ref, agg_ref, pooled_ref, hid_ref, cot_ref, wa_ref,
+    send_ref, own_ref, gedge_ref, bysrc_ref, bydst_ref, glow_ref, ghigh_ref, turned_ref,
+    *, patches, scale
+):
+    count, width = nodes_ref.shape
+    inner = edges_ref.shape[0] - edges_ref.shape[0] // 4
+    depth = low_ref.shape[0]
+    first = side_ref[0] == 0
+    gpool = gpool_ref[...]
     dst_row, src_row = dst_ref[...], src_ref[...]
     dst = column(dst_row)
     for r in tiles(edges_ref.shape[0]):
@@ -295,18 +299,22 @@
         put(blocks, index, dot(turned, right[...]) * scale, first)
 
 
-def edge_rest_kernel(
-    gpre_ref, wc_ref, bysrc_ref, wa_ref, bydst_ref, wb_ref, part_ref, edge_ref, total_ref
+def rest_kernel(
+    gedge_ref, wc_ref, hid_ref, nsec_ref, nodes_ref, bysrc_ref, wa_ref, bydst_ref, wb_ref, gnode_ref, na_ref,
+    cot_ref, edge_ref, new_ref, total_ref,
 ):
-    count, width = bysrc_ref.shape
-    for r in tiles(gpre_ref.shape[0]):
-        edge_ref[r] = dot_nt(gpre_ref[r], wc_ref[...]).astype(BF)
+    for r in tiles(gedge_ref.shape[0]):
+        edge_ref[r] = dot_nt(gedge_ref[r], wc_ref[...]).astype(BF)
     flush(edge_ref)
-    for r in tiles(count):
+    for r in tiles(bysrc_ref.shape[0]):
+        new_ref[r] = (nodes_ref[r].astype(F32) + dot(hid_ref[r], nsec_ref[...])).astype(BF)
+    flush(new_ref)
+    for r in tiles(bysrc_ref.shape[0]):
         total_ref[r] = (
-            part_ref[r]
+            cot_ref[r].astype(F32)
             + dot_nt(bysrc_ref[r], wa_ref[...])
             + dot_nt(bydst_ref[r], wb_ref[...])
+            + dot_nt(gnode_ref[r], na_ref[...])
         )
 
 
@@ -359,20 +367,32 @@
     return total
 
 
-def plane_kernel(*refs):
-    for c in range(2):
-        total = total_of(refs[c * RING : (c + 1) * RING])
+def plane_kernel(place_ref, *refs):
+    ins, outs = refs[: 2 * RING], refs[2 * RING :]
+    spots = (place_ref[1] // RING % RING, place_ref[1] % RING)
+    for c, spot in enumerate(spots):
+        keep_ref, send_ref = outs[2 * c : 2 * c + 2]
+        total = total_of(ins[c * RING : (c + 1) * RING])
         fine = total.shape[1] // RING
-        for d in range(RING):
-            refs[(2 + c) * RING + d][...] = total[:, d * fine : (d + 1) * fine].astype(BF)
-
-
-def depth_kernel(place_ref, *refs):
-    ins, (keep_ref, send_ref, hold) = refs[: 2 * RING], refs[2 * RING :]
+        parts = [total[:, d * fine : (d + 1) * fine] for d in range(RING)]
+        even = spot % 2 == 0
+        keep_ref[0] = parts[0]
+        keep_ref[1] = jnp.where(even, parts[3], parts[1])
+        send_ref[0] = jnp.where(even, parts[1], parts[3]).astype(BF)
+        send_ref[1] = parts[2].astype(BF)
+
+
+def line_kernel(keep_x, other_x, keep_y, other_y, mine_x, send_x, mine_y, send_y):
+    for keep, other, mine, send in ((keep_x, other_x, mine_x, send_x), (keep_y, other_y, mine_y, send_y)):
+        mine[...] = keep[0] + other[0].astype(F32)
+        send[...] = (keep[1] + other[1].astype(F32)).astype(BF)
+
+
+def depth_kernel(place_ref, mine_x, other_x, mine_y, other_y, keep_ref, send_ref, hold):
     depth = hold.shape[0]
     hold[...] = jnp.zeros(hold.shape, F32)
-    for c in range(2):
-        total = total_of(ins[c * RING : (c + 1) * RING])
+    for c, (mine, other) in enumerate(((mine_x, other_x), (mine_y, other_y))):
+        total = mine[...] + other[...].astype(F32)
         blocks, rows, lane = total.shape
         fine = rows // depth
         for block in range(blocks):
@@ -387,11 +407,23 @@
         send_ref[j] = jnp.where(even, high, low).astype(BF)
 
 
-def pair_kernel(place_ref, keep_ref, other_ref, *outs):
-    mine = place_ref[1] // PLANE // 2
-    for d, out in enumerate(outs):
-        j = (mine + d) % len(outs)
-        out[...] = keep_ref[j] + other_ref[j].astype(F32)
+def halve_kernel(place_ref, keep_ref, other_ref, mine_ref, send_ref, *, bit):
+    clear = (place_ref[1] // PLANE >> bit) % 2 == 0
+    for k in range(mine_ref.shape[0]):
+        low = keep_ref[2 * k] + other_ref[2 * k].astype(F32)
+        high = keep_ref[2 * k + 1] + other_ref[2 * k + 1].astype(F32)
+        mine_ref[k] = jnp.where(clear, low, high)
+        send_ref[k] = jnp.where(clear, high, low).astype(send_ref.dtype)
+
+
+def finish_kernel(place_ref, own_ref, own_far, other_ref, other_far, out_ref):
+    rows = out_ref.shape[0]
+    own = own_ref[0, :rows] + own_far[0, :rows]
+    other = other_ref[0, :rows] + other_far[0, :rows]
+    first = place_ref[0] == 0
+    lane = own.shape[1]
+    out_ref[:, :lane] = jnp.where(first, own, other)
+    out_ref[:, lane:] = jnp.where(first, other, own)
 
 
 def small_call(kernel, place, args, outs, scratch=()):
@@ -414,35 +446,62 @@
     ]
 
 
-def weight_sums(own, other, place, tied):
+def flip(value, dz=0, dy=0, dx=0, core=0):
     patches = lax.axis_size("patch")
-    depth = patches // PLANE
+    mask = dz * PLANE + dy * RING + dx
+    pairs = [
+        (m * patches + p, (m ^ core) * patches + (p ^ mask)) for m in range(2) for p in range(patches)
+    ]
+    return lax.ppermute(value, ("mesh", "patch"), pairs)
+
+
+def weight_sums(own, other, place, tied, last):
+    depth = lax.axis_size("patch") // PLANE
     blocks, _, _, rows, lane = own.shape
     fine = rows // RING // depth
+    padded = (blocks * fine + 15) // 16 * 16
     pieces = call(join_kernel, (own, other), (shape(BF, blocks, rows, lane),) * (2 * RING))
     pieces = spread(pieces, ("dx", "dy"))
-    pieces[1], tied = lax.optimization_barrier((pieces[1], tied))
-    pieces = call(plane_kernel, pieces, (shape(BF, blocks, rows // RING, lane),) * (2 * RING))
-    pieces = spread(pieces, ("dy", "dx"))
-    padded = (blocks * fine + 15) // 16 * 16
+    pieces, tied = lax.optimization_barrier((pieces, tied))
+    pair = lambda dtype: shape(dtype, 2, blocks, rows // RING, lane)
+    one = lambda dtype: shape(dtype, blocks, rows // RING, lane)
+    keep_x, send_x, keep_y, send_y = small_call(
+        plane_kernel, place, pieces, (pair(F32), pair(BF), pair(F32), pair(BF))
+    )
+    mine_x, send_x, mine_y, send_y = call(
+        line_kernel,
+        (keep_x, flip(send_x, dy=1), keep_y, flip(send_y, dx=1)),
+        (one(F32), one(BF), one(F32), one(BF)),
+    )
+    other_x, other_y = flip(send_x, dy=3), flip(send_y, dx=3)
     half = depth // 2
+    deep = lambda dtype, count: shape(dtype, count, padded, 2 * lane)
     keep, send = small_call(
         depth_kernel,
         place,
-        pieces,
-        (shape(F32, half, padded, 2 * lane), shape(BF, half, padded, 2 * lane)),
+        (mine_x, other_x, mine_y, other_y),
+        (deep(F32, half), deep(BF, half)),
         scratch=(pltpu.VMEM((depth, padded, 2 * lane), F32),),
     )
-    pairs = [(p, (p // PLANE ^ 1) * PLANE + p % PLANE) for p in range(patches)]
-    other = lax.ppermute(send, "patch", pairs)
-    pieces = small_call(pair_kernel, place, (keep, other), (shape(F32, padded, 2 * lane),) * half)
-    own = pieces[0]
-    for d in range(1, half):
-        own = own + hop(pieces[d], dz=2 * d)
-    other = from_partner(own)
-    first = lax.axis_index("mesh") == 0
-    both = jnp.concatenate([jnp.where(first, own, other), jnp.where(first, other, own)], axis=1)
-    return both[: blocks * fine].reshape(blocks, fine * 4 * lane), tied
+    bit = 0
+    while half > 1:
+        other = flip(send, dz=1 << bit)
+        bit, half = bit + 1, half // 2
+        keep, send = small_call(
+            lambda *refs, bit=bit: halve_kernel(*refs, bit=bit),
+            place,
+            (keep, other),
+            (deep(F32, half), deep(F32 if half == 1 else BF, half)),
+        )
+    tied, last, send = lax.optimization_barrier((tied, last(tied), send))
+    far = 1 << bit
+    (result,) = small_call(
+        finish_kernel,
+        place,
+        (keep, flip(send, dz=far), flip(keep, core=1), flip(send, dz=far, core=1)),
+        (shape(F32, blocks * fine, 4 * lane),),
+    )
+    return result.reshape(blocks, fine * 4 * lane), tied, last
 
 
 def shards(
@@ -502,35 +561,48 @@
     rim = shape(BF, depth, width)
     slot_block = shape(BF, slots, width)
     edge_block = shape(BF, edge_count, width)
-    total = shape(F32, count, width)
-    send, returned, own, new_nodes, part, grad_edge_pre, by_source, by_target, grad_low, grad_high = stream(
-        lambda *refs: core_kernel(*refs, patches=patches, scale=scale),
+    returned, grad_pooled, pooled, hidden, grad_node_pre = stream(
+        node_kernel,
+        (target, margin, received, message, nodes_own, weight(4), weight(5), cotangent, weight(6)),
+        (slot_block, square, square, square, square),
+        flops=count * 8 * unit,
+    )
+    crossed_back = from_partner(returned)
+    couple_back = route(crossed_back)
+    grad_pooled, crossed_back = lax.optimization_barrier((grad_pooled, crossed_back))
+    send, own, grad_edge_pre, by_source, by_target, grad_low, grad_high = stream(
+        lambda *refs: grad_kernel(*refs, patches=patches, scale=scale),
         (
-            side, target, margin, received, message, nodes_own, weight(4), weight(5), cotangent,
-            weight(6), edge_dst, weight(3), slope, agg, edges_own, edge_src, low, high, weight(0),
+            side, edge_dst, grad_pooled, weight(3), slope, edge_src, nodes_own, low, high, edges_own,
+            grad_node_pre, agg, pooled, hidden, cotangent, weight(0),
         ),
-        (grads, slot_block, grads, square, total, edge_block, square, square, rim, rim),
-        scratch=[pltpu.VMEM((count, width), BF)] * 5,
-        flops=edge_count * 18 * unit,
+        (grads, grads, edge_block, square, square, rim, rim),
+        scratch=[pltpu.VMEM((count, width), BF)],
+        flops=edge_count * 14 * unit,
     )
     other = from_partner(send)
-    crossed_back = from_partner(returned)
     back_low, back_high = shift(grad_high, 1), shift(grad_low, -1)
-    summed, tied = weight_sums(own, other, side, (crossed_back, back_low, back_high))
-    crossed_back, back_low, back_high = tied
-    couple_back = route(crossed_back)
-    edge_grads, total = stream(
-        edge_rest_kernel,
-        (grad_edge_pre, weight(2), by_source, weight(0), by_target, weight(1), part),
-        (edge_block, total),
-        flops=edge_count * 2 * unit,
-    )
-    (node_grads,) = stream(
-        last_kernel,
-        (live, halo_rows, total, back_low, back_high, couple_back),
-        (square,),
-        flops=count * 2 * unit,
-    )
+    edge_grads, new_nodes, total = stream(
+        rest_kernel,
+        (
+            grad_edge_pre, weight(2), hidden, weight(6), nodes_own, by_source, weight(0), by_target,
+            weight(1), grad_node_pre, weight(4), cotangent,
+        ),
+        (edge_block, square, shape(F32, count, width)),
+        flops=edge_count * 3 * unit,
+    )
+
+    def last(tied):
+        low_rows, high_rows, sums = tied
+        (grads,) = stream(
+            last_kernel,
+            (live, halo_rows, sums, low_rows, high_rows, couple_back),
+            (square,),
+            flops=count * 2 * unit,
+        )
+        return grads
+
+    summed, _, node_grads = weight_sums(own, other, side, (back_low, back_high, total), last)
     return (new_nodes[None], node_grads[None], edge_grads[None], summed)
 
 

time: 170 us -> 174 us (1.024)
  waiting for transfers between devices: 48.6 us -> 67.3 us
  starting transfers between devices: 78.7 us -> 60.1 us
  Pallas kernels: 35.8 us -> 42.6 us
  local copies, waits for them, and re-layouts: 5.19 us -> 2.28 us
    ppermute x15 -> x6, starting transfers between devices: 25.6 us -> 3.14 us  [hop(): return lax.ppermute(value, 'patch', pairs)]
    ppermute x4, waiting for transfers between devices: 4.23 us -> 23.3 us  [shift(): lax.ppermute(value, 'patch', [(i, (i + step) % count) for i in range(coun...]
    ppermute x1 -> x9, waiting for transfers between devices: 2.1 us -> 16.6 us  [flip(): return lax.ppermute(value, ('mesh', 'patch'), pairs)]
    ppermute x15 -> x6, waiting for transfers between devices: 18.7 us -> 4.65 us  [hop(): return lax.ppermute(value, 'patch', pairs)]
    ppermute x1 -> x9, starting transfers between devices: 1.1 us -> 14.7 us  [flip(): return lax.ppermute(value, ('mesh', 'patch'), pairs)]
    ppermute x4 -> x3, starting transfers between devices: 15 us -> 8.64 us  [from_partner(): return lax.ppermute(value, 'mesh', [(0, 1), (1, 0)])]
    pallas_call x5 -> x6, Pallas kernels: 33.9 us -> 37.5 us  [stream(): pl.pallas_call(body, out_shape=tuple(outs), in_specs=[hbm if isinstance(a...]
    all_to_all x2, starting transfers between devices: 21.6 us -> 18.3 us  [route(): lax.all_to_all(crossed, 'patch', split_axis=0, concat_axis=0, tiled=True)]
  transfers between devices with their start and end apart: 26 -> 24, of which waited for: 13 -> 12; matrix products, arithmetic and copies ran while one was open for 1% -> 0% of each run, Pallas kernels for 8% -> 11%
where the time goes in v6:
time: 174 us
  waiting for transfers between devices  67.3 us (39%)
  starting transfers between devices  60.1 us (35%)
  Pallas kernels  42.6 us (24%)
  local copies, waits for them, and re-layouts  2.28 us (1%)
    pallas_call x6, Pallas kernels, stream(): pl.pallas_call(body, out_shape=tuple(outs), in_specs=[hbm if isinstance(a...  37.5 us
    ppermute x4, waiting for transfers between devices, shift(): lax.ppermute(value, 'patch', [(i, (i + step) % count) for i in range(coun...  23.3 us
    all_to_all x2, waiting for transfers between devices, route(): lax.all_to_all(crossed, 'patch', split_axis=0, concat_axis=0, tiled=True)  20.8 us
    all_to_all x2, starting transfers between devices, route(): lax.all_to_all(crossed, 'patch', split_axis=0, concat_axis=0, tiled=True)  18.3 us
    ppermute x9, waiting for transfers between devices, flip(): return lax.ppermute(value, ('mesh', 'patch'), pairs)  16.6 us
    ppermute x4, starting transfers between devices, shift(): lax.ppermute(value, 'patch', [(i, (i + step) % count) for i in range(coun...  15.4 us
    ppermute x9, starting transfers between devices, flip(): return lax.ppermute(value, ('mesh', 'patch'), pairs)  14.7 us
    ppermute x3, starting transfers between devices, from_partner(): return lax.ppermute(value, 'mesh', [(0, 1), (1, 0)])  8.64 us
  transfers between devices with their start and end apart: 24, of which 12 were waited for; matrix products, arithmetic and copies ran while one was open for 0% of the time, Pallas kernels for 11%

profile of v6, /device:TPU:1, one launch (start us, length us, event | category | flops | bytes accessed | tf_op | source)
XLA Modules:
  0.0 173.8 jit_solution(16455187398085062083)
XLA Ops:
  0.6 3.0 %shard_map.138 = (bf16[1024,512]{1,0:T(8,128)(2,1)}, bf16[64,512]{1,0:T(8,128)(2,1)}, bf16[64,512]{1,0:T(8,128)(2,1)}, s32[1,1024]{1,0:T(1,128)}) custom-call(s32[1,1024]{1,0:T(1,128)} %bitcast.32, s32[1,128]{1,0:T(1,128)} %bitcast.33, s32[1,128]{1,0:T(1,128)} %refs_1_.5, bf16[512,512]{1,0:T(8,128)(2,1)} %bitcast.16), custom_call_target="tpu_custom_call" | custom-call | flops 603979776 | bytes 1713152 | tf_op jit(solution)/shard_map/pallas_call | solution.py:152
  3.7 3.3 %collective-permute-start = (bf16[1024,512]{1,0:T(8,128)(2,1)}, bf16[1024,512]{1,0:T(8,128)(2,1)}, u32[]{:S(2)}, u32[]{:S(2)}) collective-permute-start(bf16[1024,512]{1,0:T(8,128)(2,1)} %get-tuple-element.65), channel_id=1, source_target_pairs={{0,128},{128,0},{1,129},{129,1},{2,130},{130,2},{3,131},{131,3},{4... | collective-permute-start | bytes 3145736 | tf_op jit(solution)/shard_map/ppermute | solution.py:332
  7.0 8.5 %collective-permute-start.2 = (bf16[64,512]{1,0:T(8,128)(2,1)}, bf16[64,512]{1,0:T(8,128)(2,1)S(1)}, u32[]{:S(2)}, u32[]{:S(2)}) collective-permute-start(bf16[64,512]{1,0:T(8,128)(2,1)} %get-tuple-element.67), channel_id=1, source_target_pairs={{0,127},{1,0},{2,1},{3,2},{4,3},{5,4},{6,5},{7,6},{8,7},{9,8},{10,... | collective-permute-start | bytes 196616 | tf_op jit(solution)/shard_map/ppermute | solution.py:337
  15.5 2.6 %collective-permute-done.1.refs_4_.refs_7_ = bf16[64,512]{1,0:T(8,128)(2,1)S(1)} collective-permute-done((bf16[64,512]{1,0:T(8,128)(2,1)}, bf16[64,512]{1,0:T(8,128)(2,1)S(1)}, u32[]{:S(2)}, u32[]{:S(2)}) %collective-permute-start.1) | collective-permute-done | bytes 65568 | tf_op jit(solution)/shard_map/ppermute | solution.py:337
  18.1 10.9 %all-to-all-start = ((bf16[128,8,512]{2,1,0:T(8,128)(2,1)}), bf16[128,8,512]{2,1,0:T(8,128)(2,1)S(1)}, u32[]{:S(2)}, u32[]{:S(2)}) async-start(bf16[128,8,512]{2,1,0:T(8,128)(2,1)} %bitcast.7), calls=%async_computation | async-start | bytes 2097152 | tf_op jit(solution)/shard_map/all_to_all | solution.py:344
  29.0 6.8 %shard_map.139 = (bf16[1024,512]{1,0:T(8,128)(2,1)}, bf16[512,512]{1,0:T(8,128)(2,1)}, f32[512,512]{1,0:T(8,128)}) custom-call(s32[1,1024]{1,0:T(1,128)} %refs_1_.3, bf16[512,512]{1,0:T(8,128)(2,1)} %bitcast.17, bf16[3584,512]{1,0:T(8,128)(2,1)} %refs_10_.1, s32[1,1024]{1,0:T(1,128)} %refs_5_.3, bf16[64,512]{1,0:T(8,128)(2,1)} %copy-done.3, ...), custom_call_target="tpu_custom_call" | custom-call | flops 3221225472 | bytes 19013632 | tf_op jit(solution)/shard_map/pallas_call | solution.py:152
  35.8 20.8 %all-to-all-done = bf16[128,8,512]{2,1,0:T(8,128)(2,1)S(1)} async-done(((bf16[128,8,512]{2,1,0:T(8,128)(2,1)}), bf16[128,8,512]{2,1,0:T(8,128)(2,1)S(1)}, u32[]{:S(2)}, u32[]{:S(2)}) %all-to-all-start) | async-done | bytes 1048608 | tf_op jit(solution)/shard_map/all_to_all | solution.py:344
  57.6 5.9 %shard_map.140 = (bf16[1024,512]{1,0:T(8,128)(2,1)}, bf16[512,512]{1,0:T(8,128)(2,1)}, bf16[512,512]{1,0:T(8,128)(2,1)}, bf16[512,512]{1,0:T(8,128)(2,1)}, bf16[512,512]{1,0:T(8,128)(2,1)}) custom-call(s32[1,1024]{1,0:T(1,128)} %bitcast.28, f32[1,1024]{1,0:T(1,128)} %bitcast.29, bf16[1024,512]{1,0:T(8,128)(2,1)} %bitcast.21, ...), custom_call_target="tpu_custom_call" | custom-call | flops 2147483648 | bytes 17309696 | tf_op jit(solution)/shard_map/pallas_call | solution.py:152
  63.5 4.8 %collective-permute-start.3 = (bf16[1024,512]{1,0:T(8,128)(2,1)}, bf16[1024,512]{1,0:T(8,128)(2,1)}, u32[]{:S(2)}, u32[]{:S(2)}) collective-permute-start(bf16[1024,512]{1,0:T(8,128)(2,1)} %get-tuple-element.73), channel_id=1, source_target_pairs={{0,128},{128,0},{1,129},{129,1},{2,130},{130,2},{3,131},{131,3},{4... | collective-permute-start | bytes 3145736 | tf_op jit(solution)/shard_map/ppermute | solution.py:332
  69.0 2.0 %collective-permute-done.3 = bf16[1024,512]{1,0:T(8,128)(2,1)} collective-permute-done((bf16[1024,512]{1,0:T(8,128)(2,1)}, bf16[1024,512]{1,0:T(8,128)(2,1)}, u32[]{:S(2)}, u32[]{:S(2)}) %collective-permute-start.3) | collective-permute-done | bytes 1048608 | tf_op jit(solution)/shard_map/ppermute | solution.py:332
  71.0 13.3 %shard_map.141 = (bf16[7,2,4,128,128]{4,3,2,1,0:T(8,128)(2,1)}, bf16[7,2,4,128,128]{4,3,2,1,0:T(8,128)(2,1)}, bf16[1024,512]{1,0:T(8,128)(2,1)}, bf16[512,512]{1...) custom-call(s32[2]{0:T(128)} %pad_add_fusion.refs_0_.place_ref, ...), custom_call_target="tpu_custom_call" | custom-call | flops 7516192768 | bytes 19144712 | tf_op jit(solution)/shard_map/pallas_call | solution.py:152
  84.7 7.5 %all-to-all-start.1 = ((bf16[128,8,512]{2,1,0:T(8,128)(2,1)}), bf16[128,8,512]{2,1,0:T(8,128)(2,1)}, u32[]{:S(2)}, u32[]{:S(2)}) async-start(bf16[128,8,512]{2,1,0:T(8,128)(2,1)} %bitcast.12), calls=%async_computation.1 | async-start | bytes 2097152 | tf_op jit(solution)/shard_map/all_to_all | solution.py:344
  95.8 5.7 %collective-permute-start.12 = (bf16[64,512]{1,0:T(8,128)(2,1)S(1)}, bf16[64,512]{1,0:T(8,128)(2,1)S(1)}, u32[]{:S(2)}, u32[]{:S(2)}) collective-permute-start(bf16[64,512]{1,0:T(8,128)(2,1)S(1)} %copy-done.7), channel_id=1, source_target_pairs={{0,127},{1,0},{2,1},{3,2},{4,3},{5,4},{6,5},{7,6},{8,7},{9,8},{10,... | collective-permute-start | bytes 196616 | tf_op jit(solution)/shard_map/ppermute | solution.py:337
  101.6 20.7 %collective-permute-done.11.refs_3_ = bf16[64,512]{1,0:T(8,128)(2,1)S(1)} collective-permute-done((bf16[64,512]{1,0:T(8,128)(2,1)S(1)}, bf16[64,512]{1,0:T(8,128)(2,1)S(1)}, u32[]{:S(2)}, u32[]{:S(2)}) %collective-permute-start.11) | collective-permute-done | bytes 65568 | tf_op jit(solution)/shard_map/ppermute | solution.py:337
  122.9 2.7 %collective-permute-start.10 = (bf16[7,128,128]{2,1,0:T(8,128)(2,1)S(1)}, bf16[7,128,128]{2,1,0:T(8,128)(2,1)S(1)}, u32[]{:S(2)}, u32[]{:S(2)}) collective-permute-start(bf16[7,128,128]{2,1,0:T(8,128)(2,1)S(1)} %get-tuple-element.93), channel_id=1, source_target_pairs={{0,12},{1,13},{2,14},{3,15},{4,0},{5,1},{6,2},{7,3},{8,4},{9,5},{1... | collective-permute-start | bytes 688136 | tf_op jit(solution)/shard_map/ppermute | solution.py:354
  125.5 5.3 %shard_map.142 = (bf16[1024,512]{1,0:T(8,128)(2,1)}, bf16[512,512]{1,0:T(8,128)(2,1)}, f32[512,512]{1,0:T(8,128)}) custom-call(bf16[1024,512]{1,0:T(8,128)(2,1)} %get-tuple-element.80.refs_0_, bf16[3584,512]{1,0:T(8,128)(2,1)} %refs_10_.1, bf16[512,512]{1,0:T(8,128)(2,1)} %get-tuple-element.79.refs_13_.refs_2_, bf16[3584,512]{1,0:T(8,128)(2,1)} %refs_10_.1, ...), custom_call_target="tpu_custom_call" | custom-call | flops 1610612736 | bytes 25165824 | tf_op jit(solution)/shard_map/pallas_call | solution.py:152
  130.9 4.0 %collective-permute-done.8.refs_5_ = bf16[7,128,128]{2,1,0:T(8,128)(2,1)S(1)} collective-permute-done((bf16[7,128,128]{2,1,0:T(8,128)(2,1)S(1)}, bf16[7,128,128]{2,1,0:T(8,128)(2,1)S(1)}, u32[]{:S(2)}, u32[]{:S(2)}) %collective-permute-start.8) | collective-permute-done | bytes 229408 | tf_op jit(solution)/shard_map/ppermute | solution.py:354
  138.0 2.2 %collective-permute-done.13.other_x = bf16[2,7,32,128]{3,2,1,0:T(8,128)(2,1)S(1)} collective-permute-done((bf16[2,7,32,128]{3,2,1,0:T(8,128)(2,1)S(1)}, bf16[2,7,32,128]{3,2,1,0:T(8,128)(2,1)S(1)}, u32[]{:S(2)}, u32[]{:S(2)}) %collective-permute-start.13) | collective-permute-done | bytes 114720 | tf_op jit(solution)/shard_map/ppermute | solution.py:455
  143.9 2.4 %collective-permute-done.15.other_x = bf16[7,32,128]{2,1,0:T(8,128)(2,1)S(1)} collective-permute-done((bf16[7,32,128]{2,1,0:T(8,128)(2,1)S(1)}, bf16[7,32,128]{2,1,0:T(8,128)(2,1)S(1)}, u32[]{:S(2)}, u32[]{:S(2)}) %collective-permute-start.15) | collective-permute-done | bytes 57376 | tf_op jit(solution)/shard_map/ppermute | solution.py:455
  146.3 2.1 %collective-permute-done.16.other_y = bf16[7,32,128]{2,1,0:T(8,128)(2,1)S(1)} collective-permute-done((bf16[7,32,128]{2,1,0:T(8,128)(2,1)S(1)}, bf16[7,32,128]{2,1,0:T(8,128)(2,1)S(1)}, u32[]{:S(2)}, u32[]{:S(2)}) %collective-permute-start.16) | collective-permute-done | bytes 57376 | tf_op jit(solution)/shard_map/ppermute | solution.py:455
  149.1 3.1 %collective-permute-done.17.refs_2_ = bf16[4,32,256]{2,1,0:T(8,128)(2,1)S(1)} collective-permute-done((bf16[4,32,256]{2,1,0:T(8,128)(2,1)S(1)}, bf16[4,32,256]{2,1,0:T(8,128)(2,1)S(1)}, u32[]{:S(2)}, u32[]{:S(2)}) %collective-permute-start.17) | collective-permute-done | bytes 65568 | tf_op jit(solution)/shard_map/ppermute | solution.py:455
  153.6 3.2 %shard_map.144 = bf16[512,512]{1,0:T(8,128)(2,1)} custom-call(s32[1,1024]{1,0:T(1,128)} %get-tuple-element.100.refs_0_, s32[1,128]{1,0:T(1,128)} %refs_1_.5, f32[512,512]{1,0:T(8,128)} %get-tuple-element.99.refs_2_, bf16[64,512]{1,0:T(8,128)(2,1)} %copy-done.5, bf16[64,512]{1,0:T(8,128)(2,1)} %copy-done.6, bf16[1024,512]{1,0:T(8,128)(2,1)} %bitcast.13.refs_5_), custom_call_target="tpu_custom_call" | custom-call | flops 536870912 | bytes 2757120 | tf_op jit(solution)/shard_map/pallas_call | solution.py:152
  157.5 8.5 %collective-permute-start.21 = (f32[1,32,256]{2,1,0:T(8,128)S(1)}, f32[1,32,256]{2,1,0:T(8,128)S(1)}, u32[]{:S(2)}, u32[]{:S(2)}) collective-permute-start(f32[1,32,256]{2,1,0:T(8,128)S(1)} %get-tuple-element.125), channel_id=1, source_target_pairs={{0,192},{1,193},{2,194},{3,195},{4,196},{5,197},{6,198},{7,199},{8... | collective-permute-start | bytes 98312 | tf_op jit(solution)/shard_map/ppermute | solution.py:455
  167.6 5.0 %collective-permute-done.19.own_far = f32[1,32,256]{2,1,0:T(8,128)S(1)} collective-permute-done((f32[1,32,256]{2,1,0:T(8,128)S(1)}, f32[1,32,256]{2,1,0:T(8,128)S(1)}, u32[]{:S(2)}, u32[]{:S(2)}) %collective-permute-start.19) | collective-permute-done | bytes 32800 | tf_op jit(solution)/shard_map/ppermute | solution.py:455
  (57 shorter events, 18.8 us)
Async XLA Ops:
  3.7 14.4 %collective-permute-start = (bf16[1024,512]{1,0:T(8,128)(2,1)}, bf16[1024,512]{1,0:T(8,128)(2,1)}, u32[]{:S(2)}, u32[]{:S(2)}) collective-permute-start(bf16[1024,512]{1,0:T(8,128)(2,1)} %get-tuple-element.65), channel_id=1, source_target_pairs={{0,128},{128,0},{1,129},{129,1},{2,130},{130,2},{3,131},{131,3},{4... | collective-permute-start | bytes 3145736 | tf_op jit(solution)/shard_map/ppermute | solution.py:332
  7.0 11.1 %collective-permute-start.1 = (bf16[64,512]{1,0:T(8,128)(2,1)}, bf16[64,512]{1,0:T(8,128)(2,1)S(1)}, u32[]{:S(2)}, u32[]{:S(2)}) collective-permute-start(bf16[64,512]{1,0:T(8,128)(2,1)} %get-tuple-element.66), channel_id=1, source_target_pairs={{0,1},{1,2},{2,3},{3,4},{4,5},{5,6},{6,7},{7,8},{8,9},{9,10},{10,1... | collective-permute-start | bytes 196616 | tf_op jit(solution)/shard_map/ppermute | solution.py:337
  7.0 11.1 %collective-permute-start.2 = (bf16[64,512]{1,0:T(8,128)(2,1)}, bf16[64,512]{1,0:T(8,128)(2,1)S(1)}, u32[]{:S(2)}, u32[]{:S(2)}) collective-permute-start(bf16[64,512]{1,0:T(8,128)(2,1)} %get-tuple-element.67), channel_id=1, source_target_pairs={{0,127},{1,0},{2,1},{3,2},{4,3},{5,4},{6,5},{7,6},{8,7},{9,8},{10,... | collective-permute-start | bytes 196616 | tf_op jit(solution)/shard_map/ppermute | solution.py:337
  18.1 38.5 %all-to-all-start = ((bf16[128,8,512]{2,1,0:T(8,128)(2,1)}), bf16[128,8,512]{2,1,0:T(8,128)(2,1)S(1)}, u32[]{:S(2)}, u32[]{:S(2)}) async-start(bf16[128,8,512]{2,1,0:T(8,128)(2,1)} %bitcast.7), calls=%async_computation | async-start | bytes 2097152 | tf_op jit(solution)/shard_map/all_to_all | solution.py:344
  63.5 7.5 %collective-permute-start.3 = (bf16[1024,512]{1,0:T(8,128)(2,1)}, bf16[1024,512]{1,0:T(8,128)(2,1)}, u32[]{:S(2)}, u32[]{:S(2)}) collective-permute-start(bf16[1024,512]{1,0:T(8,128)(2,1)} %get-tuple-element.73), channel_id=1, source_target_pairs={{0,128},{128,0},{1,129},{129,1},{2,130},{130,2},{3,131},{131,3},{4... | collective-permute-start | bytes 3145736 | tf_op jit(solution)/shard_map/ppermute | solution.py:332
  84.2 7.9 %collective-permute-start.4 = (bf16[7,2,4,128,128]{4,3,2,1,0:T(8,128)(2,1)}, bf16[7,2,4,128,128]{4,3,2,1,0:T(8,128)(2,1)}, u32[]{:S(2)}, u32[]{:S(2)}) collective-permute-start(bf16[7,2,4,128,128]{4,3,2,1,0:T(8,128)(2,1)} %get-tuple-element.85), channel_id=1, source_target_pairs={{0,128},{128,0},{1,129},{129,1},{2,130},{130,2},{3,131},{131,3},{4... | collective-permute-start | bytes 5505032 | tf_op jit(solution)/shard_map/ppermute | solution.py:332
  84.7 68.9 %all-to-all-start.1 = ((bf16[128,8,512]{2,1,0:T(8,128)(2,1)}), bf16[128,8,512]{2,1,0:T(8,128)(2,1)}, u32[]{:S(2)}, u32[]{:S(2)}) async-start(bf16[128,8,512]{2,1,0:T(8,128)(2,1)} %bitcast.12), calls=%async_computation.1 | async-start | bytes 2097152 | tf_op jit(solution)/shard_map/all_to_all | solution.py:344
  94.2 28.7 %collective-permute-start.5 = (bf16[7,128,128]{2,1,0:T(8,128)(2,1)S(1)}, bf16[7,128,128]{2,1,0:T(8,128)(2,1)S(1)}, u32[]{:S(2)}, u32[]{:S(2)}) collective-permute-start(bf16[7,128,128]{2,1,0:T(8,128)(2,1)S(1)} %get-tuple-element.87), channel_id=1, source_target_pairs={{0,1},{1,2},{2,3},{3,0},{4,5},{5,6},{6,7},{7,4},{8,9},{9,10},{10,1... | collective-permute-start | bytes 688136 | tf_op jit(solution)/shard_map/ppermute | solution.py:354
  94.6 27.6 %collective-permute-start.11 = (bf16[64,512]{1,0:T(8,128)(2,1)S(1)}, bf16[64,512]{1,0:T(8,128)(2,1)S(1)}, u32[]{:S(2)}, u32[]{:S(2)}) collective-permute-start(bf16[64,512]{1,0:T(8,128)(2,1)S(1)} %copy-done.8), channel_id=1, source_target_pairs={{0,1},{1,2},{2,3},{3,4},{4,5},{5,6},{6,7},{7,8},{8,9},{9,10},{10,1... | collective-permute-start | bytes 196616 | tf_op jit(solution)/shard_map/ppermute | solution.py:337
  95.8 26.4 %collective-permute-start.12 = (bf16[64,512]{1,0:T(8,128)(2,1)S(1)}, bf16[64,512]{1,0:T(8,128)(2,1)S(1)}, u32[]{:S(2)}, u32[]{:S(2)}) collective-permute-start(bf16[64,512]{1,0:T(8,128)(2,1)S(1)} %copy-done.7), channel_id=1, source_target_pairs={{0,127},{1,0},{2,1},{3,2},{4,3},{5,4},{6,5},{7,6},{8,7},{9,8},{10,... | collective-permute-start | bytes 196616 | tf_op jit(solution)/shard_map/ppermute | solution.py:337
  101.5 29.3 %collective-permute-start.6 = (bf16[7,128,128]{2,1,0:T(8,128)(2,1)S(1)}, bf16[7,128,128]{2,1,0:T(8,128)(2,1)S(1)}, u32[]{:S(2)}, u32[]{:S(2)}) collective-permute-start(bf16[7,128,128]{2,1,0:T(8,128)(2,1)S(1)} %get-tuple-element.88), channel_id=1, source_target_pairs={{0,2},{1,3},{2,0},{3,1},{4,6},{5,7},{6,4},{7,5},{8,10},{9,11},{10,... | collective-permute-start | bytes 688136 | tf_op jit(solution)/shard_map/ppermute | solution.py:354
  101.5 29.3 %collective-permute-start.7 = (bf16[7,128,128]{2,1,0:T(8,128)(2,1)S(1)}, bf16[7,128,128]{2,1,0:T(8,128)(2,1)S(1)}, u32[]{:S(2)}, u32[]{:S(2)}) collective-permute-start(bf16[7,128,128]{2,1,0:T(8,128)(2,1)S(1)} %get-tuple-element.89), channel_id=1, source_target_pairs={{0,3},{1,0},{2,1},{3,2},{4,7},{5,4},{6,5},{7,6},{8,11},{9,8},{10,9... | collective-permute-start | bytes 688136 | tf_op jit(solution)/shard_map/ppermute | solution.py:354
  122.2 12.7 %collective-permute-start.8 = (bf16[7,128,128]{2,1,0:T(8,128)(2,1)S(1)}, bf16[7,128,128]{2,1,0:T(8,128)(2,1)S(1)}, u32[]{:S(2)}, u32[]{:S(2)}) collective-permute-start(bf16[7,128,128]{2,1,0:T(8,128)(2,1)S(1)} %get-tuple-element.91), channel_id=1, source_target_pairs={{0,4},{1,5},{2,6},{3,7},{4,8},{5,9},{6,10},{7,11},{8,12},{9,13},{1... | collective-permute-start | bytes 688136 | tf_op jit(solution)/shard_map/ppermute | solution.py:354
  122.9 12.0 %collective-permute-start.9 = (bf16[7,128,128]{2,1,0:T(8,128)(2,1)S(1)}, bf16[7,128,128]{2,1,0:T(8,128)(2,1)S(1)}, u32[]{:S(2)}, u32[]{:S(2)}) collective-permute-start(bf16[7,128,128]{2,1,0:T(8,128)(2,1)S(1)} %get-tuple-element.92), channel_id=1, source_target_pairs={{0,8},{1,9},{2,10},{3,11},{4,12},{5,13},{6,14},{7,15},{8,0},{9,1},... | collective-permute-start | bytes 688136 | tf_op jit(solution)/shard_map/ppermute | solution.py:354
  122.9 12.7 %collective-permute-start.10 = (bf16[7,128,128]{2,1,0:T(8,128)(2,1)S(1)}, bf16[7,128,128]{2,1,0:T(8,128)(2,1)S(1)}, u32[]{:S(2)}, u32[]{:S(2)}) collective-permute-start(bf16[7,128,128]{2,1,0:T(8,128)(2,1)S(1)} %get-tuple-element.93), channel_id=1, source_target_pairs={{0,12},{1,13},{2,14},{3,15},{4,0},{5,1},{6,2},{7,3},{8,4},{9,5},{1... | collective-permute-start | bytes 688136 | tf_op jit(solution)/shard_map/ppermute | solution.py:354
  136.3 3.8 %collective-permute-start.13 = (bf16[2,7,32,128]{3,2,1,0:T(8,128)(2,1)S(1)}, bf16[2,7,32,128]{3,2,1,0:T(8,128)(2,1)S(1)}, u32[]{:S(2)}, u32[]{:S(2)}) collective-permute-start(bf16[2,7,32,128]{3,2,1,0:T(8,128)(2,1)S(1)} %get-tuple-element.110), channel_id=1, source_target_pairs={{0,4},{1,5},{2,6},{3,7},{4,0},{5,1},{6,2},{7,3},{8,12},{9,13},{10,... | collective-permute-start | bytes 344072 | tf_op jit(solution)/shard_map/ppermute | solution.py:455
  138.0 3.9 %collective-permute-start.14 = (bf16[2,7,32,128]{3,2,1,0:T(8,128)(2,1)S(1)}, bf16[2,7,32,128]{3,2,1,0:T(8,128)(2,1)S(1)}, u32[]{:S(2)}, u32[]{:S(2)}) collective-permute-start(bf16[2,7,32,128]{3,2,1,0:T(8,128)(2,1)S(1)} %get-tuple-element.112), channel_id=1, source_target_pairs={{0,1},{1,0},{2,3},{3,2},{4,5},{5,4},{6,7},{7,6},{8,9},{9,8},{10,11... | collective-permute-start | bytes 344072 | tf_op jit(solution)/shard_map/ppermute | solution.py:455
  141.9 4.3 %collective-permute-start.15 = (bf16[7,32,128]{2,1,0:T(8,128)(2,1)S(1)}, bf16[7,32,128]{2,1,0:T(8,128)(2,1)S(1)}, u32[]{:S(2)}, u32[]{:S(2)}) collective-permute-start(bf16[7,32,128]{2,1,0:T(8,128)(2,1)S(1)} %get-tuple-element.114), channel_id=1, source_target_pairs={{0,12},{1,13},{2,14},{3,15},{4,8},{5,9},{6,10},{7,11},{8,4},{9,5},... | collective-permute-start | bytes 172040 | tf_op jit(solution)/shard_map/ppermute | solution.py:455
  143.9 4.5 %collective-permute-start.16 = (bf16[7,32,128]{2,1,0:T(8,128)(2,1)S(1)}, bf16[7,32,128]{2,1,0:T(8,128)(2,1)S(1)}, u32[]{:S(2)}, u32[]{:S(2)}) collective-permute-start(bf16[7,32,128]{2,1,0:T(8,128)(2,1)S(1)} %get-tuple-element.116), channel_id=1, source_target_pairs={{0,3},{1,2},{2,1},{3,0},{4,7},{5,6},{6,5},{7,4},{8,11},{9,10},{10,... | collective-permute-start | bytes 172040 | tf_op jit(solution)/shard_map/ppermute | solution.py:455
  149.0 3.2 %collective-permute-start.17 = (bf16[4,32,256]{2,1,0:T(8,128)(2,1)S(1)}, bf16[4,32,256]{2,1,0:T(8,128)(2,1)S(1)}, u32[]{:S(2)}, u32[]{:S(2)}) collective-permute-start(bf16[4,32,256]{2,1,0:T(8,128)(2,1)S(1)} %get-tuple-element.118), channel_id=1, source_target_pairs={{0,16},{1,17},{2,18},{3,19},{4,20},{5,21},{6,22},{7,23},{8,24},{9,... | collective-permute-start | bytes 196616 | tf_op jit(solution)/shard_map/ppermute | solution.py:455
  152.8 4.1 %collective-permute-start.18 = (bf16[2,32,256]{2,1,0:T(8,128)(2,1)S(1)}, bf16[2,32,256]{2,1,0:T(8,128)(2,1)S(1)}, u32[]{:S(2)}, u32[]{:S(2)}) collective-permute-start(bf16[2,32,256]{2,1,0:T(8,128)(2,1)S(1)} %get-tuple-element.120), channel_id=1, source_target_pairs={{0,32},{1,33},{2,34},{3,35},{4,36},{5,37},{6,38},{7,39},{8,40},{9,... | collective-permute-start | bytes 98312 | tf_op jit(solution)/shard_map/ppermute | solution.py:455
  157.5 10.2 %collective-permute-start.21 = (f32[1,32,256]{2,1,0:T(8,128)S(1)}, f32[1,32,256]{2,1,0:T(8,128)S(1)}, u32[]{:S(2)}, u32[]{:S(2)}) collective-permute-start(f32[1,32,256]{2,1,0:T(8,128)S(1)} %get-tuple-element.125), channel_id=1, source_target_pairs={{0,192},{1,193},{2,194},{3,195},{4,196},{5,197},{6,198},{7,199},{8... | collective-permute-start | bytes 98312 | tf_op jit(solution)/shard_map/ppermute | solution.py:455
  165.9 6.7 %collective-permute-start.19 = (f32[1,32,256]{2,1,0:T(8,128)S(1)}, f32[1,32,256]{2,1,0:T(8,128)S(1)}, u32[]{:S(2)}, u32[]{:S(2)}) collective-permute-start(f32[1,32,256]{2,1,0:T(8,128)S(1)} %get-tuple-element.125), channel_id=1, source_target_pairs={{0,64},{1,65},{2,66},{3,67},{4,68},{5,69},{6,70},{7,71},{8,72},{9,... | collective-permute-start | bytes 98312 | tf_op jit(solution)/shard_map/ppermute | solution.py:455
  167.6 5.0 %collective-permute-start.20 = (f32[1,32,256]{2,1,0:T(8,128)S(1)}, f32[1,32,256]{2,1,0:T(8,128)S(1)}, u32[]{:S(2)}, u32[]{:S(2)}) collective-permute-start(f32[1,32,256]{2,1,0:T(8,128)S(1)} %get-tuple-element.124.own_ref), channel_id=1, source_target_pairs={{0,128},{1,129},{2,130},{3,131},{4,132},{5,133},{6,134},{7,135},{8... | collective-permute-start | bytes 98312 | tf_op jit(solution)/shard_map/ppermute | solution.py:455
  (9 other events, 56.1 us)
